TPU v7x, 128 devices: a whole 4x4x4 slice. The times are simulated.
128 devices in a mesh: section: 2 (over x_hi), dp: 16 (over x_lo, y, core), mp: 4 (over z).
Axes of the slice: x: 4 (x_hi: 2, x_lo: 2; x = x_hi * 2 + x_lo), y: 4, z: 4, core: 2. Of those that a mesh axis runs over, the one named last changes fastest.
Arguments:
- hidden: bfloat16 [32, 256, 8192], P(('section', 'dp'), None, 'mp'), may hold values from -6 to 6
- query_weight: bfloat16 [2, 8192, 4096], P('section', None, 'mp'), may hold values from -1 to 1
- keyval_weight: bfloat16 [2, 8192, 2, 512], P('section', None, None, 'mp'), may hold values from -1 to 1
- reward_head: float32 [4096], P('mp'), may hold values from -6 to 6
- lengths: int32 [32], replicated, may hold values from 1 to 256, as said below
- group_ids: int32 [32], replicated, may hold values from 0 to 7, as said below
- dest: int32 [1024, 1], P(('section', 'dp')), may hold values from 0 to 31; in each aligned block of 32 rows (0 to 31, 32 to 63, ...) at most 2 rows name the same one
Outputs:
- relayed: bfloat16 [32, 32, 2, 16, 4096], P(('section', 'dp'), None, None, None, 'mp')
- advantage: float32 [32], P(('section', 'dp'))
Inputs may be any that keep to these rules, and one draw needn't show every extreme that they name: `lengths`: at least one row has length 256. `group_ids`: each group id names exactly 4 rows. `dest`: among the 32 blocks of one source no shard is named more than 2 times.
All inputs are finite; a program needn't handle non-finite values.
Results may differ from a plain program's by a relative error of at most 0.0065.
Values may be sent and summed in bfloat16 or wider, within the bound.
No kernel may reach another device: no remote copies, remote signals or barrier semaphores. Data moves between devices by JAX's collectives and lax.ppermute only.
A program may use at most 128 MiB of HBM per device.

v0:
```python
import math

import jax
import jax.numpy as jnp
from jax import lax
from jax.sharding import PartitionSpec as P

HD = 128
BLK = 16
GSIZE = 4


def attend(query, keys, values, length):
    seq = query.shape[0]
    kv_heads = keys.shape[1] // HD
    heads = query.shape[1] // HD
    group = heads // kv_heads
    q_heads = query.reshape(seq, kv_heads, group, HD)
    k_heads = keys.reshape(seq, kv_heads, HD)
    v_heads = values.reshape(seq, kv_heads, HD)
    scores = jnp.einsum("tkgd,skd->kgts", q_heads, k_heads, preferred_element_type=jnp.float32) * (
        1.0 / math.sqrt(HD)
    )
    places = jnp.arange(seq)
    allowed = (places[None, :] <= places[:, None]) & (places[None, :] < length)
    scores = jnp.where(allowed, scores, -1e30)
    highest = jnp.max(scores, axis=-1, keepdims=True)
    probs = jnp.exp(scores - highest)
    probs = probs / jnp.sum(probs, axis=-1, keepdims=True)
    weights = probs.astype(jnp.bfloat16)
    output = jnp.einsum("kgts,skd->tkgd", weights, v_heads, preferred_element_type=jnp.float32)
    output = jnp.where((places < length)[:, None, None, None], output, 0.0)
    return output.reshape(seq, heads * HD).astype(jnp.bfloat16)


def body(hidden, query_weight, keyval_weight, reward_head, lengths, group_ids, dest):
    both_rows = lax.all_gather(hidden, "section", axis=0, tiled=True)
    full_rows = lax.all_gather(both_rows, "mp", axis=2, tiled=True)
    sections = lax.axis_size("section")
    dp_size = lax.axis_size("dp")
    section_idx = lax.axis_index("section")
    dp_idx = lax.axis_index("dp")
    row_ids = jnp.arange(sections, dtype=jnp.int32) * dp_size + dp_idx
    row_lengths = lengths[row_ids]
    query = jnp.einsum(
        "rtd,dc->rtc", full_rows, query_weight[0], preferred_element_type=jnp.float32
    ).astype(jnp.bfloat16)
    keyval = jnp.einsum(
        "rtd,dzc->rtzc", full_rows, keyval_weight[0], preferred_element_type=jnp.float32
    ).astype(jnp.bfloat16)
    states = jax.vmap(attend)(query, keyval[:, :, 0], keyval[:, :, 1], row_lengths)
    partial_reward = jnp.sum(states.astype(jnp.float32) * reward_head[None, None, :], axis=(1, 2))
    partial_reward = partial_reward / row_lengths.astype(jnp.float32)
    partial_reward = jnp.where(section_idx == 1, partial_reward, 0.0)
    total_rows = lengths.shape[0]
    placed = jnp.where(
        jnp.arange(total_rows)[:, None] == row_ids[None, :], partial_reward[None, :], 0.0
    )
    reward = lax.psum(jnp.sum(placed, axis=1), ("section", "dp", "mp"))
    member = group_ids[:, None] == jnp.arange(total_rows // GSIZE)[None, :]
    means = jnp.sum(jnp.where(member, reward[:, None], 0.0), axis=0) / GSIZE
    advantage_all = reward - jnp.sum(jnp.where(member, means[None, :], 0.0), axis=1)
    own_index = section_idx * dp_size + dp_idx
    advantage = lax.dynamic_slice_in_dim(advantage_all, own_index, 1, 0)
    block_count = dest.shape[0]
    features = states.shape[2]
    most = max(2, 2 * block_count // total_rows)
    blocks = states.reshape(block_count, BLK * features)
    targets = dest[:, 0]
    order = jnp.arange(block_count)
    same = (targets[:, None] == targets[None, :]) & (order[None, :] < order[:, None])
    rank = jnp.sum(same.astype(jnp.int32), axis=1)
    slot = targets * most + rank
    onehot = (jnp.arange(total_rows * most)[:, None] == slot[None, :]).astype(jnp.bfloat16)
    outgoing = jnp.dot(onehot, blocks, preferred_element_type=jnp.float32).astype(jnp.bfloat16)
    outgoing = outgoing.reshape(total_rows, most, BLK, features)
    received = lax.all_to_all(outgoing, ("section", "dp"), split_axis=0, concat_axis=0, tiled=True)
    return (received[None], advantage)


def solution(mesh):
    return jax.shard_map(
        body,
        mesh=mesh,
        in_specs=(
            P(("section", "dp"), None, "mp"),
            P("section", None, "mp"),
            P("section", None, None, "mp"),
            P("mp"),
            P(),
            P(),
            P(("section", "dp"), None),
        ),
        out_specs=(P(("section", "dp"), None, None, None, "mp"), P(("section", "dp"))),
        check_vma=False,
    )
```

profile of v0, /device:TPU:0, one launch (start us, length us, event | category | flops | bytes accessed | tf_op | source)
XLA Modules:
  0.0 260.6 jit_solution(10097574017462434394)
XLA Ops:
  7.2 0.0 copy-start
  7.2 0.0 all-gather.3.cloned.1.call-start
  7.2 0.7 all-gather.3.cloned.1.call-update
  7.9 0.0 all-gather.5.cloned.1.call-start
  8.0 41.3 %all-gather.3.cloned.1.call-done = bf16[2,256,2048]{2,1,0:T(8,128)(2,1)} async-done(((bf16[1,256,2048]{2,1,0:T(8,128)(2,1)}), bf16[2,256,2048]{2,1,0:T(8,128)(2,1)}) %all-gather.3.cloned.1.call-update) | async-done | bytes 2097168 | tf_op jit(solution)/shard_map/all_gather | solution.py:37
  49.3 0.0 all-gather.5.cloned.1.call-update
  49.4 0.0 copy-done
  49.4 0.6 gather_fusion
  50.0 0.9 convert_reduce_fusion
  51.0 0.7 multiply_add_fusion.1
  51.6 0.1 iota_compare_fusion.5
  51.7 0.1 broadcast_and_fusion
  51.8 81.9 %all-gather.5.cloned.1.call-done = bf16[2,256,8192]{2,1,0:T(8,128)(2,1)} async-done(((bf16[2,256,2048]{2,1,0:T(8,128)(2,1)}), bf16[2,256,8192]{2,1,0:T(8,128)(2,1)}) %all-gather.5.cloned.1.call-update) | async-done | bytes 8388624 | tf_op jit(solution)/shard_map/all_gather | solution.py:38
  133.8 0.0 copy-start.1
  133.8 7.1 %fusion.23 = bf16[2,256,2,128]{3,1,2,0:T(8,128)(2,1)S(1)} fusion(bf16[8192,2,128]{2,1,0:T(2,128)(2,1)} %bitcast.99, bf16[2,256,8192]{2,1,0:T(8,128)(2,1)} %all-gather.5.cloned.1.call-done), kind=kOutput, calls=%fused_computation.22 | convolution fusion | flops 2147614720 | bytes 12845056 | tf_op jit(solution)/shard_map/rtd,dzc->rtzc/dot_general | solution.py:48
  140.9 2.3 copy-done.1
  143.1 11.5 %fusion.15 = bf16[2,32,8,8,128]{4,3,2,1,0:T(8,128)(2,1)S(1)} fusion(bf16[2,256,8192]{2,1,0:T(8,128)(2,1)} %all-gather.5.cloned.1.call-done, bf16[1,8192,1024]{2,1,0:T(8,128)(2,1)S(1)} %copy-done.1), kind=kOutput, calls=%fused_computation.20 | convolution fusion | flops 8590458880 | bytes 26214400 | tf_op jit(solution)/shard_map/rtd,dc->rtc/dot_general | solution.py:45
  154.6 0.0 copy-start.2
  154.6 0.8 fusion.7
  155.5 0.9 fusion.6
  156.4 0.0 copy-done.2
  156.4 1.6 multiply_reduce_fusion
  158.1 0.7 copy.27
  158.8 0.5 convert_element_type.46
  159.3 0.7 convolution_convert_fusion
  160.0 0.0 copy-start.3
  160.0 2.5 copy.35
  162.6 7.1 %all-to-all-start = ((bf16[32,2,16,1024]{3,2,1,0:T(8,128)(2,1)}), bf16[32,2,16,1024]{3,2,1,0:T(8,128)(2,1)S(1)}, u32[]{:S(2)}, u32[]{:S(2)}) async-start(bf16[32,2,16,1024]{3,2,1,0:T(8,128)(2,1)} %bitcast.97), calls=%async_computation | async-start | bytes 4194304 | tf_op jit(solution)/shard_map/all_to_all | solution.py:77
  169.7 0.1 fusion.33
  169.8 81.8 %psum.7 = f32[32]{0:T(128)S(1)} all-reduce(f32[32]{0:T(128)S(1)} %fusion.33), channel_id=1, replica_groups=mesh['section'=2,'dp'=16,'mp'=4] {'section','dp','mp'}, use_global_device_ids=true, to_apply=%region_5.6 | all-reduce | flops 32 | bytes 256 | tf_op jit(solution)/shard_map/psum | solution.py:59
  251.6 0.0 copy-done.3
  251.6 0.1 select_reduce_fusion.1
  251.7 0.1 select_reduce_fusion
  251.8 0.6 dynamic_slice.3
  252.4 0.0 all-to-all-done
  252.4 1.3 copy.49
  (7 shorter events, 0.1 us)
Async XLA Ops:
  7.2 42.2 %copy-start = (s32[32]{0:T(128)S(1)}, s32[32]{0:T(128)}, u32[]{:S(2)}) copy-start(s32[32]{0:T(128)} %param.11) | copy-start | bytes 388
  7.2 42.1 %all-gather.3.cloned.1.call-start = ((), (), s32[]{:S(2)}) async-start(), calls=%async_computation.1 | async-start | bytes 3145728 | tf_op jit(solution)/shard_map/all_gather | solution.py:37
  7.9 125.9 %all-gather.5.cloned.1.call-start = ((), (), s32[]{:S(2)}) async-start(), calls=%async_computation.2 | async-start | bytes 10485760 | tf_op jit(solution)/shard_map/all_gather | solution.py:38
  133.8 9.3 %copy-start.1 = (bf16[1,8192,1024]{2,1,0:T(8,128)(2,1)S(1)}, bf16[1,8192,1024]{2,1,0:T(8,128)(2,1)}, u32[]{:S(2)}) copy-start(bf16[1,8192,1024]{2,1,0:T(8,128)(2,1)} %param.8) | copy-start | bytes 50331652
  154.6 1.8 copy-start.2
  160.0 91.6 %copy-start.3 = (s32[32]{0:T(128)S(1)}, s32[32]{0:T(128)}, u32[]{:S(2)}) copy-start(s32[32]{0:T(128)} %param.12) | copy-start | bytes 388
  162.6 89.8 %all-to-all-start = ((bf16[32,2,16,1024]{3,2,1,0:T(8,128)(2,1)}), bf16[32,2,16,1024]{3,2,1,0:T(8,128)(2,1)S(1)}, u32[]{:S(2)}, u32[]{:S(2)}) async-start(bf16[32,2,16,1024]{3,2,1,0:T(8,128)(2,1)} %bitcast.97), calls=%async_computation | async-start | bytes 4194304 | tf_op jit(solution)/shard_map/all_to_all | solution.py:77
Sparse Core Ops, SparseCore 0:
  9.7 39.5 all-gather.2
  51.0 82.7 all-gather.4
where the time goes:
time: 262 us; the launch traced here: 261 us
  waiting for transfers between devices  124 us (47%)
  blocking collectives  81.8 us (31%)
  matrix products  21.7 us (8%)
  between operations  14.2 us (5%)
  local copies, waits for them, and re-layouts  8.61 us (3%)
  starting transfers between devices  7.17 us (3%)
  other arithmetic  3.08 us (1%)
    all_gather x1, waiting for transfers between devices, body(): full_rows = lax.all_gather(both_rows, 'mp', axis=2, tiled=True)  81.9 us
    psum x1, blocking collectives, body(): reward = lax.psum(jnp.sum(placed, axis=1), ('section', 'dp', 'mp'))  81.8 us
    all_gather x1, waiting for transfers between devices, body(): both_rows = lax.all_gather(hidden, 'section', axis=0, tiled=True)  41.3 us
    dot_general x1, matrix products, body(): jnp.einsum('rtd,dc->rtc', full_rows, query_weight[0], preferred_element_t...  11.5 us
    all_to_all x1, starting transfers between devices, body(): lax.all_to_all(outgoing, ('section', 'dp'), split_axis=0, concat_axis=0,...  7.09 us
    dot_general x1, matrix products, body(): jnp.einsum('rtd,dzc->rtzc', full_rows, keyval_weight[0], preferred_elemen...  7.08 us
    unnamed x10, local copies, waits for them, and re-layouts  6.13 us
  transfers between devices with their start and end apart: 3, of which 2 were waited for; matrix products, arithmetic and copies ran while one was open for 1% of the time, Pallas kernels for 0%

commit v1 on v0

v1 whole, which is shorter than its diff:
```python
import functools
import math

import jax
import jax.numpy as jnp
from jax import lax
from jax.experimental import pallas as pl
from jax.experimental.pallas import tpu as pltpu
from jax.sharding import PartitionSpec as P

HD = 128
BLK = 16
GSIZE = 4
LANES = 128
DEPTH = 1024
PLANE = ("section", "dp")
VMEM_LIMIT = 48 * 1024 * 1024


def x_opposite(sections, dp_size):
    count = sections * dp_size
    return [(i, (i + dp_size) % count) for i in range(count)]


def ring(size, step):
    return [(i, (i + step) % size) for i in range(size)]


def project(step, depth_steps, pieces, query_weight, keyval_weight, total):
    features = query_weight.shape[-1]
    piece_step = lax.rem(step, depth_steps)
    for number, (low, high) in enumerate(pieces):
        @pl.when(step // depth_steps == number)
        def _():
            columns = pl.ds(pl.multiple_of(piece_step * DEPTH, DEPTH), DEPTH)
            rows = jnp.concatenate([low[:, columns], high[:, columns]], axis=0)
            total[:, :features] += jnp.dot(rows, query_weight[0], preferred_element_type=jnp.float32)
            total[:, features:] += jnp.dot(rows, keyval_weight[...], preferred_element_type=jnp.float32)


def first_kernel(depth_steps, places, *refs):
    pieces, (query_weight, keyval_weight, total) = refs[:-3], refs[-3:]
    step = pl.program_id(0)

    @pl.when(step == 0)
    def _():
        total[...] = jnp.zeros_like(total)

    project(step, depth_steps, list(zip(pieces[0::2], pieces[1::2])), query_weight, keyval_weight, total)


def attend(total, features, length, states, base):
    seq = total.shape[0]
    half = seq // 2
    keys = total[:, features:features + HD].astype(jnp.bfloat16)
    values = total[:, features + HD:features + 2 * HD].astype(jnp.bfloat16)
    values = jnp.concatenate([values, jnp.ones_like(values)], axis=1)
    scale = math.log2(math.e) / math.sqrt(HD)
    for head in range(features // HD):
        cols = pl.ds(head * HD, HD)
        for begin, size in ((0, half), (half, half)):
            reach = begin + size
            query = total[begin:reach, cols].astype(jnp.bfloat16)
            scores = lax.dot_general(
                query, keys[:reach], (((1,), (1,)), ((), ())), preferred_element_type=jnp.float32
            )
            token = lax.broadcasted_iota(jnp.int32, scores.shape, 0) + begin
            place = lax.broadcasted_iota(jnp.int32, scores.shape, 1)
            scores = jnp.where(place <= token, scores, -1e30)
            highest = jnp.max(scores, axis=1, keepdims=True)
            weights = jnp.exp2((scores - highest) * scale).astype(jnp.bfloat16)
            mixed = jnp.dot(weights, values[:reach], preferred_element_type=jnp.float32)
            output = mixed[:, :HD] / mixed[:, HD:]
            token = lax.broadcasted_iota(jnp.int32, output.shape, 0) + begin
            output = jnp.where(token < length, output, 0.0)
            states[pl.ds(base + begin, size), cols] = output.astype(jnp.bfloat16)


def row_reward(states, base, seq, head, scale, place):
    terms = states[pl.ds(base, seq), :].astype(jnp.float32) * head[...]
    summed = jnp.sum(jnp.sum(terms, axis=0, keepdims=True), axis=1, keepdims=True) * scale
    lane = lax.broadcasted_iota(jnp.int32, (1, LANES), 1)
    return jnp.where(lane == place, jnp.broadcast_to(summed, (1, LANES)), 0.0)


def row_kernel(depth_steps, places, low, high, query_weight, keyval_weight, partial, head, scale, states, reward, total):
    step = pl.program_id(0)

    @pl.when(step == 0)
    def _():
        total[...] = partial[...]

    project(step, depth_steps, [(low, high)], query_weight, keyval_weight, total)

    @pl.when(step == pl.num_programs(0) - 1)
    def _():
        seq = total.shape[0]
        attend(total, query_weight.shape[-1], places[1], states, 0)
        reward[...] = row_reward(states, 0, seq, head, scale[...], places[2])


def last_kernel(
    depth_steps, places, low, high, query_weight, keyval_weight, partial, head, scale, first_states, first_reward,
    outgoing, reward, total, states,
):
    step = pl.program_id(0)
    seq = total.shape[0]

    @pl.when(step == 0)
    def _():
        total[...] = partial[...]
        states[pl.ds(0, seq), :] = first_states[...]

    project(step, depth_steps, [(low, high)], query_weight, keyval_weight, total)

    @pl.when(step == pl.num_programs(0) - 1)
    def _():
        attend(total, query_weight.shape[-1], places[1], states, seq)
        reward[...] = first_reward[...] + row_reward(states, seq, seq, head, scale[...], places[2])
        shards, most = outgoing.shape[0], outgoing.shape[1]

        def fill(shard, carry):
            for k in range(most):
                block = places[3 + shard * most + k]

                @pl.when(block >= 0)
                def _():
                    outgoing[shard, k] = states[pl.ds(pl.multiple_of(block * BLK, BLK), BLK), :]

                @pl.when(block < 0)
                def _():
                    outgoing[shard, k] = jnp.zeros(outgoing.shape[2:], outgoing.dtype)
            return carry

        lax.fori_loop(0, shards, fill, 0)


def whole(shape):
    return pl.BlockSpec(shape, lambda i, places: (0,) * len(shape))


def weight_specs(depth_steps, features):
    def place(i, places):
        return places[i // depth_steps] * depth_steps + i % depth_steps

    return [
        pl.BlockSpec((1, DEPTH, features), lambda i, places: (0, place(i, places), 0)),
        pl.BlockSpec((DEPTH, 2 * HD), lambda i, places: (place(i, places), 0)),
    ]


def estimate(seq, depth, width):
    return pl.CostEstimate(flops=2 * seq * depth * width, bytes_accessed=2 * depth * width, transcendentals=0)


def body(hidden, query_weight, keyval_weight, reward_head, lengths, group_ids, dest):
    sections = lax.axis_size("section")
    dp_size = lax.axis_size("dp")
    mp_size = lax.axis_size("mp")
    section_idx = lax.axis_index("section")
    dp_idx = lax.axis_index("dp")
    mp_idx = lax.axis_index("mp")
    total_rows = lengths.shape[0]
    own = section_idx * dp_size + dp_idx
    other = (1 - section_idx) * dp_size + dp_idx

    seq, depth = hidden.shape[1], hidden.shape[2]
    features = query_weight.shape[2]
    width = features + 2 * HD
    half = seq // 2
    depth_steps = depth // DEPTH
    keyval_weight = keyval_weight.reshape(keyval_weight.shape[1], 2 * HD)

    up = functools.partial(lax.ppermute, axis_name="mp", perm=ring(mp_size, 1))
    down = functools.partial(lax.ppermute, axis_name="mp", perm=ring(mp_size, -1))
    across = functools.partial(lax.ppermute, axis_name=PLANE, perm=x_opposite(sections, dp_size))

    mine_low, mine_high = hidden[0, :half], hidden[0, half:]
    below_low = up(mine_low)
    above_high = down(mine_high)
    theirs = across(hidden[0])
    below_high = up(mine_high)
    above_low = down(mine_low)
    far_low = up(below_low)
    far_high = down(above_high)
    theirs_low, theirs_high = theirs[:half], theirs[half:]
    their_below_low = across(below_low)
    their_above_high = across(above_high)
    their_below_high = up(theirs_high)
    their_above_low = down(theirs_low)
    their_far_low = up(their_below_low)
    their_far_high = down(their_above_high)

    block_count = dest.shape[0]
    most = max(2, 2 * block_count // total_rows)
    targets = dest[:, 0]
    order = jnp.arange(block_count, dtype=jnp.int32)
    same = (targets[:, None] == targets[None, :]) & (order[None, :] < order[:, None])
    slot = targets * most + jnp.sum(same.astype(jnp.int32), axis=1)
    held = jnp.where(section_idx == 0, order, (order + block_count // 2) % block_count)
    hit = jnp.arange(total_rows * most, dtype=jnp.int32)[:, None] == slot[None, :]
    source = jnp.sum(jnp.where(hit, held[None, :] + 1, 0), axis=1) - 1

    below, above, far = (mp_idx + mp_size - 1) % mp_size, (mp_idx + 1) % mp_size, (mp_idx + 2) % mp_size
    three = jnp.stack([mp_idx, below, above]).astype(jnp.int32)
    head = reward_head.reshape(1, features)
    reward_scale = jnp.where(section_idx == 1, 1.0 / lengths.astype(jnp.float32), 0.0)

    def first(pieces):
        return pl.pallas_call(
            functools.partial(first_kernel, depth_steps),
            grid_spec=pltpu.PrefetchScalarGridSpec(
                num_scalar_prefetch=1,
                grid=(depth_steps * len(pieces) // 2,),
                in_specs=[whole((half, depth))] * len(pieces) + weight_specs(depth_steps, features),
                out_specs=whole((seq, width)),
            ),
            out_shape=jax.ShapeDtypeStruct((seq, width), jnp.float32),
            compiler_params=pltpu.CompilerParams(vmem_limit_bytes=VMEM_LIMIT),
            cost_estimate=estimate(seq, depth * len(pieces) // 2, width),
        )(three, *pieces, query_weight, keyval_weight)

    def row_places(row, *more):
        return jnp.concatenate([jnp.stack([far, lengths[row], row]).astype(jnp.int32), *more])

    row_specs = [whole((half, depth))] * 2 + weight_specs(depth_steps, features)
    row_specs += [whole((seq, width)), whole((1, features)), whole((1, 1))]

    own_partial = first([mine_low, mine_high, below_low, below_high, above_low, above_high])
    own_states, own_reward = pl.pallas_call(
        functools.partial(row_kernel, depth_steps),
        grid_spec=pltpu.PrefetchScalarGridSpec(
            num_scalar_prefetch=1,
            grid=(depth_steps,),
            in_specs=row_specs,
            out_specs=[whole((seq, features)), whole((1, LANES))],
            scratch_shapes=[pltpu.VMEM((seq, width), jnp.float32)],
        ),
        out_shape=[
            jax.ShapeDtypeStruct((seq, features), jnp.bfloat16),
            jax.ShapeDtypeStruct((1, LANES), jnp.float32),
        ],
        compiler_params=pltpu.CompilerParams(vmem_limit_bytes=VMEM_LIMIT),
        cost_estimate=estimate(seq, depth, width),
    )(row_places(own), far_low, far_high, query_weight, keyval_weight, own_partial, head, reward_scale[own].reshape(1, 1))

    their_partial = first([theirs_low, theirs_high, their_below_low, their_below_high, their_above_low, their_above_high])
    outgoing, rewards = pl.pallas_call(
        functools.partial(last_kernel, depth_steps),
        grid_spec=pltpu.PrefetchScalarGridSpec(
            num_scalar_prefetch=1,
            grid=(depth_steps,),
            in_specs=row_specs + [whole((seq, features)), whole((1, LANES))],
            out_specs=[whole((total_rows, most, BLK, features)), whole((1, LANES))],
            scratch_shapes=[pltpu.VMEM((seq, width), jnp.float32), pltpu.VMEM((2 * seq, features), jnp.bfloat16)],
        ),
        out_shape=[
            jax.ShapeDtypeStruct((total_rows, most, BLK, features), jnp.bfloat16),
            jax.ShapeDtypeStruct((1, LANES), jnp.float32),
        ],
        compiler_params=pltpu.CompilerParams(vmem_limit_bytes=VMEM_LIMIT),
        cost_estimate=estimate(seq, depth, width),
    )(
        row_places(other, source), their_far_low, their_far_high, query_weight, keyval_weight, their_partial, head,
        reward_scale[other].reshape(1, 1), own_states, own_reward,
    )

    received = lax.all_to_all(outgoing, PLANE, split_axis=0, concat_axis=0, tiled=True)

    for step in (1, 2):
        rewards += lax.ppermute(rewards, "mp", [(i, i ^ step) for i in range(mp_size)])
    step = 1
    while step < sections * dp_size:
        rewards += lax.ppermute(rewards, PLANE, [(i, i ^ step) for i in range(sections * dp_size)])
        step *= 2
    rewards = rewards[0, :total_rows]
    alike = group_ids == group_ids[own]
    advantage = rewards[own] - jnp.sum(jnp.where(alike, rewards, 0.0)) / GSIZE
    return (received[None], advantage[None])


def solution(mesh):
    return jax.shard_map(
        body,
        mesh=mesh,
        in_specs=(
            P(("section", "dp"), None, "mp"),
            P("section", None, "mp"),
            P("section", None, None, "mp"),
            P("mp"),
            P(),
            P(),
            P(("section", "dp"), None),
        ),
        out_specs=(P(("section", "dp"), None, None, None, "mp"), P(("section", "dp"))),
        check_vma=False,
    )
```

time: 262 us -> 147 us (0.56)
  blocking collectives: 81.8 us -> 0 us
  waiting for transfers between devices: 124 us -> 52.2 us
  starting transfers between devices: 7.17 us -> 42.3 us
  Pallas kernels: 0 us -> 34.1 us
  matrix products: 21.7 us -> 0 us
  between operations: 14.2 us -> 3.31 us
    all_gather x2 -> x0, waiting for transfers between devices: 123 us -> none  [the longest x1 81.9 us: body(): full_rows = lax.all_gather(both_rows, 'mp', axis=2, tiled=True)]
    psum x1 -> x0, blocking collectives: 81.8 us -> none  [body(): reward = lax.psum(jnp.sum(placed, axis=1), ('section', 'dp', 'mp'))]
    ppermute x0 -> x20, waiting for transfers between devices: none -> 52.2 us  [the longest x5 20.7 us: body(): lax.ppermute(rewards, PLANE, [(i, i ^ step) for i in range(sections * dp_...]
    ppermute x0 -> x20, starting transfers between devices: none -> 34.9 us  [the longest x5 8.46 us: body(): lax.ppermute(rewards, PLANE, [(i, i ^ step) for i in range(sections * dp_...]
    pallas_call x0 -> x4, Pallas kernels: none -> 34.1 us  [the longest x2 19.4 us: first(): pl.pallas_call(functools.partial(first_kernel, depth_steps), grid_spec=pl...]
    dot_general x5 -> x0, matrix products: 21.7 us -> none  [the longest x1 11.5 us: body(): jnp.einsum('rtd,dc->rtc', full_rows, query_weight[0], preferred_element_t...]
  transfers between devices with their start and end apart: 3 -> 21, of which waited for: 2 -> 11; matrix products, arithmetic and copies ran while one was open for 1% -> 8% of each run, Pallas kernels for 0% -> 18%
where the time goes in v1:
time: 147 us; the launch traced here: 146 us
  waiting for transfers between devices  52.2 us (36%)
  starting transfers between devices  42.3 us (29%)
  Pallas kernels  34.1 us (23%)
  local copies, waits for them, and re-layouts  11 us (7%)
  between operations  3.31 us (2%)
  other arithmetic  3.01 us (2%)
    ppermute x5, waiting for transfers between devices, body(): lax.ppermute(rewards, PLANE, [(i, i ^ step) for i in range(sections * dp_...  20.7 us
    pallas_call x2, Pallas kernels, first(): pl.pallas_call(functools.partial(first_kernel, depth_steps), grid_spec=pl...  19.4 us
    ppermute x1, waiting for transfers between devices, body(): below_low = up(mine_low)  9.18 us
    ppermute x2, waiting for transfers between devices, body(): lax.ppermute(rewards, 'mp', [(i, i ^ step) for i in range(mp_size)])  8.57 us
    pallas_call x1, Pallas kernels, body(): pl.pallas_call(functools.partial(last_kernel, depth_steps), grid_spec=plt...  8.55 us
    ppermute x5, starting transfers between devices, body(): lax.ppermute(rewards, PLANE, [(i, i ^ step) for i in range(sections * dp_...  8.46 us
    ppermute x1, waiting for transfers between devices, body(): their_above_high = across(above_high)  8.14 us
    all_to_all x1, starting transfers between devices, body(): lax.all_to_all(outgoing, PLANE, split_axis=0, concat_axis=0, tiled=True)  7.36 us
  transfers between devices with their start and end apart: 21, of which 11 were waited for; matrix products, arithmetic and copies ran while one was open for 8% of the time, Pallas kernels for 18%

profile of v1, /device:TPU:0, one launch (start us, length us, event | category | flops | bytes accessed | tf_op | source)
XLA Modules:
  0.0 145.9 jit_solution(9301794593533240371)
XLA Ops:
  0.6 0.0 copy-start.2
  0.6 0.0 copy-start.1
  0.6 1.3 slice_bitcast_fusion
  1.9 4.2 %collective-permute-start.3 = (bf16[128,2048]{1,0:T(8,128)(2,1)S(1)}, bf16[128,2048]{1,0:T(8,128)(2,1)S(1)}, u32[]{:S(2)}, u32[]{:S(2)}) collective-permute-start(bf16[128,2048]{1,0:T(8,128)(2,1)S(1)} %get-tuple-element.12.refs_1_), channel_id=1, source_target_pairs={{0,3},{1,0},{2,1},{3,2},{4,7},{5,4},{6,5},{7,6},{8,11},{9,8},{10,9... | collective-permute-start | bytes 1572872 | tf_op jit(solution)/shard_map/ppermute | solution.py:180
  6.1 0.0 collective-permute-start.11
  6.1 0.0 collective-permute-start
  6.1 3.3 %collective-permute-start.12 = (bf16[128,2048]{1,0:T(8,128)(2,1)S(1)}, bf16[128,2048]{1,0:T(8,128)(2,1)S(1)}, u32[]{:S(2)}, u32[]{:S(2)}) collective-permute-start(bf16[128,2048]{1,0:T(8,128)(2,1)S(1)} %get-tuple-element.13.refs_0_), channel_id=1, source_target_pairs={{0,3},{1,0},{2,1},{3,2},{4,7},{5,4},{6,5},{7,6},{8,11},{9,8},{10,9... | collective-permute-start | bytes 1572872 | tf_op jit(solution)/shard_map/ppermute | solution.py:183
  9.4 3.0 %collective-permute-start.6 = (bf16[256,2048]{1,0:T(8,128)(2,1)}, bf16[256,2048]{1,0:T(8,128)(2,1)}, u32[]{:S(2)}, u32[]{:S(2)}) collective-permute-start(bf16[256,2048]{1,0:T(8,128)(2,1)} %bitcast.8), channel_id=1, source_target_pairs={{0,64},{4,68},{8,72},{12,76},{16,80},{20,84},{24,88},{28,92},{32,9... | collective-permute-start | bytes 3145736 | tf_op jit(solution)/shard_map/ppermute | solution.py:181
  12.4 0.0 copy-done.2
  12.4 0.2 convert_reduce_fusion
  12.6 0.0 copy-done.1
  12.6 0.6 fusion.6
  13.3 0.1 select_reduce_fusion
  13.4 0.1 pad_add_fusion.1.places
  13.4 5.0 %collective-permute-done.3.refs_5_ = bf16[128,2048]{1,0:T(8,128)(2,1)S(1)} collective-permute-done((bf16[128,2048]{1,0:T(8,128)(2,1)S(1)}, bf16[128,2048]{1,0:T(8,128)(2,1)S(1)}, u32[]{:S(2)}, u32[]{:S(2)}) %collective-permute-start.3) | collective-permute-done | bytes 524320 | tf_op jit(solution)/shard_map/ppermute | solution.py:180
  18.5 3.7 %collective-permute-start.10 = (bf16[128,2048]{1,0:T(8,128)(2,1)S(1)}, bf16[128,2048]{1,0:T(8,128)(2,1)S(1)}, u32[]{:S(2)}, u32[]{:S(2)}) collective-permute-start(bf16[128,2048]{1,0:T(8,128)(2,1)S(1)} %collective-permute-done.3.refs_5_), channel_id=1, source_target_pairs={{0,3},{1,0},{2,1},{3,2},{4,7},{5,4},{6,5},{7,6},{8,11},{9,8},{10,9... | collective-permute-start | bytes 1572872 | tf_op jit(solution)/shard_map/ppermute | solution.py:185
  22.1 0.6 pad_add_fusion.2.places
  22.8 9.2 %collective-permute-done.refs_2_ = bf16[128,2048]{1,0:T(8,128)(2,1)S(1)} collective-permute-done((bf16[128,2048]{1,0:T(8,128)(2,1)S(1)}, bf16[128,2048]{1,0:T(8,128)(2,1)S(1)}, u32[]{:S(2)}, u32[]{:S(2)}) %collective-permute-start) | collective-permute-done | bytes 524320 | tf_op jit(solution)/shard_map/ppermute | solution.py:179
  32.0 0.0 collective-permute-start.9
  32.0 0.0 collective-permute-done.11.refs_3_
  32.0 3.0 %collective-permute-start.1 = (bf16[128,2048]{1,0:T(8,128)(2,1)S(1)}, bf16[128,2048]{1,0:T(8,128)(2,1)S(1)}, u32[]{:S(2)}, u32[]{:S(2)}) collective-permute-start(bf16[128,2048]{1,0:T(8,128)(2,1)S(1)} %collective-permute-done.refs_2_), channel_id=1, source_target_pairs={{0,64},{4,68},{8,72},{12,76},{16,80},{20,84},{24,88},{28,92},{32,9... | collective-permute-start | bytes 1572872 | tf_op jit(solution)/shard_map/ppermute | solution.py:187
  35.0 0.6 collective-permute-done.6
  35.6 3.1 %collective-permute-start.4 = (bf16[128,2048]{1,0:T(8,128)(2,1)S(1)}, bf16[128,2048]{1,0:T(8,128)(2,1)S(1)}, u32[]{:S(2)}, u32[]{:S(2)}) collective-permute-start(bf16[128,2048]{1,0:T(8,128)(2,1)S(1)} %collective-permute-done.3.refs_5_), channel_id=1, source_target_pairs={{0,64},{4,68},{8,72},{12,76},{16,80},{20,84},{24,88},{28,92},{32,9... | collective-permute-start | bytes 1572872 | tf_op jit(solution)/shard_map/ppermute | solution.py:188
  38.7 1.3 fusion.4
  40.0 0.0 collective-permute-done.12.refs_4_
  40.0 0.1 collective-permute-start.7
  40.1 0.0 collective-permute-done.10.high
  40.1 3.4 %collective-permute-start.8 = (bf16[128,2048]{1,0:T(8,128)(2,1)S(1)}, bf16[128,2048]{1,0:T(8,128)(2,1)S(1)}, u32[]{:S(2)}, u32[]{:S(2)}) collective-permute-start(bf16[128,2048]{1,0:T(8,128)(2,1)S(1)} %get-tuple-element.11.refs_0_), channel_id=1, source_target_pairs={{0,3},{1,0},{2,1},{3,2},{4,7},{5,4},{6,5},{7,6},{8,11},{9,8},{10,9... | collective-permute-start | bytes 1572872 | tf_op jit(solution)/shard_map/ppermute | solution.py:190
  43.5 0.7 pad_add_fusion.places
  44.2 4.7 %copy.11 = bf16[1024,8,2,128]{3,1,2,0:T(8,128)(2,1)} copy(bf16[1024,8,2,128]{3,2,1,0:T(2,128)(2,1)} %bitcast.35) | data formatting | bytes 8388608
  48.8 0.7 fusion.5
  49.5 0.0 collective-permute-done.1.refs_2_
  49.5 0.0 collective-permute-start.2
  49.5 8.1 %collective-permute-done.4.refs_5_ = bf16[128,2048]{1,0:T(8,128)(2,1)S(1)} collective-permute-done((bf16[128,2048]{1,0:T(8,128)(2,1)S(1)}, bf16[128,2048]{1,0:T(8,128)(2,1)S(1)}, u32[]{:S(2)}, u32[]{:S(2)}) %collective-permute-start.4) | collective-permute-done | bytes 524320 | tf_op jit(solution)/shard_map/ppermute | solution.py:188
  57.6 2.6 %collective-permute-start.5 = (bf16[128,2048]{1,0:T(8,128)(2,1)S(1)}, bf16[128,2048]{1,0:T(8,128)(2,1)S(1)}, u32[]{:S(2)}, u32[]{:S(2)}) collective-permute-start(bf16[128,2048]{1,0:T(8,128)(2,1)S(1)} %collective-permute-done.4.refs_5_), channel_id=1, source_target_pairs={{0,3},{1,0},{2,1},{3,2},{4,7},{5,4},{6,5},{7,6},{8,11},{9,8},{10,9... | collective-permute-start | bytes 1572872 | tf_op jit(solution)/shard_map/ppermute | solution.py:192
  60.2 9.7 %shard_map.87.partial = f32[256,1280]{1,0:T(8,128)S(1)} custom-call(s32[3]{0:T(128)S(1)} %pad_add_fusion.1.places, bf16[128,2048]{1,0:T(8,128)(2,1)S(1)} %get-tuple-element.13.refs_0_, bf16[128,2048]{1,0:T(8,128)(2,1)S(1)} %get-tuple-element.12.refs_1_, bf16[128,2048]{1,0:T(8,128)(2,1)S(1)} %collective-permute-done.refs_2_, ...), custom_call_target="tpu_custom_call" | custom-call | flops 4026531840 | bytes 15728640 | tf_op jit(solution)/shard_map/pallas_call | solution.py:210
  69.9 0.0 collective-permute-done.9.low
  70.0 6.1 %shard_map.88 = (bf16[256,1024]{1,0:T(8,128)(2,1)S(1)}, f32[1,128]{1,0:T(1,128)S(1)}) custom-call(s32[3]{0:T(128)S(1)} %pad_add_fusion.2.places, bf16[128,2048]{1,0:T(8,128)(2,1)S(1)} %collective-permute-done.9.low, bf16[128,2048]{1,0:T(8,128)(2,1)S(1)} %collective-permute-done.10.high, bf16[1,8192,1024]{2,1,0:T(8,128)(2,1)} %query_weight.3, ...), custom_call_target="tpu_custom_call" | custom-call | flops 1342177280 | bytes 5242880 | tf_op jit(solution)/shard_map/pallas_call | solution.py:230
  76.1 0.0 collective-permute-done.7.refs_3_
  76.1 0.0 collective-permute-done.8.refs_4_
  76.1 9.7 %shard_map.86.partial = f32[256,1280]{1,0:T(8,128)S(1)} custom-call(s32[3]{0:T(128)S(1)} %pad_add_fusion.1.places, bf16[128,2048]{1,0:T(8,128)(2,1)S(1)} %get-tuple-element.11.refs_0_, bf16[128,2048]{1,0:T(8,128)(2,1)S(1)} %get-tuple-element.10.refs_1_, bf16[128,2048]{1,0:T(8,128)(2,1)S(1)} %collective-permute-done.1.refs_2_, ...), custom_call_target="tpu_custom_call" | custom-call | flops 4026531840 | bytes 15728640 | tf_op jit(solution)/shard_map/pallas_call | solution.py:210
  85.8 0.0 collective-permute-done.2.low
  85.8 0.0 collective-permute-done.5.high
  85.8 8.6 %shard_map.89 = (bf16[32,2,16,1024]{3,2,1,0:T(8,128)(2,1)}, f32[1,128]{1,0:T(1,128)S(1)}) custom-call(s32[67]{0:T(128)S(1)} %pad_add_fusion.places, bf16[128,2048]{1,0:T(8,128)(2,1)S(1)} %collective-permute-done.2.low, bf16[128,2048]{1,0:T(8,128)(2,1)S(1)} %collective-permute-done.5.high, bf16[1,8192,1024]{2,1,0:T(8,128)(2,1)} %query_weight.3, ...), custom_call_target="tpu_custom_call" | custom-call | flops 1342177280 | bytes 5242880 | tf_op jit(solution)/shard_map/pallas_call | solution.py:248
  94.4 7.4 %all-to-all-start = ((bf16[32,2,16,1024]{3,2,1,0:T(8,128)(2,1)}), bf16[32,2,16,1024]{3,2,1,0:T(8,128)(2,1)S(1)}, u32[]{:S(2)}, u32[]{:S(2)}) async-start(bf16[32,2,16,1024]{3,2,1,0:T(8,128)(2,1)} %get-tuple-element.8), calls=%async_computation | async-start | bytes 4194304 | tf_op jit(solution)/shard_map/all_to_all | solution.py:268
  101.8 0.1 collective-permute-start.13
  101.9 3.5 %collective-permute-done.13 = f32[1,128]{1,0:T(1,128)S(1)} collective-permute-done((f32[1,128]{1,0:T(1,128)S(1)}, f32[1,128]{1,0:T(1,128)S(1)}, u32[]{:S(2)}, u32[]{:S(2)}) %collective-permute-start.13) | collective-permute-done | bytes 544 | tf_op jit(solution)/shard_map/ppermute | solution.py:271
  105.4 0.0 collective-permute-start.14
  105.4 5.0 %collective-permute-done.14 = f32[1,128]{1,0:T(1,128)S(1)} collective-permute-done((f32[1,128]{1,0:T(1,128)S(1)}, f32[1,128]{1,0:T(1,128)S(1)}, u32[]{:S(2)}, u32[]{:S(2)}) %collective-permute-start.14) | collective-permute-done | bytes 544 | tf_op jit(solution)/shard_map/ppermute | solution.py:271
  110.4 0.0 collective-permute-start.15
  110.4 1.1 collective-permute-done.15
  111.6 1.8 %collective-permute-start.16 = (f32[1,128]{1,0:T(1,128)S(1)}, f32[1,128]{1,0:T(1,128)S(1)}, u32[]{:S(2)}, u32[]{:S(2)}) collective-permute-start(f32[1,128]{1,0:T(1,128)S(1)} %add.113), channel_id=1, source_target_pairs={{0,8},{4,12},{8,0},{12,4},{16,24},{20,28},{24,16},{28,20},{32,40},... | collective-permute-start | bytes 1544 | tf_op jit(solution)/shard_map/ppermute | solution.py:274
  113.4 11.6 %collective-permute-done.16 = f32[1,128]{1,0:T(1,128)S(1)} collective-permute-done((f32[1,128]{1,0:T(1,128)S(1)}, f32[1,128]{1,0:T(1,128)S(1)}, u32[]{:S(2)}, u32[]{:S(2)}) %collective-permute-start.16) | collective-permute-done | bytes 544 | tf_op jit(solution)/shard_map/ppermute | solution.py:274
  125.0 0.0 collective-permute-start.17
  125.0 5.5 %collective-permute-done.17 = f32[1,128]{1,0:T(1,128)S(1)} collective-permute-done((f32[1,128]{1,0:T(1,128)S(1)}, f32[1,128]{1,0:T(1,128)S(1)}, u32[]{:S(2)}, u32[]{:S(2)}) %collective-permute-start.17) | collective-permute-done | bytes 544 | tf_op jit(solution)/shard_map/ppermute | solution.py:274
  130.5 3.0 %collective-permute-start.18 = (f32[1,128]{1,0:T(1,128)S(1)}, f32[1,128]{1,0:T(1,128)S(1)}, u32[]{:S(2)}, u32[]{:S(2)}) collective-permute-start(f32[1,128]{1,0:T(1,128)S(1)} %add.115), channel_id=1, source_target_pairs={{0,32},{4,36},{8,40},{12,44},{16,48},{20,52},{24,56},{28,60},{32,0... | collective-permute-start | bytes 1544 | tf_op jit(solution)/shard_map/ppermute | solution.py:274
  133.5 1.5 %collective-permute-done.18 = f32[1,128]{1,0:T(1,128)S(1)} collective-permute-done((f32[1,128]{1,0:T(1,128)S(1)}, f32[1,128]{1,0:T(1,128)S(1)}, u32[]{:S(2)}, u32[]{:S(2)}) %collective-permute-start.18) | collective-permute-done | bytes 544 | tf_op jit(solution)/shard_map/ppermute | solution.py:274
  135.0 3.7 %collective-permute-start.19 = (f32[1,128]{1,0:T(1,128)S(1)}, f32[1,128]{1,0:T(1,128)S(1)}, u32[]{:S(2)}, u32[]{:S(2)}) collective-permute-start(f32[1,128]{1,0:T(1,128)S(1)} %add.116), channel_id=1, source_target_pairs={{0,64},{4,68},{8,72},{12,76},{16,80},{20,84},{24,88},{28,92},{32,9... | collective-permute-start | bytes 1544 | tf_op jit(solution)/shard_map/ppermute | solution.py:274
  138.7 0.6 dynamic_slice.23
  139.3 0.9 collective-permute-done.19
  140.2 0.6 constant_dynamic-slice_fusion
  140.8 1.3 fusion.1
  143.4 0.0 all-to-all-done
  143.4 1.3 copy.13
  (14 shorter events, 0.0 us)
Async XLA Ops:
  0.6 11.8 %copy-start.2 = (s32[32,1]{0,1:T(1,128)S(1)}, s32[32,1]{0,1:T(1,128)}, u32[]{:S(2)}) copy-start(s32[32,1]{0,1:T(1,128)} %param.13) | copy-start | bytes 388
  0.6 12.0 %copy-start.1 = (s32[32]{0:T(128)S(1)}, s32[32]{0:T(128)}, u32[]{:S(2)}) copy-start(s32[32]{0:T(128)} %param.11) | copy-start | bytes 388
  1.9 16.5 %collective-permute-start.3 = (bf16[128,2048]{1,0:T(8,128)(2,1)S(1)}, bf16[128,2048]{1,0:T(8,128)(2,1)S(1)}, u32[]{:S(2)}, u32[]{:S(2)}) collective-permute-start(bf16[128,2048]{1,0:T(8,128)(2,1)S(1)} %get-tuple-element.12.refs_1_), channel_id=1, source_target_pairs={{0,3},{1,0},{2,1},{3,2},{4,7},{5,4},{6,5},{7,6},{8,11},{9,8},{10,9... | collective-permute-start | bytes 1572872 | tf_op jit(solution)/shard_map/ppermute | solution.py:180
  6.1 25.8 %collective-permute-start.11 = (bf16[128,2048]{1,0:T(8,128)(2,1)S(1)}, bf16[128,2048]{1,0:T(8,128)(2,1)S(1)}, u32[]{:S(2)}, u32[]{:S(2)}) collective-permute-start(bf16[128,2048]{1,0:T(8,128)(2,1)S(1)} %get-tuple-element.12.refs_1_), channel_id=1, source_target_pairs={{0,1},{1,2},{2,3},{3,0},{4,5},{5,6},{6,7},{7,4},{8,9},{9,10},{10,1... | collective-permute-start | bytes 1572872 | tf_op jit(solution)/shard_map/ppermute | solution.py:182
  6.1 25.8 %collective-permute-start = (bf16[128,2048]{1,0:T(8,128)(2,1)S(1)}, bf16[128,2048]{1,0:T(8,128)(2,1)S(1)}, u32[]{:S(2)}, u32[]{:S(2)}) collective-permute-start(bf16[128,2048]{1,0:T(8,128)(2,1)S(1)} %get-tuple-element.13.refs_0_), channel_id=1, source_target_pairs={{0,1},{1,2},{2,3},{3,0},{4,5},{5,6},{6,7},{7,4},{8,9},{9,10},{10,1... | collective-permute-start | bytes 1572872 | tf_op jit(solution)/shard_map/ppermute | solution.py:179
  6.1 33.9 %collective-permute-start.12 = (bf16[128,2048]{1,0:T(8,128)(2,1)S(1)}, bf16[128,2048]{1,0:T(8,128)(2,1)S(1)}, u32[]{:S(2)}, u32[]{:S(2)}) collective-permute-start(bf16[128,2048]{1,0:T(8,128)(2,1)S(1)} %get-tuple-element.13.refs_0_), channel_id=1, source_target_pairs={{0,3},{1,0},{2,1},{3,2},{4,7},{5,4},{6,5},{7,6},{8,11},{9,8},{10,9... | collective-permute-start | bytes 1572872 | tf_op jit(solution)/shard_map/ppermute | solution.py:183
  9.4 26.2 %collective-permute-start.6 = (bf16[256,2048]{1,0:T(8,128)(2,1)}, bf16[256,2048]{1,0:T(8,128)(2,1)}, u32[]{:S(2)}, u32[]{:S(2)}) collective-permute-start(bf16[256,2048]{1,0:T(8,128)(2,1)} %bitcast.8), channel_id=1, source_target_pairs={{0,64},{4,68},{8,72},{12,76},{16,80},{20,84},{24,88},{28,92},{32,9... | collective-permute-start | bytes 3145736 | tf_op jit(solution)/shard_map/ppermute | solution.py:181
  18.5 21.6 %collective-permute-start.10 = (bf16[128,2048]{1,0:T(8,128)(2,1)S(1)}, bf16[128,2048]{1,0:T(8,128)(2,1)S(1)}, u32[]{:S(2)}, u32[]{:S(2)}) collective-permute-start(bf16[128,2048]{1,0:T(8,128)(2,1)S(1)} %collective-permute-done.3.refs_5_), channel_id=1, source_target_pairs={{0,3},{1,0},{2,1},{3,2},{4,7},{5,4},{6,5},{7,6},{8,11},{9,8},{10,9... | collective-permute-start | bytes 1572872 | tf_op jit(solution)/shard_map/ppermute | solution.py:185
  32.0 38.0 %collective-permute-start.9 = (bf16[128,2048]{1,0:T(8,128)(2,1)S(1)}, bf16[128,2048]{1,0:T(8,128)(2,1)S(1)}, u32[]{:S(2)}, u32[]{:S(2)}) collective-permute-start(bf16[128,2048]{1,0:T(8,128)(2,1)S(1)} %collective-permute-done.refs_2_), channel_id=1, source_target_pairs={{0,1},{1,2},{2,3},{3,0},{4,5},{5,6},{6,7},{7,4},{8,9},{9,10},{10,1... | collective-permute-start | bytes 1572872 | tf_op jit(solution)/shard_map/ppermute | solution.py:184
  32.0 17.5 %collective-permute-start.1 = (bf16[128,2048]{1,0:T(8,128)(2,1)S(1)}, bf16[128,2048]{1,0:T(8,128)(2,1)S(1)}, u32[]{:S(2)}, u32[]{:S(2)}) collective-permute-start(bf16[128,2048]{1,0:T(8,128)(2,1)S(1)} %collective-permute-done.refs_2_), channel_id=1, source_target_pairs={{0,64},{4,68},{8,72},{12,76},{16,80},{20,84},{24,88},{28,92},{32,9... | collective-permute-start | bytes 1572872 | tf_op jit(solution)/shard_map/ppermute | solution.py:187
  35.6 22.1 %collective-permute-start.4 = (bf16[128,2048]{1,0:T(8,128)(2,1)S(1)}, bf16[128,2048]{1,0:T(8,128)(2,1)S(1)}, u32[]{:S(2)}, u32[]{:S(2)}) collective-permute-start(bf16[128,2048]{1,0:T(8,128)(2,1)S(1)} %collective-permute-done.3.refs_5_), channel_id=1, source_target_pairs={{0,64},{4,68},{8,72},{12,76},{16,80},{20,84},{24,88},{28,92},{32,9... | collective-permute-start | bytes 1572872 | tf_op jit(solution)/shard_map/ppermute | solution.py:188
  40.0 36.1 %collective-permute-start.7 = (bf16[128,2048]{1,0:T(8,128)(2,1)S(1)}, bf16[128,2048]{1,0:T(8,128)(2,1)S(1)}, u32[]{:S(2)}, u32[]{:S(2)}) collective-permute-start(bf16[128,2048]{1,0:T(8,128)(2,1)S(1)} %get-tuple-element.10.refs_1_), channel_id=1, source_target_pairs={{0,1},{1,2},{2,3},{3,0},{4,5},{5,6},{6,7},{7,4},{8,9},{9,10},{10,1... | collective-permute-start | bytes 1572872 | tf_op jit(solution)/shard_map/ppermute | solution.py:189
  40.1 36.0 %collective-permute-start.8 = (bf16[128,2048]{1,0:T(8,128)(2,1)S(1)}, bf16[128,2048]{1,0:T(8,128)(2,1)S(1)}, u32[]{:S(2)}, u32[]{:S(2)}) collective-permute-start(bf16[128,2048]{1,0:T(8,128)(2,1)S(1)} %get-tuple-element.11.refs_0_), channel_id=1, source_target_pairs={{0,3},{1,0},{2,1},{3,2},{4,7},{5,4},{6,5},{7,6},{8,11},{9,8},{10,9... | collective-permute-start | bytes 1572872 | tf_op jit(solution)/shard_map/ppermute | solution.py:190
  49.5 36.3 %collective-permute-start.2 = (bf16[128,2048]{1,0:T(8,128)(2,1)S(1)}, bf16[128,2048]{1,0:T(8,128)(2,1)S(1)}, u32[]{:S(2)}, u32[]{:S(2)}) collective-permute-start(bf16[128,2048]{1,0:T(8,128)(2,1)S(1)} %collective-permute-done.1.refs_2_), channel_id=1, source_target_pairs={{0,1},{1,2},{2,3},{3,0},{4,5},{5,6},{6,7},{7,4},{8,9},{9,10},{10,1... | collective-permute-start | bytes 1572872 | tf_op jit(solution)/shard_map/ppermute | solution.py:191
  57.6 28.2 %collective-permute-start.5 = (bf16[128,2048]{1,0:T(8,128)(2,1)S(1)}, bf16[128,2048]{1,0:T(8,128)(2,1)S(1)}, u32[]{:S(2)}, u32[]{:S(2)}) collective-permute-start(bf16[128,2048]{1,0:T(8,128)(2,1)S(1)} %collective-permute-done.4.refs_5_), channel_id=1, source_target_pairs={{0,3},{1,0},{2,1},{3,2},{4,7},{5,4},{6,5},{7,6},{8,11},{9,8},{10,9... | collective-permute-start | bytes 1572872 | tf_op jit(solution)/shard_map/ppermute | solution.py:192
  60.2 9.7 %copy-start = (f32[1024]{0:T(1024)S(1)}, f32[1024]{0:T(1024)}, u32[]{:S(2)}) copy-start(f32[1024]{0:T(1024)} %param.10) | copy-start | bytes 12292
  94.4 44.3 %copy-start.3 = (s32[32]{0:T(128)S(1)}, s32[32]{0:T(128)}, u32[]{:S(2)}) copy-start(s32[32]{0:T(128)} %param.12) | copy-start | bytes 388
  94.4 49.0 %all-to-all-start = ((bf16[32,2,16,1024]{3,2,1,0:T(8,128)(2,1)}), bf16[32,2,16,1024]{3,2,1,0:T(8,128)(2,1)S(1)}, u32[]{:S(2)}, u32[]{:S(2)}) async-start(bf16[32,2,16,1024]{3,2,1,0:T(8,128)(2,1)} %get-tuple-element.8), calls=%async_computation | async-start | bytes 4194304 | tf_op jit(solution)/shard_map/all_to_all | solution.py:268
  101.8 3.6 %collective-permute-start.13 = (f32[1,128]{1,0:T(1,128)S(1)}, f32[1,128]{1,0:T(1,128)S(1)}, u32[]{:S(2)}, u32[]{:S(2)}) collective-permute-start(f32[1,128]{1,0:T(1,128)S(1)} %get-tuple-element.9), channel_id=1, source_target_pairs={{0,1},{1,0},{2,3},{3,2},{4,5},{5,4},{6,7},{7,6},{8,9},{9,8},{10,11... | collective-permute-start | bytes 1544 | tf_op jit(solution)/shard_map/ppermute | solution.py:271
  105.4 5.0 %collective-permute-start.14 = (f32[1,128]{1,0:T(1,128)S(1)}, f32[1,128]{1,0:T(1,128)S(1)}, u32[]{:S(2)}, u32[]{:S(2)}) collective-permute-start(f32[1,128]{1,0:T(1,128)S(1)} %add.111), channel_id=1, source_target_pairs={{0,2},{1,3},{2,0},{3,1},{4,6},{5,7},{6,4},{7,5},{8,10},{9,11},{10,... | collective-permute-start | bytes 1544 | tf_op jit(solution)/shard_map/ppermute | solution.py:271
  110.4 1.1 collective-permute-start.15
  111.6 13.4 %collective-permute-start.16 = (f32[1,128]{1,0:T(1,128)S(1)}, f32[1,128]{1,0:T(1,128)S(1)}, u32[]{:S(2)}, u32[]{:S(2)}) collective-permute-start(f32[1,128]{1,0:T(1,128)S(1)} %add.113), channel_id=1, source_target_pairs={{0,8},{4,12},{8,0},{12,4},{16,24},{20,28},{24,16},{28,20},{32,40},... | collective-permute-start | bytes 1544 | tf_op jit(solution)/shard_map/ppermute | solution.py:274
  125.0 5.5 %collective-permute-start.17 = (f32[1,128]{1,0:T(1,128)S(1)}, f32[1,128]{1,0:T(1,128)S(1)}, u32[]{:S(2)}, u32[]{:S(2)}) collective-permute-start(f32[1,128]{1,0:T(1,128)S(1)} %add.114), channel_id=1, source_target_pairs={{0,16},{4,20},{8,24},{12,28},{16,0},{20,4},{24,8},{28,12},{32,48},... | collective-permute-start | bytes 1544 | tf_op jit(solution)/shard_map/ppermute | solution.py:274
  130.5 4.5 %collective-permute-start.18 = (f32[1,128]{1,0:T(1,128)S(1)}, f32[1,128]{1,0:T(1,128)S(1)}, u32[]{:S(2)}, u32[]{:S(2)}) collective-permute-start(f32[1,128]{1,0:T(1,128)S(1)} %add.115), channel_id=1, source_target_pairs={{0,32},{4,36},{8,40},{12,44},{16,48},{20,52},{24,56},{28,60},{32,0... | collective-permute-start | bytes 1544 | tf_op jit(solution)/shard_map/ppermute | solution.py:274
  135.0 5.2 %collective-permute-start.19 = (f32[1,128]{1,0:T(1,128)S(1)}, f32[1,128]{1,0:T(1,128)S(1)}, u32[]{:S(2)}, u32[]{:S(2)}) collective-permute-start(f32[1,128]{1,0:T(1,128)S(1)} %add.116), channel_id=1, source_target_pairs={{0,64},{4,68},{8,72},{12,76},{16,80},{20,84},{24,88},{28,92},{32,9... | collective-permute-start | bytes 1544 | tf_op jit(solution)/shard_map/ppermute | solution.py:274

commit v2 on v1

v2 whole, which is shorter than its diff:
```python
import functools
import math

import jax
import jax.numpy as jnp
from jax import lax
from jax.experimental import pallas as pl
from jax.experimental.pallas import tpu as pltpu
from jax.sharding import PartitionSpec as P

HD = 128
BLK = 16
GSIZE = 4
LANES = 128
START_TILE = 1024
MIDDLE_TILE = 2048
LAST_TILE = 1024
END = 80
PASSED = 80
PLANE = ("section", "dp")
VMEM_LIMIT = 32 * 1024 * 1024


def x_opposite(sections, dp_size):
    count = sections * dp_size
    return [(i, (i + dp_size) % count) for i in range(count)]


def ring(size, step):
    return [(i, (i + step) % size) for i in range(size)]


def turn(count, span, size, step):
    return [(i, i + ((i // span + step) % size - i // span % size) * span) for i in range(count)]


def project(parts, query_weight, keyval_weight, total):
    features = query_weight.shape[-1]
    rows = jnp.concatenate(parts, axis=0)
    total[:, :features] += jnp.dot(rows, query_weight[0], preferred_element_type=jnp.float32)
    total[:, features:] += jnp.dot(rows, keyval_weight[...], preferred_element_type=jnp.float32)


def project_kernel(depth_steps, number, places, *refs):
    parts, (partial, query_weight, keyval_weight, total) = refs[:-4], refs[-4:]
    step = pl.program_id(0)

    @pl.when(step == 0)
    def _():
        total[...] = jnp.zeros_like(total) if partial is None else partial[...]

    each = len(parts) // number
    depth = query_weight.shape[1]
    columns = pl.ds(pl.multiple_of(lax.rem(step, depth_steps) * depth, depth), depth)
    for piece in range(number):
        @pl.when(step // depth_steps == piece)
        def _():
            held = [part[:, columns] for part in parts[piece * each:(piece + 1) * each]]
            project(held, query_weight, keyval_weight, total)


def start_kernel(depth_steps, places, *refs):
    project_kernel(depth_steps, 1, places, *refs[:-3], None, *refs[-3:])


def attend(total, features, length, states, base):
    seq = total.shape[0]
    half = seq // 2
    keys = total[:, features:features + HD].astype(jnp.bfloat16)
    values = total[:, features + HD:features + 2 * HD].astype(jnp.bfloat16)
    values = jnp.concatenate([values, jnp.ones_like(values)], axis=1)
    scale = math.log2(math.e) / math.sqrt(HD)
    for head in range(features // HD):
        cols = pl.ds(head * HD, HD)
        for begin, size in ((0, half), (half, half)):
            reach = begin + size
            query = total[begin:reach, cols].astype(jnp.bfloat16)
            scores = lax.dot_general(
                query, keys[:reach], (((1,), (1,)), ((), ())), preferred_element_type=jnp.float32
            )
            token = lax.broadcasted_iota(jnp.int32, scores.shape, 0) + begin
            place = lax.broadcasted_iota(jnp.int32, scores.shape, 1)
            scores = jnp.where(place <= token, scores, -1e30)
            highest = jnp.max(scores, axis=1, keepdims=True)
            weights = jnp.exp2((scores - highest) * scale).astype(jnp.bfloat16)
            mixed = jnp.dot(weights, values[:reach], preferred_element_type=jnp.float32)
            output = mixed[:, :HD] / mixed[:, HD:]
            token = lax.broadcasted_iota(jnp.int32, output.shape, 0) + begin
            output = jnp.where(token < length, output, 0.0)
            states[pl.ds(base + begin, size), cols] = output.astype(jnp.bfloat16)


def row_reward(states, base, seq, head, scale, place):
    terms = states[pl.ds(base, seq), :].astype(jnp.float32) * head[...]
    summed = jnp.sum(jnp.sum(terms, axis=0, keepdims=True), axis=1, keepdims=True) * scale
    lane = lax.broadcasted_iota(jnp.int32, (1, LANES), 1)
    return jnp.where(lane == place, jnp.broadcast_to(summed, (1, LANES)), 0.0)


def row_kernel(depth_steps, places, *refs):
    parts, (head, scale, earlier, states, reward, total) = refs[:-6], refs[-6:]
    project_kernel(depth_steps, 1, places, *parts, total)

    @pl.when(pl.program_id(0) == pl.num_programs(0) - 1)
    def _():
        attend(total, states.shape[1], places[1], states, 0)
        reward[...] = earlier[...] + row_reward(states, 0, total.shape[0], head, scale[...], places[2])


def place_kernel(slots, first, second, outgoing):
    shards, most = outgoing.shape[0], outgoing.shape[1]
    seq = first.shape[0]

    def fill(shard, carry):
        for k in range(most):
            block = slots[shard * most + k]
            rows = pl.ds(pl.multiple_of(lax.rem(jnp.maximum(block, 0), seq // BLK) * BLK, BLK), BLK)
            held = jnp.where(block < seq // BLK, first[rows, :], second[rows, :])
            outgoing[shard, k] = jnp.where(block >= 0, held, jnp.zeros_like(held))
        return carry

    lax.fori_loop(0, shards, fill, 0, unroll=4)


def advantage_kernel(rewards, shares, advantage):
    advantage[...] = jnp.sum(rewards[...] * shares[...], axis=1, keepdims=True)


def whole(shape):
    return pl.BlockSpec(shape, lambda i, places: (0,) * len(shape))


def weight_specs(tile, depth_steps, features):
    def place(i, places):
        return places[i // depth_steps] * depth_steps + i % depth_steps

    return [
        pl.BlockSpec((1, tile, features), lambda i, places: (0, place(i, places), 0)),
        pl.BlockSpec((tile, 2 * HD), lambda i, places: (place(i, places), 0)),
    ]


def estimate(seq, depth, width):
    return pl.CostEstimate(flops=2 * seq * depth * width, bytes_accessed=2 * depth * width, transcendentals=0)


def body(hidden, query_weight, keyval_weight, reward_head, lengths, group_ids, dest):
    sections = lax.axis_size("section")
    dp_size = lax.axis_size("dp")
    mp_size = lax.axis_size("mp")
    section_idx = lax.axis_index("section")
    dp_idx = lax.axis_index("dp")
    mp_idx = lax.axis_index("mp")
    total_rows = lengths.shape[0]
    own = section_idx * dp_size + dp_idx
    other = (1 - section_idx) * dp_size + dp_idx

    seq, depth = hidden.shape[1], hidden.shape[2]
    features = query_weight.shape[2]
    width = features + 2 * HD
    half = seq // 2
    keyval_weight = keyval_weight.reshape(keyval_weight.shape[1], 2 * HD)

    up = functools.partial(lax.ppermute, axis_name="mp", perm=ring(mp_size, 1))
    down = functools.partial(lax.ppermute, axis_name="mp", perm=ring(mp_size, -1))
    across = functools.partial(lax.ppermute, axis_name=PLANE, perm=x_opposite(sections, dp_size))

    block_count = dest.shape[0]
    most = max(2, 2 * block_count // total_rows)
    targets = dest[:, 0]
    order = jnp.arange(block_count, dtype=jnp.int32)
    same = (targets[:, None] == targets[None, :]) & (order[None, :] < order[:, None])
    slot = targets * most + jnp.sum(same.astype(jnp.int32), axis=1)
    held = jnp.where(section_idx == 0, order, (order + block_count // 2) % block_count)
    hit = jnp.arange(total_rows * most, dtype=jnp.int32)[:, None] == slot[None, :]
    source = jnp.sum(jnp.where(hit, held[None, :] + 1, 0), axis=1) - 1

    mine = hidden[0]
    below, above = up(mine), down(mine)
    theirs = across(mine)

    below_idx, above_idx, far_idx = (mp_idx + mp_size - 1) % mp_size, (mp_idx + 1) % mp_size, (mp_idx + 2) % mp_size
    head = reward_head.reshape(1, features)
    reward_scale = jnp.where(section_idx == 1, 1.0 / lengths.astype(jnp.float32), 0.0)

    rows = jnp.arange(total_rows)
    shares = jnp.where(rows == own, 1.0, 0.0) - jnp.where(group_ids == group_ids[own], 1.0 / GSIZE, 0.0)
    shares = jnp.pad(shares, (0, LANES - total_rows)).reshape(1, LANES)

    def indices(*values):
        return jnp.stack([jnp.asarray(value, jnp.int32) for value in values])

    def call(kernel, tile, pieces, places, operands, in_specs, out_specs, out_shape, scratch=()):
        depth_steps = depth // tile
        return pl.pallas_call(
            functools.partial(kernel, depth_steps),
            grid_spec=pltpu.PrefetchScalarGridSpec(
                num_scalar_prefetch=1,
                grid=(depth_steps * pieces,),
                in_specs=in_specs[:-1] + weight_specs(tile, depth_steps, features) + in_specs[-1],
                out_specs=out_specs,
                scratch_shapes=scratch,
            ),
            out_shape=out_shape,
            compiler_params=pltpu.CompilerParams(vmem_limit_bytes=VMEM_LIMIT),
            cost_estimate=estimate(seq, depth * pieces, width),
        )(places, *operands[:-1], query_weight, keyval_weight, *operands[-1])

    total_spec = whole((seq, width))

    def start(piece):
        return call(
            start_kernel, START_TILE, 1, indices(mp_idx), [piece, []], [whole((seq, depth)), []],
            total_spec, jax.ShapeDtypeStruct((seq, width), jnp.float32),
        )

    def middle(parts, total):
        return call(
            lambda steps, *refs: project_kernel(steps, 2, *refs), MIDDLE_TILE, 2, indices(below_idx, above_idx),
            [*parts, total, []], [whole(part.shape) for part in parts] + [total_spec, []],
            total_spec, jax.ShapeDtypeStruct((seq, width), jnp.float32),
        )

    def finish(parts, partial, row, earlier):
        return call(
            row_kernel, LAST_TILE, 1, indices(far_idx, lengths[row], row),
            [*parts, partial, [head, reward_scale[row].reshape(1, 1), earlier]],
            [whole(part.shape) for part in parts]
            + [total_spec, [whole((1, features)), whole((1, 1)), whole((1, LANES))]],
            [whole((seq, features)), whole((1, LANES))],
            [jax.ShapeDtypeStruct((seq, features), jnp.bfloat16), jax.ShapeDtypeStruct((1, LANES), jnp.float32)],
            [pltpu.VMEM((seq, width), jnp.float32)],
        )

    def ahead(*arrays):
        return lax.optimization_barrier(arrays)

    own_start = start(mine)
    below, above, own_start = ahead(below, above, own_start)
    far_low, far_high = up(below[:half]), down(above[half:])
    crossed = across(jnp.concatenate([below[:END], above[seq - END:]], axis=0))
    theirs, below, above = ahead(theirs, below, above)
    own_partial = middle([below, above], own_start)
    theirs, own_partial = ahead(theirs, own_partial)
    their_below_high, their_above_low = up(theirs[END:]), down(theirs[:seq - END])
    theirs, far_low, far_high = ahead(theirs, far_low, far_high)
    far_middle = across(jnp.concatenate([far_low[PASSED:], far_high[:half - PASSED]], axis=0))
    own_states, own_reward = finish([far_low, far_high], own_partial, own, jnp.zeros((1, LANES), jnp.float32))
    their_start = start(theirs)
    crossed, own_states = ahead(crossed, own_states)
    their_far_low, their_far_high = up(crossed[:PASSED]), down(crossed[2 * END - PASSED:])
    their_partial = middle([crossed[:END], their_below_high, their_above_low, crossed[END:]], their_start)
    their_states, rewards = finish([their_far_low, far_middle, their_far_high], their_partial, other, own_reward)

    block_spec = pl.BlockSpec((seq, features), lambda i, slots: (0, 0))
    outgoing = pl.pallas_call(
        place_kernel,
        grid_spec=pltpu.PrefetchScalarGridSpec(
            num_scalar_prefetch=1,
            grid=(1,),
            in_specs=[block_spec, block_spec],
            out_specs=pl.BlockSpec((total_rows, most, BLK, features), lambda i, slots: (0, 0, 0, 0)),
        ),
        out_shape=jax.ShapeDtypeStruct((total_rows, most, BLK, features), jnp.bfloat16),
        compiler_params=pltpu.CompilerParams(vmem_limit_bytes=VMEM_LIMIT),
        cost_estimate=pl.CostEstimate(flops=0, bytes_accessed=6 * seq * features, transcendentals=0),
    )(source, own_states, their_states)
    received = lax.all_to_all(outgoing, PLANE, split_axis=0, concat_axis=0, tiled=True)

    rewards += sum(lax.ppermute(rewards, "mp", ring(mp_size, step)) for step in range(1, mp_size))
    cores = 2
    across_size = sections * 2
    along = sections * dp_size // (cores * across_size)
    for span, size in ((1, cores), (cores, along), (cores * along, across_size)):
        rewards += sum(lax.ppermute(rewards, PLANE, turn(sections * dp_size, span, size, step)) for step in range(1, size))
    advantage = pl.pallas_call(
        advantage_kernel, out_shape=jax.ShapeDtypeStruct((1, 1), jnp.float32)
    )(rewards, shares)
    return (received[None], advantage.reshape(1))


def solution(mesh):
    return jax.shard_map(
        body,
        mesh=mesh,
        in_specs=(
            P(("section", "dp"), None, "mp"),
            P("section", None, "mp"),
            P("section", None, None, "mp"),
            P("mp"),
            P(),
            P(),
            P(("section", "dp"), None),
        ),
        out_specs=(P(("section", "dp"), None, None, None, "mp"), P(("section", "dp"))),
        check_vma=False,
    )
```

time: 147 us -> 126 us (0.86)
  waiting for transfers between devices: 52.2 us -> 37.4 us
  starting transfers between devices: 42.3 us -> 36.4 us
  between operations: 3.31 us -> 0.9 us
    ppermute x20 -> x21, waiting for transfers between devices: 52.2 us -> 37.4 us  [the longest x7 12.7 us: body(): lax.ppermute(rewards, PLANE, turn(sections * dp_size, span, size, step))]
    ppermute x20 -> x21, starting transfers between devices: 34.9 us -> 30.9 us  [the longest x7 13 us: body(): lax.ppermute(rewards, PLANE, turn(sections * dp_size, span, size, step))]
    unnamed x10 -> x16, local copies, waits for them, and re-layouts: 6.01 us -> 9.48 us
    all_to_all x1, starting transfers between devices: 7.36 us -> 5.56 us  [body(): lax.all_to_all(outgoing, PLANE, split_axis=0, concat_axis=0, tiled=True)]
    pallas_call x4 -> x8, Pallas kernels: 34.1 us -> 34.5 us  [the longest x6 31 us: call(): pl.pallas_call(functools.partial(kernel, depth_steps), grid_spec=pltpu.Pr...]
  transfers between devices with their start and end apart: 21 -> 22, of which waited for: 11 -> 11; matrix products, arithmetic and copies ran while one was open for 8% -> 9% of each run, Pallas kernels for 18% -> 21%
where the time goes in v2:
time: 126 us; the launch traced here: 125 us
  waiting for transfers between devices  37.4 us (30%)
  starting transfers between devices  36.4 us (29%)
  Pallas kernels  34.5 us (27%)
  local copies, waits for them, and re-layouts  12.3 us (10%)
  other arithmetic  3.79 us (3%)
    pallas_call x6, Pallas kernels, call(): pl.pallas_call(functools.partial(kernel, depth_steps), grid_spec=pltpu.Pr...  31 us
    ppermute x7, starting transfers between devices, body(): lax.ppermute(rewards, PLANE, turn(sections * dp_size, span, size, step))  13 us
    ppermute x7, waiting for transfers between devices, body(): lax.ppermute(rewards, PLANE, turn(sections * dp_size, span, size, step))  12.7 us
    ppermute x2, waiting for transfers between devices, body(): below, above = (up(mine), down(mine))  10.2 us
    unnamed x16, local copies, waits for them, and re-layouts  9.48 us
    ppermute x1, waiting for transfers between devices, body(): crossed = across(jnp.concatenate([below[:END], above[seq - END:]], axis=0))  5.79 us
    all_to_all x1, starting transfers between devices, body(): lax.all_to_all(outgoing, PLANE, split_axis=0, concat_axis=0, tiled=True)  5.56 us
    ppermute x2, waiting for transfers between devices, body(): far_low, far_high = (up(below[:half]), down(above[half:]))  4.49 us
  transfers between devices with their start and end apart: 22, of which 11 were waited for; matrix products, arithmetic and copies ran while one was open for 9% of the time, Pallas kernels for 21%

profile of v2, /device:TPU:0, one launch (start us, length us, event | category | flops | bytes accessed | tf_op | source)
XLA Modules:
  0.0 125.3 jit_solution(18253089994655218907)
XLA Ops:
  0.6 3.2 %collective-permute-start.3 = (bf16[256,2048]{1,0:T(8,128)(2,1)}, bf16[256,2048]{1,0:T(8,128)(2,1)S(1)}, u32[]{:S(2)}, u32[]{:S(2)}) collective-permute-start(bf16[256,2048]{1,0:T(8,128)(2,1)} %bitcast.28), channel_id=1, source_target_pairs={{0,64},{4,68},{8,72},{12,76},{16,80},{20,84},{24,88},{28,92},{32,9... | collective-permute-start | bytes 3145736 | tf_op jit(solution)/shard_map/ppermute | solution.py:180
  3.8 4.0 %collective-permute-start.1 = (bf16[256,2048]{1,0:T(8,128)(2,1)}, bf16[256,2048]{1,0:T(8,128)(2,1)S(1)}, u32[]{:S(2)}, u32[]{:S(2)}) collective-permute-start(bf16[256,2048]{1,0:T(8,128)(2,1)} %bitcast.29), channel_id=1, source_target_pairs={{0,3},{1,0},{2,1},{3,2},{4,7},{5,4},{6,5},{7,6},{8,11},{9,8},{10,9... | collective-permute-start | bytes 3145736 | tf_op jit(solution)/shard_map/ppermute | solution.py:179
  7.9 0.7 broadcast_select_fusion
  8.5 0.1 pad_add_fusion.1.refs_0_
  8.6 4.7 %copy.11 = bf16[1024,8,2,128]{3,1,2,0:T(8,128)(2,1)} copy(bf16[1024,8,2,128]{3,2,1,0:T(2,128)(2,1)} %bitcast.35) | data formatting | bytes 8388608
  13.3 0.6 fusion.7
  14.0 0.6 fusion.6
  14.6 0.7 pad_add_fusion.2.places
  15.3 0.7 pad_add_fusion.places
  16.0 0.2 convert_reduce_fusion
  16.2 0.1 select_reduce_fusion
  16.3 2.2 %copy-done = bf16[1024,8,2,128]{3,1,2,0:T(8,128)(2,1)S(1)} copy-done((bf16[1024,8,2,128]{3,1,2,0:T(8,128)(2,1)S(1)}, bf16[1024,8,2,128]{3,1,2,0:T(8,128)(2,1)}, u32[]{:S(2)}) %copy-start) | copy-done | bytes 4194328
  18.5 1.2 copy-done.2
  19.7 3.6 %shard_map.86.refs_3_ = f32[256,1280]{1,0:T(8,128)S(1)} custom-call(s32[1]{0:T(128)} %bitcast.2.places, bf16[256,2048]{1,0:T(8,128)(2,1)S(1)} %bitcast.31, bf16[1,8192,1024]{2,1,0:T(8,128)(2,1)} %refs_4_.3, bf16[8192,256]{1,0:T(8,128)(2,1)S(1)} %bitcast.22), custom_call_target="tpu_custom_call" | custom-call | flops 1342177280 | bytes 5242880 | tf_op jit(solution)/shard_map/pallas_call | solution.py:195
  23.4 6.9 %collective-permute-done.1.refs_2_ = bf16[256,2048]{1,0:T(8,128)(2,1)S(1)} collective-permute-done((bf16[256,2048]{1,0:T(8,128)(2,1)}, bf16[256,2048]{1,0:T(8,128)(2,1)S(1)}, u32[]{:S(2)}, u32[]{:S(2)}) %collective-permute-start.1) | collective-permute-done | bytes 1048608 | tf_op jit(solution)/shard_map/ppermute | solution.py:179
  30.3 3.3 %collective-permute-done.refs_1_ = bf16[256,2048]{1,0:T(8,128)(2,1)S(1)} collective-permute-done((bf16[256,2048]{1,0:T(8,128)(2,1)}, bf16[256,2048]{1,0:T(8,128)(2,1)S(1)}, u32[]{:S(2)}, u32[]{:S(2)}) %collective-permute-start) | collective-permute-done | bytes 1048608 | tf_op jit(solution)/shard_map/ppermute | solution.py:179
  33.8 0.0 collective-permute-done.3.refs_0_
  33.8 0.4 collective-permute-start.5
  34.1 1.7 %collective-permute-start.4 = (bf16[128,2048]{1,0:T(8,128)(2,1)S(1)}, bf16[128,2048]{1,0:T(8,128)(2,1)S(1)}, u32[]{:S(2)}, u32[]{:S(2)}) collective-permute-start(bf16[128,2048]{1,0:T(8,128)(2,1)S(1)} %slice.34), channel_id=1, source_target_pairs={{0,1},{1,2},{2,3},{3,0},{4,5},{5,6},{6,7},{7,4},{8,9},{9,10},{10,1... | collective-permute-start | bytes 1572872 | tf_op jit(solution)/shard_map/ppermute | solution.py:240
  35.9 6.0 %shard_map.87.refs_2_ = f32[256,1280]{1,0:T(8,128)S(1)} custom-call(s32[2]{0:T(128)S(1)} %pad_add_fusion.1.refs_0_, bf16[256,2048]{1,0:T(8,128)(2,1)S(1)} %collective-permute-done.refs_1_, bf16[256,2048]{1,0:T(8,128)(2,1)S(1)} %collective-permute-done.1.refs_2_, f32[256,1280]{1,0:T(8,128)S(1)} %shard_map.86.refs_3_, bf16[1,8192,1024]{2,1,0:T(8,128)(2,1)} %refs_4_.3, ...), custom_call_target="tpu_custom_call" | custom-call | flops 2684354560 | bytes 10485760 | tf_op jit(solution)/shard_map/pallas_call | solution.py:195
  41.9 0.6 collective-permute-start.2
  42.5 0.2 fusion.4
  42.7 0.0 copy-start.3
  42.7 1.6 %collective-permute-start.10 = (bf16[176,2048]{1,0:T(8,128)(2,1)S(1)}, bf16[176,2048]{1,0:T(8,128)(2,1)S(1)}, u32[]{:S(2)}, u32[]{:S(2)}) collective-permute-start(bf16[176,2048]{1,0:T(8,128)(2,1)S(1)} %get-tuple-element.36), channel_id=1, source_target_pairs={{0,3},{1,0},{2,1},{3,2},{4,7},{5,4},{6,5},{7,6},{8,11},{9,8},{10,9... | collective-permute-start | bytes 2162696 | tf_op jit(solution)/shard_map/ppermute | solution.py:245
  44.2 0.5 collective-permute-start.9
  44.8 3.9 %collective-permute-done.5.refs_1_ = bf16[128,2048]{1,0:T(8,128)(2,1)S(1)} collective-permute-done((bf16[128,2048]{1,0:T(8,128)(2,1)S(1)}, bf16[128,2048]{1,0:T(8,128)(2,1)S(1)}, u32[]{:S(2)}, u32[]{:S(2)}) %collective-permute-start.5) | collective-permute-done | bytes 524320 | tf_op jit(solution)/shard_map/ppermute | solution.py:240
  48.7 0.6 collective-permute-done.4.refs_0_
  49.3 0.1 collective-permute-start.7
  49.5 5.9 %shard_map.88 = (bf16[256,1024]{1,0:T(8,128)(2,1)S(1)}, f32[1,128]{1,0:T(1,128)S(1)}) custom-call(s32[3]{0:T(128)S(1)} %pad_add_fusion.places, bf16[128,2048]{1,0:T(8,128)(2,1)S(1)} %collective-permute-done.4.refs_0_, bf16[128,2048]{1,0:T(8,128)(2,1)S(1)} %collective-permute-done.5.refs_1_, f32[256,1280]{1,0:T(8,128)S(1)} %shard_map.87.refs_2_, ...), custom_call_target="tpu_custom_call" | custom-call | flops 1342177280 | bytes 5242880 | tf_op jit(solution)/shard_map/pallas_call | solution.py:195
  55.4 5.8 %collective-permute-done.2 = bf16[160,2048]{1,0:T(8,128)(2,1)S(1)} collective-permute-done((bf16[160,2048]{1,0:T(8,128)(2,1)S(1)}, bf16[160,2048]{1,0:T(8,128)(2,1)S(1)}, u32[]{:S(2)}, u32[]{:S(2)}) %collective-permute-start.2) | collective-permute-done | bytes 655392 | tf_op jit(solution)/shard_map/ppermute | solution.py:241
  61.2 1.6 %collective-permute-start.8 = (bf16[80,2048]{1,0:T(8,128)(2,1)S(1)}, bf16[80,2048]{1,0:T(8,128)(2,1)S(1)}, u32[]{:S(2)}, u32[]{:S(2)}) collective-permute-start(bf16[80,2048]{1,0:T(8,128)(2,1)S(1)} %get-tuple-element.38.refs_4_), channel_id=1, source_target_pairs={{0,3},{1,0},{2,1},{3,2},{4,7},{5,4},{6,5},{7,6},{8,11},{9,8},{10,9... | collective-permute-start | bytes 983048 | tf_op jit(solution)/shard_map/ppermute | solution.py:251
  62.8 0.5 collective-permute-start.6
  63.3 3.5 %shard_map.89.refs_5_ = f32[256,1280]{1,0:T(8,128)S(1)} custom-call(s32[1]{0:T(128)} %bitcast.2.places, bf16[256,2048]{1,0:T(8,128)(2,1)S(1)} %collective-permute-done.3.refs_0_, bf16[1,8192,1024]{2,1,0:T(8,128)(2,1)} %refs_4_.3, bf16[8192,256]{1,0:T(8,128)(2,1)S(1)} %bitcast.25), custom_call_target="tpu_custom_call" | custom-call | flops 1342177280 | bytes 5242880 | tf_op jit(solution)/shard_map/pallas_call | solution.py:195
  66.8 0.0 collective-permute-done.10.refs_3_
  66.8 0.0 collective-permute-done.9.refs_2_
  66.8 6.0 %shard_map.90.refs_3_ = f32[256,1280]{1,0:T(8,128)S(1)} custom-call(s32[2]{0:T(128)S(1)} %pad_add_fusion.1.refs_0_, bf16[80,2048]{1,0:T(8,128)(2,1)S(1)} %get-tuple-element.39.refs_1_, bf16[176,2048]{1,0:T(8,128)(2,1)S(1)} %collective-permute-done.9.refs_2_, bf16[176,2048]{1,0:T(8,128)(2,1)S(1)} %collective-permute-done.10.refs_3_, ...), custom_call_target="tpu_custom_call" | custom-call | flops 2684354560 | bytes 10485760 | tf_op jit(solution)/shard_map/pallas_call | solution.py:195
  72.8 0.0 collective-permute-done.6.refs_0_
  72.8 6.0 %shard_map.91 = (bf16[256,1024]{1,0:T(8,128)(2,1)S(1)}, f32[1,128]{1,0:T(1,128)S(1)}) custom-call(s32[3]{0:T(128)S(1)} %pad_add_fusion.2.places, bf16[80,2048]{1,0:T(8,128)(2,1)S(1)} %collective-permute-done.6.refs_0_, bf16[96,2048]{1,0:T(8,128)(2,1)S(1)} %collective-permute-done.7.refs_1_, bf16[80,2048]{1,0:T(8,128)(2,1)S(1)} %collective-permute-done.8.refs_2_, ...), custom_call_target="tpu_custom_call" | custom-call | flops 1342177280 | bytes 5242880 | tf_op jit(solution)/shard_map/pallas_call | solution.py:195
  78.9 2.2 %shard_map.92 = bf16[32,2,16,1024]{3,2,1,0:T(8,128)(2,1)} custom-call(s32[64]{0:T(128)S(1)} %broadcast_add_fusion.slots, bf16[256,1024]{1,0:T(8,128)(2,1)S(1)} %get-tuple-element.30.first, bf16[256,1024]{1,0:T(8,128)(2,1)S(1)} %get-tuple-element.34.second), custom_call_target="tpu_custom_call" | custom-call | bytes 1572864 | tf_op jit(solution)/shard_map/pallas_call | solution.py:256
  81.1 5.6 %all-to-all-start = ((bf16[32,2,16,1024]{3,2,1,0:T(8,128)(2,1)}), bf16[32,2,16,1024]{3,2,1,0:T(8,128)(2,1)S(1)}, u32[]{:S(2)}, u32[]{:S(2)}) async-start(bf16[32,2,16,1024]{3,2,1,0:T(8,128)(2,1)} %shard_map.92), calls=%async_computation | async-start | bytes 4194304 | tf_op jit(solution)/shard_map/all_to_all | solution.py:268
  86.6 2.8 %collective-permute-start.13 = (f32[1,128]{1,0:T(1,128)S(1)}, f32[1,128]{1,0:T(1,128)S(1)}, u32[]{:S(2)}, u32[]{:S(2)}) collective-permute-start(f32[1,128]{1,0:T(1,128)S(1)} %get-tuple-element.35), channel_id=1, source_target_pairs={{0,3},{1,0},{2,1},{3,2},{4,7},{5,4},{6,5},{7,6},{8,11},{9,8},{10,9... | collective-permute-start | bytes 1544 | tf_op jit(solution)/shard_map/ppermute | solution.py:270
  89.4 0.9 collective-permute-start.11
  90.4 0.3 collective-permute-done.13
  90.7 3.7 %collective-permute-done.12 = f32[1,128]{1,0:T(1,128)S(1)} collective-permute-done((f32[1,128]{1,0:T(1,128)S(1)}, f32[1,128]{1,0:T(1,128)S(1)}, u32[]{:S(2)}, u32[]{:S(2)}) %collective-permute-start.12) | collective-permute-done | bytes 544 | tf_op jit(solution)/shard_map/ppermute | solution.py:270
  94.5 0.0 collective-permute-done.11
  94.5 0.1 collective-permute-start.14
  94.6 0.7 dynamic_slice.19
  95.3 0.4 collective-permute-done.14
  95.7 3.0 %collective-permute-start.17 = (f32[1,128]{1,0:T(1,128)S(1)}, f32[1,128]{1,0:T(1,128)S(1)}, u32[]{:S(2)}, u32[]{:S(2)}) collective-permute-start(f32[1,128]{1,0:T(1,128)S(1)} %add.124), channel_id=1, source_target_pairs={{0,24},{4,28},{8,0},{12,4},{16,8},{20,12},{24,16},{28,20},{32,56},... | collective-permute-start | bytes 1544 | tf_op jit(solution)/shard_map/ppermute | solution.py:275
  98.7 0.9 collective-permute-start.16
  99.5 0.9 collective-permute-start.15
  100.4 0.7 fusion.1
  101.1 8.8 %collective-permute-done.17 = f32[1,128]{1,0:T(1,128)S(1)} collective-permute-done((f32[1,128]{1,0:T(1,128)S(1)}, f32[1,128]{1,0:T(1,128)S(1)}, u32[]{:S(2)}, u32[]{:S(2)}) %collective-permute-start.17) | collective-permute-done | bytes 544 | tf_op jit(solution)/shard_map/ppermute | solution.py:275
  109.9 0.0 collective-permute-done.15
  109.9 6.6 %collective-permute-start.20 = (f32[1,128]{1,0:T(1,128)S(1)}, f32[1,128]{1,0:T(1,128)S(1)}, u32[]{:S(2)}, u32[]{:S(2)}) collective-permute-start(f32[1,128]{1,0:T(1,128)S(1)} %add_add_fusion.1), channel_id=1, source_target_pairs={{0,96},{4,100},{8,104},{12,108},{16,112},{20,116},{24,120},{28,124... | collective-permute-start | bytes 1544 | tf_op jit(solution)/shard_map/ppermute | solution.py:275
  116.5 0.9 collective-permute-start.19
  117.3 0.7 collective-permute-start.18
  118.1 0.5 pad_bitcast_fusion.shares
  118.6 0.0 collective-permute-done.20
  118.6 2.9 %collective-permute-done.19 = f32[1,128]{1,0:T(1,128)S(1)} collective-permute-done((f32[1,128]{1,0:T(1,128)S(1)}, f32[1,128]{1,0:T(1,128)S(1)}, u32[]{:S(2)}, u32[]{:S(2)}) %collective-permute-start.19) | collective-permute-done | bytes 544 | tf_op jit(solution)/shard_map/ppermute | solution.py:275
  121.5 0.6 collective-permute-done.18
  122.1 0.6 add_add_fusion.rewards
  122.7 1.3 %shard_map.93 = f32[1,1]{1,0:T(1,128)} custom-call(f32[1,128]{1,0:T(1,128)} %add_add_fusion.rewards, f32[1,128]{1,0:T(1,128)} %pad_bitcast_fusion.shares), custom_call_target="tpu_custom_call" | custom-call | tf_op jit(solution)/shard_map/pallas_call | solution.py:276
  124.0 1.3 %copy.13 = bf16[1,32,2,16,1024]{4,3,2,1,0:T(8,128)(2,1)} copy(bf16[1,32,2,16,1024]{4,3,2,1,0:T(8,128)(2,1)S(1)} %bitcast.34) | data formatting | bytes 4194304
  (32 shorter events, 0.3 us)
Async XLA Ops:
  0.6 33.1 %collective-permute-start.3 = (bf16[256,2048]{1,0:T(8,128)(2,1)}, bf16[256,2048]{1,0:T(8,128)(2,1)S(1)}, u32[]{:S(2)}, u32[]{:S(2)}) collective-permute-start(bf16[256,2048]{1,0:T(8,128)(2,1)} %bitcast.28), channel_id=1, source_target_pairs={{0,64},{4,68},{8,72},{12,76},{16,80},{20,84},{24,88},{28,92},{32,9... | collective-permute-start | bytes 3145736 | tf_op jit(solution)/shard_map/ppermute | solution.py:180
  3.8 26.5 %collective-permute-start.1 = (bf16[256,2048]{1,0:T(8,128)(2,1)}, bf16[256,2048]{1,0:T(8,128)(2,1)S(1)}, u32[]{:S(2)}, u32[]{:S(2)}) collective-permute-start(bf16[256,2048]{1,0:T(8,128)(2,1)} %bitcast.29), channel_id=1, source_target_pairs={{0,3},{1,0},{2,1},{3,2},{4,7},{5,4},{6,5},{7,6},{8,11},{9,8},{10,9... | collective-permute-start | bytes 3145736 | tf_op jit(solution)/shard_map/ppermute | solution.py:179
  7.9 25.8 %collective-permute-start = (bf16[256,2048]{1,0:T(8,128)(2,1)}, bf16[256,2048]{1,0:T(8,128)(2,1)S(1)}, u32[]{:S(2)}, u32[]{:S(2)}) collective-permute-start(bf16[256,2048]{1,0:T(8,128)(2,1)} %bitcast.30), channel_id=1, source_target_pairs={{0,1},{1,2},{2,3},{3,0},{4,5},{5,6},{6,7},{7,4},{8,9},{9,10},{10,1... | collective-permute-start | bytes 3145736 | tf_op jit(solution)/shard_map/ppermute | solution.py:179
  8.6 4.7 %copy-start.4 = (s32[32]{0:T(128)S(1)}, s32[32]{0:T(128)}, u32[]{:S(2)}) copy-start(s32[32]{0:T(128)} %param.11) | copy-start | bytes 388
  8.6 7.4 %copy-start.5 = (s32[32,1]{0,1:T(1,128)S(1)}, s32[32,1]{0,1:T(1,128)}, u32[]{:S(2)}) copy-start(s32[32,1]{0,1:T(1,128)} %param.13) | copy-start | bytes 388
  16.3 2.2 %copy-start = (bf16[1024,8,2,128]{3,1,2,0:T(8,128)(2,1)S(1)}, bf16[1024,8,2,128]{3,1,2,0:T(8,128)(2,1)}, u32[]{:S(2)}) copy-start(bf16[1024,8,2,128]{3,1,2,0:T(8,128)(2,1)} %copy.11) | copy-start | bytes 12582916
  18.5 1.2 copy-start.2
  19.7 16.1 %copy-start.1 = (bf16[1024,8,2,128]{3,1,2,0:T(8,128)(2,1)S(1)}, bf16[1024,8,2,128]{3,1,2,0:T(8,128)(2,1)}, u32[]{:S(2)}) copy-start(bf16[1024,8,2,128]{3,1,2,0:T(8,128)(2,1)} %copy.11) | copy-start | bytes 12582916
  33.8 14.9 %collective-permute-start.5 = (bf16[128,2048]{1,0:T(8,128)(2,1)S(1)}, bf16[128,2048]{1,0:T(8,128)(2,1)S(1)}, u32[]{:S(2)}, u32[]{:S(2)}) collective-permute-start(bf16[128,2048]{1,0:T(8,128)(2,1)S(1)} %slice.35), channel_id=1, source_target_pairs={{0,3},{1,0},{2,1},{3,2},{4,7},{5,4},{6,5},{7,6},{8,11},{9,8},{10,9... | collective-permute-start | bytes 1572872 | tf_op jit(solution)/shard_map/ppermute | solution.py:240
  34.1 15.1 %collective-permute-start.4 = (bf16[128,2048]{1,0:T(8,128)(2,1)S(1)}, bf16[128,2048]{1,0:T(8,128)(2,1)S(1)}, u32[]{:S(2)}, u32[]{:S(2)}) collective-permute-start(bf16[128,2048]{1,0:T(8,128)(2,1)S(1)} %slice.34), channel_id=1, source_target_pairs={{0,1},{1,2},{2,3},{3,0},{4,5},{5,6},{6,7},{7,4},{8,9},{9,10},{10,1... | collective-permute-start | bytes 1572872 | tf_op jit(solution)/shard_map/ppermute | solution.py:240
  41.9 19.3 %collective-permute-start.2 = (bf16[160,2048]{1,0:T(8,128)(2,1)S(1)}, bf16[160,2048]{1,0:T(8,128)(2,1)S(1)}, u32[]{:S(2)}, u32[]{:S(2)}) collective-permute-start(bf16[160,2048]{1,0:T(8,128)(2,1)S(1)} %pad_maximum_fusion), channel_id=1, source_target_pairs={{0,64},{4,68},{8,72},{12,76},{16,80},{20,84},{24,88},{28,92},{32,9... | collective-permute-start | bytes 1966088 | tf_op jit(solution)/shard_map/ppermute | solution.py:241
  42.7 6.8 %copy-start.3 = (f32[1024]{0:T(1024)S(1)}, f32[1024]{0:T(1024)}, u32[]{:S(2)}) copy-start(f32[1024]{0:T(1024)} %param.10) | copy-start | bytes 12292
  42.7 24.1 %collective-permute-start.10 = (bf16[176,2048]{1,0:T(8,128)(2,1)S(1)}, bf16[176,2048]{1,0:T(8,128)(2,1)S(1)}, u32[]{:S(2)}, u32[]{:S(2)}) collective-permute-start(bf16[176,2048]{1,0:T(8,128)(2,1)S(1)} %get-tuple-element.36), channel_id=1, source_target_pairs={{0,3},{1,0},{2,1},{3,2},{4,7},{5,4},{6,5},{7,6},{8,11},{9,8},{10,9... | collective-permute-start | bytes 2162696 | tf_op jit(solution)/shard_map/ppermute | solution.py:245
  44.2 22.6 %collective-permute-start.9 = (bf16[176,2048]{1,0:T(8,128)(2,1)S(1)}, bf16[176,2048]{1,0:T(8,128)(2,1)S(1)}, u32[]{:S(2)}, u32[]{:S(2)}) collective-permute-start(bf16[176,2048]{1,0:T(8,128)(2,1)S(1)} %get-tuple-element.37), channel_id=1, source_target_pairs={{0,1},{1,2},{2,3},{3,0},{4,5},{5,6},{6,7},{7,4},{8,9},{9,10},{10,1... | collective-permute-start | bytes 2162696 | tf_op jit(solution)/shard_map/ppermute | solution.py:245
  49.3 23.5 %collective-permute-start.7 = (bf16[96,2048]{1,0:T(8,128)(2,1)S(1)}, bf16[96,2048]{1,0:T(8,128)(2,1)S(1)}, u32[]{:S(2)}, u32[]{:S(2)}) collective-permute-start(bf16[96,2048]{1,0:T(8,128)(2,1)S(1)} %pad_maximum_fusion.1), channel_id=1, source_target_pairs={{0,64},{4,68},{8,72},{12,76},{16,80},{20,84},{24,88},{28,92},{32,9... | collective-permute-start | bytes 1179656 | tf_op jit(solution)/shard_map/ppermute | solution.py:247
  61.2 11.6 %collective-permute-start.8 = (bf16[80,2048]{1,0:T(8,128)(2,1)S(1)}, bf16[80,2048]{1,0:T(8,128)(2,1)S(1)}, u32[]{:S(2)}, u32[]{:S(2)}) collective-permute-start(bf16[80,2048]{1,0:T(8,128)(2,1)S(1)} %get-tuple-element.38.refs_4_), channel_id=1, source_target_pairs={{0,3},{1,0},{2,1},{3,2},{4,7},{5,4},{6,5},{7,6},{8,11},{9,8},{10,9... | collective-permute-start | bytes 983048 | tf_op jit(solution)/shard_map/ppermute | solution.py:251
  62.8 10.1 %collective-permute-start.6 = (bf16[80,2048]{1,0:T(8,128)(2,1)S(1)}, bf16[80,2048]{1,0:T(8,128)(2,1)S(1)}, u32[]{:S(2)}, u32[]{:S(2)}) collective-permute-start(bf16[80,2048]{1,0:T(8,128)(2,1)S(1)} %get-tuple-element.39.refs_1_), channel_id=1, source_target_pairs={{0,1},{1,2},{2,3},{3,0},{4,5},{5,6},{6,7},{7,4},{8,9},{9,10},{10,1... | collective-permute-start | bytes 983048 | tf_op jit(solution)/shard_map/ppermute | solution.py:251
  81.1 13.5 %copy-start.6 = (s32[32]{0:T(128)S(1)}, s32[32]{0:T(128)}, u32[]{:S(2)}) copy-start(s32[32]{0:T(128)} %param.12) | copy-start | bytes 388
  81.1 42.9 %all-to-all-start = ((bf16[32,2,16,1024]{3,2,1,0:T(8,128)(2,1)}), bf16[32,2,16,1024]{3,2,1,0:T(8,128)(2,1)S(1)}, u32[]{:S(2)}, u32[]{:S(2)}) async-start(bf16[32,2,16,1024]{3,2,1,0:T(8,128)(2,1)} %shard_map.92), calls=%async_computation | async-start | bytes 4194304 | tf_op jit(solution)/shard_map/all_to_all | solution.py:268
  86.6 4.1 %collective-permute-start.13 = (f32[1,128]{1,0:T(1,128)S(1)}, f32[1,128]{1,0:T(1,128)S(1)}, u32[]{:S(2)}, u32[]{:S(2)}) collective-permute-start(f32[1,128]{1,0:T(1,128)S(1)} %get-tuple-element.35), channel_id=1, source_target_pairs={{0,3},{1,0},{2,1},{3,2},{4,7},{5,4},{6,5},{7,6},{8,11},{9,8},{10,9... | collective-permute-start | bytes 1544 | tf_op jit(solution)/shard_map/ppermute | solution.py:270
  89.4 5.0 %collective-permute-start.12 = (f32[1,128]{1,0:T(1,128)S(1)}, f32[1,128]{1,0:T(1,128)S(1)}, u32[]{:S(2)}, u32[]{:S(2)}) collective-permute-start(f32[1,128]{1,0:T(1,128)S(1)} %get-tuple-element.35), channel_id=1, source_target_pairs={{0,2},{1,3},{2,0},{3,1},{4,6},{5,7},{6,4},{7,5},{8,10},{9,11},{10,... | collective-permute-start | bytes 1544 | tf_op jit(solution)/shard_map/ppermute | solution.py:270
  89.4 5.0 %collective-permute-start.11 = (f32[1,128]{1,0:T(1,128)S(1)}, f32[1,128]{1,0:T(1,128)S(1)}, u32[]{:S(2)}, u32[]{:S(2)}) collective-permute-start(f32[1,128]{1,0:T(1,128)S(1)} %get-tuple-element.35), channel_id=1, source_target_pairs={{0,1},{1,2},{2,3},{3,0},{4,5},{5,6},{6,7},{7,4},{8,9},{9,10},{10,1... | collective-permute-start | bytes 1544 | tf_op jit(solution)/shard_map/ppermute | solution.py:270
  94.5 1.2 collective-permute-start.14
  95.7 14.2 %collective-permute-start.17 = (f32[1,128]{1,0:T(1,128)S(1)}, f32[1,128]{1,0:T(1,128)S(1)}, u32[]{:S(2)}, u32[]{:S(2)}) collective-permute-start(f32[1,128]{1,0:T(1,128)S(1)} %add.124), channel_id=1, source_target_pairs={{0,24},{4,28},{8,0},{12,4},{16,8},{20,12},{24,16},{28,20},{32,56},... | collective-permute-start | bytes 1544 | tf_op jit(solution)/shard_map/ppermute | solution.py:275
  98.7 11.2 %collective-permute-start.16 = (f32[1,128]{1,0:T(1,128)S(1)}, f32[1,128]{1,0:T(1,128)S(1)}, u32[]{:S(2)}, u32[]{:S(2)}) collective-permute-start(f32[1,128]{1,0:T(1,128)S(1)} %add.124), channel_id=1, source_target_pairs={{0,16},{4,20},{8,24},{12,28},{16,0},{20,4},{24,8},{28,12},{32,48},... | collective-permute-start | bytes 1544 | tf_op jit(solution)/shard_map/ppermute | solution.py:275
  99.5 10.3 %collective-permute-start.15 = (f32[1,128]{1,0:T(1,128)S(1)}, f32[1,128]{1,0:T(1,128)S(1)}, u32[]{:S(2)}, u32[]{:S(2)}) collective-permute-start(f32[1,128]{1,0:T(1,128)S(1)} %add.124), channel_id=1, source_target_pairs={{0,8},{4,12},{8,16},{12,20},{16,24},{20,28},{24,0},{28,4},{32,40},... | collective-permute-start | bytes 1544 | tf_op jit(solution)/shard_map/ppermute | solution.py:275
  109.9 8.7 %collective-permute-start.20 = (f32[1,128]{1,0:T(1,128)S(1)}, f32[1,128]{1,0:T(1,128)S(1)}, u32[]{:S(2)}, u32[]{:S(2)}) collective-permute-start(f32[1,128]{1,0:T(1,128)S(1)} %add_add_fusion.1), channel_id=1, source_target_pairs={{0,96},{4,100},{8,104},{12,108},{16,112},{20,116},{24,120},{28,124... | collective-permute-start | bytes 1544 | tf_op jit(solution)/shard_map/ppermute | solution.py:275
  116.5 5.0 %collective-permute-start.19 = (f32[1,128]{1,0:T(1,128)S(1)}, f32[1,128]{1,0:T(1,128)S(1)}, u32[]{:S(2)}, u32[]{:S(2)}) collective-permute-start(f32[1,128]{1,0:T(1,128)S(1)} %add_add_fusion.1), channel_id=1, source_target_pairs={{0,64},{4,68},{8,72},{12,76},{16,80},{20,84},{24,88},{28,92},{32,9... | collective-permute-start | bytes 1544 | tf_op jit(solution)/shard_map/ppermute | solution.py:275
  117.3 4.8 %collective-permute-start.18 = (f32[1,128]{1,0:T(1,128)S(1)}, f32[1,128]{1,0:T(1,128)S(1)}, u32[]{:S(2)}, u32[]{:S(2)}) collective-permute-start(f32[1,128]{1,0:T(1,128)S(1)} %add_add_fusion.1), channel_id=1, source_target_pairs={{0,32},{4,36},{8,40},{12,44},{16,48},{20,52},{24,56},{28,60},{32,6... | collective-permute-start | bytes 1544 | tf_op jit(solution)/shard_map/ppermute | solution.py:275

commit v3 on v2

--- a/solution.py
+++ b/solution.py
@@ -16,7 +16,7 @@
 MIDDLE_TILE = 2048
 LAST_TILE = 1024
 END = 80
-PASSED = 80
+PASSED = 64
 PLANE = ("section", "dp")
 VMEM_LIMIT = 32 * 1024 * 1024
 
@@ -177,7 +177,8 @@
 
     mine = hidden[0]
     below, above = up(mine), down(mine)
-    theirs = across(mine)
+    mine_across, keyval_weight = lax.optimization_barrier((mine, keyval_weight))
+    theirs = across(mine_across)
 
     below_idx, above_idx, far_idx = (mp_idx + mp_size - 1) % mp_size, (mp_idx + 1) % mp_size, (mp_idx + 2) % mp_size
     head = reward_head.reshape(1, features)
@@ -239,7 +240,6 @@
     below, above, own_start = ahead(below, above, own_start)
     far_low, far_high = up(below[:half]), down(above[half:])
     crossed = across(jnp.concatenate([below[:END], above[seq - END:]], axis=0))
-    theirs, below, above = ahead(theirs, below, above)
     own_partial = middle([below, above], own_start)
     theirs, own_partial = ahead(theirs, own_partial)
     their_below_high, their_above_low = up(theirs[END:]), down(theirs[:seq - END])
@@ -265,14 +265,20 @@
         compiler_params=pltpu.CompilerParams(vmem_limit_bytes=VMEM_LIMIT),
         cost_estimate=pl.CostEstimate(flops=0, bytes_accessed=6 * seq * features, transcendentals=0),
     )(source, own_states, their_states)
-    received = lax.all_to_all(outgoing, PLANE, split_axis=0, concat_axis=0, tiled=True)
-
-    rewards += sum(lax.ppermute(rewards, "mp", ring(mp_size, step)) for step in range(1, mp_size))
     cores = 2
     across_size = sections * 2
     along = sections * dp_size // (cores * across_size)
-    for span, size in ((1, cores), (cores, along), (cores * along, across_size)):
-        rewards += sum(lax.ppermute(rewards, PLANE, turn(sections * dp_size, span, size, step)) for step in range(1, size))
+
+    def summed(terms, span, size):
+        pairs = [turn(sections * dp_size, span, size, step) for step in range(1, size)]
+        return terms + sum(lax.ppermute(terms, PLANE, pair) for pair in pairs)
+
+    rewards = summed(rewards, cores, along)
+    outgoing, rewards = ahead(outgoing, rewards)
+    received = lax.all_to_all(outgoing, PLANE, split_axis=0, concat_axis=0, tiled=True)
+    rewards += sum(lax.ppermute(rewards, "mp", ring(mp_size, step)) for step in range(1, mp_size))
+    rewards = summed(rewards, 1, cores)
+    rewards = summed(rewards, cores * along, across_size)
     advantage = pl.pallas_call(
         advantage_kernel, out_shape=jax.ShapeDtypeStruct((1, 1), jnp.float32)
     )(rewards, shares)

time: 126 us -> 120 us (0.952)
  waiting for transfers between devices: 37.4 us -> 29.1 us
  starting transfers between devices: 36.4 us -> 39.9 us
    ppermute x1, waiting for transfers between devices: 5.79 us -> 0.01 us  [body(): crossed = across(jnp.concatenate([below[:END], above[seq - END:]], axis=0))]
    ppermute x1, starting transfers between devices: 0.09 us -> 5 us  [body(): across(jnp.concatenate([far_low[PASSED:], far_high[:half - PASSED]], axis...]
    ppermute x2, waiting for transfers between devices: 4.49 us -> 0.56 us  [body(): far_low, far_high = (up(below[:half]), down(above[half:]))]
    ppermute x8, starting transfers between devices: 16.2 us -> 12.4 us  [the longest x7 9.33 us: summed(): return terms + sum((lax.ppermute(terms, PLANE, pair) for pair in pairs))]
    ppermute x1, starting transfers between devices: 0.59 us -> 3.1 us  [body(): crossed = across(jnp.concatenate([below[:END], above[seq - END:]], axis=0))]
    ppermute x8, waiting for transfers between devices: 12.7 us -> 14.8 us  [the longest x7 14.8 us: summed(): return terms + sum((lax.ppermute(terms, PLANE, pair) for pair in pairs))]
    unnamed x16 -> x14, local copies, waits for them, and re-layouts: 9.48 us -> 8.25 us
  transfers between devices with their start and end apart: 22 -> 22, of which waited for: 11 -> 11; matrix products, arithmetic and copies ran while one was open for 9% -> 9% of each run, Pallas kernels for 21% -> 24%
where the time goes in v3:
time: 120 us; the launch traced here: 119 us
  starting transfers between devices  39.9 us (33%)
  Pallas kernels  34.9 us (29%)
  waiting for transfers between devices  29.1 us (24%)
  local copies, waits for them, and re-layouts  11.1 us (9%)
  other arithmetic  3.18 us (3%)
    pallas_call x6, Pallas kernels, call(): pl.pallas_call(functools.partial(kernel, depth_steps), grid_spec=pltpu.Pr...  31.4 us
    ppermute x7, waiting for transfers between devices, summed(): return terms + sum((lax.ppermute(terms, PLANE, pair) for pair in pairs))  14.8 us
    ppermute x7, starting transfers between devices, summed(): return terms + sum((lax.ppermute(terms, PLANE, pair) for pair in pairs))  9.33 us
    ppermute x2, waiting for transfers between devices, body(): below, above = (up(mine), down(mine))  9.08 us
    unnamed x14, local copies, waits for them, and re-layouts  8.25 us
    all_to_all x1, starting transfers between devices, body(): lax.all_to_all(outgoing, PLANE, split_axis=0, concat_axis=0, tiled=True)  5.82 us
    ppermute x1, starting transfers between devices, body(): across(jnp.concatenate([far_low[PASSED:], far_high[:half - PASSED]], axis...  5 us
    ppermute x2, starting transfers between devices, body(): below, above = (up(mine), down(mine))  4.19 us
  transfers between devices with their start and end apart: 22, of which 11 were waited for; matrix products, arithmetic and copies ran while one was open for 9% of the time, Pallas kernels for 24%

profile of v3, /device:TPU:0, one launch (start us, length us, event | category | flops | bytes accessed | tf_op | source)
XLA Modules:
  0.0 119.1 jit_solution(11761684336739698154)
XLA Ops:
  0.6 4.2 %collective-permute-start.1 = (bf16[256,2048]{1,0:T(8,128)(2,1)}, bf16[256,2048]{1,0:T(8,128)(2,1)S(1)}, u32[]{:S(2)}, u32[]{:S(2)}) collective-permute-start(bf16[256,2048]{1,0:T(8,128)(2,1)} %bitcast.1.refs_0_), channel_id=1, source_target_pairs={{0,3},{1,0},{2,1},{3,2},{4,7},{5,4},{6,5},{7,6},{8,11},{9,8},{10,9... | collective-permute-start | bytes 3145736 | tf_op jit(solution)/shard_map/ppermute | solution.py:179
  4.8 0.0 collective-permute-start
  4.8 4.7 %copy.11 = bf16[1024,8,2,128]{3,1,2,0:T(8,128)(2,1)} copy(bf16[1024,8,2,128]{3,2,1,0:T(2,128)(2,1)} %bitcast.31) | data formatting | bytes 8388608
  9.5 3.0 %collective-permute-start.3 = (bf16[256,2048]{1,0:T(8,128)(2,1)}, bf16[256,2048]{1,0:T(8,128)(2,1)S(1)}, u32[]{:S(2)}, u32[]{:S(2)}) collective-permute-start(bf16[256,2048]{1,0:T(8,128)(2,1)} %bitcast.1.refs_0_), channel_id=1, source_target_pairs={{0,64},{4,68},{8,72},{12,76},{16,80},{20,84},{24,88},{28,92},{32,9... | collective-permute-start | bytes 3145736 | tf_op jit(solution)/shard_map/ppermute | solution.py:181
  12.6 0.6 fusion.8
  13.2 0.7 fusion.7
  13.9 0.1 pad_add_fusion.1.refs_0_
  14.0 0.7 pad_add_fusion.2.places
  14.7 0.2 convert_reduce_fusion
  14.8 0.7 pad_add_fusion.places
  15.6 0.1 select_reduce_fusion
  15.7 2.2 %copy-done = bf16[1024,8,2,128]{3,1,2,0:T(8,128)(2,1)S(1)} copy-done((bf16[1024,8,2,128]{3,1,2,0:T(8,128)(2,1)S(1)}, bf16[1024,8,2,128]{3,1,2,0:T(8,128)(2,1)}, u32[]{:S(2)}) %copy-start) | copy-done | bytes 4194328
  17.9 3.9 %shard_map.86.refs_3_ = f32[256,1280]{1,0:T(8,128)S(1)} custom-call(s32[1]{0:T(128)} %bitcast.2.places, bf16[256,2048]{1,0:T(8,128)(2,1)} %bitcast.1.refs_0_, bf16[1,8192,1024]{2,1,0:T(8,128)(2,1)} %refs_4_.3, bf16[8192,256]{1,0:T(8,128)(2,1)S(1)} %bitcast.22), custom_call_target="tpu_custom_call" | custom-call | flops 1342177280 | bytes 5242880 | tf_op jit(solution)/shard_map/pallas_call | solution.py:196
  21.8 5.8 %collective-permute-done.1.refs_2_ = bf16[256,2048]{1,0:T(8,128)(2,1)S(1)} collective-permute-done((bf16[256,2048]{1,0:T(8,128)(2,1)}, bf16[256,2048]{1,0:T(8,128)(2,1)S(1)}, u32[]{:S(2)}, u32[]{:S(2)}) %collective-permute-start.1) | collective-permute-done | bytes 1048608 | tf_op jit(solution)/shard_map/ppermute | solution.py:179
  27.6 3.3 %collective-permute-done.refs_1_ = bf16[256,2048]{1,0:T(8,128)(2,1)S(1)} collective-permute-done((bf16[256,2048]{1,0:T(8,128)(2,1)}, bf16[256,2048]{1,0:T(8,128)(2,1)S(1)}, u32[]{:S(2)}, u32[]{:S(2)}) %collective-permute-start) | collective-permute-done | bytes 1048608 | tf_op jit(solution)/shard_map/ppermute | solution.py:179
  31.0 0.4 collective-permute-start.5
  31.4 1.7 %collective-permute-start.4 = (bf16[128,2048]{1,0:T(8,128)(2,1)S(1)}, bf16[128,2048]{1,0:T(8,128)(2,1)S(1)}, u32[]{:S(2)}, u32[]{:S(2)}) collective-permute-start(bf16[128,2048]{1,0:T(8,128)(2,1)S(1)} %slice.38), channel_id=1, source_target_pairs={{0,1},{1,2},{2,3},{3,0},{4,5},{5,6},{6,7},{7,4},{8,9},{9,10},{10,1... | collective-permute-start | bytes 1572872 | tf_op jit(solution)/shard_map/ppermute | solution.py:241
  33.1 6.0 %shard_map.87.refs_2_ = f32[256,1280]{1,0:T(8,128)S(1)} custom-call(s32[2]{0:T(128)S(1)} %pad_add_fusion.1.refs_0_, bf16[256,2048]{1,0:T(8,128)(2,1)S(1)} %collective-permute-done.refs_1_, bf16[256,2048]{1,0:T(8,128)(2,1)S(1)} %collective-permute-done.1.refs_2_, f32[256,1280]{1,0:T(8,128)S(1)} %shard_map.86.refs_3_, bf16[1,8192,1024]{2,1,0:T(8,128)(2,1)} %refs_4_.3, ...), custom_call_target="tpu_custom_call" | custom-call | flops 2684354560 | bytes 10485760 | tf_op jit(solution)/shard_map/pallas_call | solution.py:196
  39.1 0.1 pad_maximum_fusion
  39.2 3.1 %collective-permute-start.2 = (bf16[160,2048]{1,0:T(8,128)(2,1)S(1)}, bf16[160,2048]{1,0:T(8,128)(2,1)S(1)}, u32[]{:S(2)}, u32[]{:S(2)}) collective-permute-start(bf16[160,2048]{1,0:T(8,128)(2,1)S(1)} %pad_maximum_fusion), channel_id=1, source_target_pairs={{0,64},{4,68},{8,72},{12,76},{16,80},{20,84},{24,88},{28,92},{32,9... | collective-permute-start | bytes 1966088 | tf_op jit(solution)/shard_map/ppermute | solution.py:242
  42.3 0.1 fusion.4
  42.4 1.6 %collective-permute-start.10 = (bf16[176,2048]{1,0:T(8,128)(2,1)S(1)}, bf16[176,2048]{1,0:T(8,128)(2,1)S(1)}, u32[]{:S(2)}, u32[]{:S(2)}) collective-permute-start(bf16[176,2048]{1,0:T(8,128)(2,1)S(1)} %get-tuple-element.38), channel_id=1, source_target_pairs={{0,3},{1,0},{2,1},{3,2},{4,7},{5,4},{6,5},{7,6},{8,11},{9,8},{10,9... | collective-permute-start | bytes 2162696 | tf_op jit(solution)/shard_map/ppermute | solution.py:245
  44.0 0.5 collective-permute-start.9
  44.5 0.6 collective-permute-done.4.refs_0_
  45.2 0.0 copy-start.2
  45.2 5.0 %collective-permute-start.7 = (bf16[128,2048]{1,0:T(8,128)(2,1)S(1)}, bf16[128,2048]{1,0:T(8,128)(2,1)S(1)}, u32[]{:S(2)}, u32[]{:S(2)}) collective-permute-start(bf16[128,2048]{1,0:T(8,128)(2,1)S(1)} %pad_maximum_fusion.1), channel_id=1, source_target_pairs={{0,64},{4,68},{8,72},{12,76},{16,80},{20,84},{24,88},{28,92},{32,9... | collective-permute-start | bytes 1572872 | tf_op jit(solution)/shard_map/ppermute | solution.py:247
  50.2 3.5 %shard_map.89.refs_5_ = f32[256,1280]{1,0:T(8,128)S(1)} custom-call(s32[1]{0:T(128)} %bitcast.2.places, bf16[256,2048]{1,0:T(8,128)(2,1)S(1)} %collective-permute-done.3.refs_0_, bf16[1,8192,1024]{2,1,0:T(8,128)(2,1)} %refs_4_.3, bf16[8192,256]{1,0:T(8,128)(2,1)S(1)} %bitcast.24), custom_call_target="tpu_custom_call" | custom-call | flops 1342177280 | bytes 5242880 | tf_op jit(solution)/shard_map/pallas_call | solution.py:196
  53.7 6.0 %shard_map.88 = (bf16[256,1024]{1,0:T(8,128)(2,1)S(1)}, f32[1,128]{1,0:T(1,128)S(1)}) custom-call(s32[3]{0:T(128)S(1)} %pad_add_fusion.places, bf16[128,2048]{1,0:T(8,128)(2,1)S(1)} %collective-permute-done.4.refs_0_, bf16[128,2048]{1,0:T(8,128)(2,1)S(1)} %collective-permute-done.5.refs_1_, f32[256,1280]{1,0:T(8,128)S(1)} %shard_map.87.refs_2_, ...), custom_call_target="tpu_custom_call" | custom-call | flops 1342177280 | bytes 5242880 | tf_op jit(solution)/shard_map/pallas_call | solution.py:196
  59.7 0.0 collective-permute-done.2
  59.8 0.3 collective-permute-start.8
  60.2 1.7 %collective-permute-start.6 = (bf16[64,2048]{1,0:T(8,128)(2,1)S(1)}, bf16[64,2048]{1,0:T(8,128)(2,1)S(1)}, u32[]{:S(2)}, u32[]{:S(2)}) collective-permute-start(bf16[64,2048]{1,0:T(8,128)(2,1)S(1)} %get-tuple-element.43), channel_id=1, source_target_pairs={{0,1},{1,2},{2,3},{3,0},{4,5},{5,6},{6,7},{7,4},{8,9},{9,10},{10,1... | collective-permute-start | bytes 786440 | tf_op jit(solution)/shard_map/ppermute | solution.py:251
  61.9 0.1 fusion.5
  62.0 0.6 collective-permute-done.9.refs_2_
  62.6 6.0 %shard_map.90.refs_3_ = f32[256,1280]{1,0:T(8,128)S(1)} custom-call(s32[2]{0:T(128)S(1)} %pad_add_fusion.1.refs_0_, bf16[80,2048]{1,0:T(8,128)(2,1)S(1)} %get-tuple-element.41.refs_1_, bf16[176,2048]{1,0:T(8,128)(2,1)S(1)} %collective-permute-done.9.refs_2_, bf16[176,2048]{1,0:T(8,128)(2,1)S(1)} %collective-permute-done.10.refs_3_, ...), custom_call_target="tpu_custom_call" | custom-call | flops 2684354560 | bytes 10485760 | tf_op jit(solution)/shard_map/pallas_call | solution.py:196
  68.5 0.0 collective-permute-done.8.refs_2_
  68.6 0.0 collective-permute-done.6.refs_0_
  68.6 6.0 %shard_map.91 = (bf16[256,1024]{1,0:T(8,128)(2,1)S(1)}, f32[1,128]{1,0:T(1,128)S(1)}) custom-call(s32[3]{0:T(128)S(1)} %pad_add_fusion.2.places, bf16[64,2048]{1,0:T(8,128)(2,1)S(1)} %collective-permute-done.6.refs_0_, bf16[128,2048]{1,0:T(8,128)(2,1)S(1)} %collective-permute-done.7.refs_1_, bf16[64,2048]{1,0:T(8,128)(2,1)S(1)} %collective-permute-done.8.refs_2_, ...), custom_call_target="tpu_custom_call" | custom-call | flops 1342177280 | bytes 5242880 | tf_op jit(solution)/shard_map/pallas_call | solution.py:196
  74.6 3.0 %collective-permute-start.13 = (f32[1,128]{1,0:T(1,128)S(1)}, f32[1,128]{1,0:T(1,128)S(1)}, u32[]{:S(2)}, u32[]{:S(2)}) collective-permute-start(f32[1,128]{1,0:T(1,128)S(1)} %get-tuple-element.35), channel_id=1, source_target_pairs={{0,24},{4,28},{8,0},{12,4},{16,8},{20,12},{24,16},{28,20},{32,56},... | collective-permute-start | bytes 1544 | tf_op jit(solution)/shard_map/ppermute | solution.py:274
  77.6 0.6 collective-permute-start.12
  78.2 1.0 collective-permute-start.11
  79.2 2.2 %shard_map.92 = bf16[32,2,16,1024]{3,2,1,0:T(8,128)(2,1)} custom-call(s32[64]{0:T(128)S(1)} %broadcast_add_fusion.slots, bf16[256,1024]{1,0:T(8,128)(2,1)S(1)} %get-tuple-element.30.first, bf16[256,1024]{1,0:T(8,128)(2,1)S(1)} %get-tuple-element.34.second), custom_call_target="tpu_custom_call" | custom-call | bytes 1572864 | tf_op jit(solution)/shard_map/pallas_call | solution.py:256
  81.4 0.0 collective-permute-done.13
  81.4 1.2 %collective-permute-done.12 = f32[1,128]{1,0:T(1,128)S(1)} collective-permute-done((f32[1,128]{1,0:T(1,128)S(1)}, f32[1,128]{1,0:T(1,128)S(1)}, u32[]{:S(2)}, u32[]{:S(2)}) %collective-permute-start.12) | collective-permute-done | bytes 544 | tf_op jit(solution)/shard_map/ppermute | solution.py:274
  82.6 0.3 collective-permute-done.11
  83.0 5.8 %all-to-all-start = ((bf16[32,2,16,1024]{3,2,1,0:T(8,128)(2,1)}), bf16[32,2,16,1024]{3,2,1,0:T(8,128)(2,1)S(1)}, u32[]{:S(2)}, u32[]{:S(2)}) async-start(bf16[32,2,16,1024]{3,2,1,0:T(8,128)(2,1)} %shard_map.92), calls=%async_computation | async-start | bytes 4194304 | tf_op jit(solution)/shard_map/all_to_all | solution.py:278
  88.8 1.0 collective-permute-start.16
  89.8 2.1 %collective-permute-start.15 = (f32[1,128]{1,0:T(1,128)S(1)}, f32[1,128]{1,0:T(1,128)S(1)}, u32[]{:S(2)}, u32[]{:S(2)}) collective-permute-start(f32[1,128]{1,0:T(1,128)S(1)} %add_add_fusion.2), channel_id=1, source_target_pairs={{0,2},{1,3},{2,0},{3,1},{4,6},{5,7},{6,4},{7,5},{8,10},{9,11},{10,... | collective-permute-start | bytes 1544 | tf_op jit(solution)/shard_map/ppermute | solution.py:279
  91.9 0.0 collective-permute-start.14
  91.9 0.7 dynamic_slice.19
  92.6 0.0 collective-permute-done.16
  92.6 2.2 %collective-permute-done.15 = f32[1,128]{1,0:T(1,128)S(1)} collective-permute-done((f32[1,128]{1,0:T(1,128)S(1)}, f32[1,128]{1,0:T(1,128)S(1)}, u32[]{:S(2)}, u32[]{:S(2)}) %collective-permute-start.15) | collective-permute-done | bytes 544 | tf_op jit(solution)/shard_map/ppermute | solution.py:279
  94.9 1.8 %collective-permute-done.14 = f32[1,128]{1,0:T(1,128)S(1)} collective-permute-done((f32[1,128]{1,0:T(1,128)S(1)}, f32[1,128]{1,0:T(1,128)S(1)}, u32[]{:S(2)}, u32[]{:S(2)}) %collective-permute-start.14) | collective-permute-done | bytes 544 | tf_op jit(solution)/shard_map/ppermute | solution.py:279
  96.7 0.7 fusion.1
  97.4 0.4 collective-permute-done.17
  97.8 3.0 %collective-permute-start.20 = (f32[1,128]{1,0:T(1,128)S(1)}, f32[1,128]{1,0:T(1,128)S(1)}, u32[]{:S(2)}, u32[]{:S(2)}) collective-permute-start(f32[1,128]{1,0:T(1,128)S(1)} %add.127), channel_id=1, source_target_pairs={{0,96},{4,100},{8,104},{12,108},{16,112},{20,116},{24,120},{28,124... | collective-permute-start | bytes 1544 | tf_op jit(solution)/shard_map/ppermute | solution.py:274
  100.9 0.8 collective-permute-start.19
  101.7 0.9 collective-permute-start.18
  102.5 0.5 pad_bitcast_fusion.shares
  103.1 11.4 %collective-permute-done.20 = f32[1,128]{1,0:T(1,128)S(1)} collective-permute-done((f32[1,128]{1,0:T(1,128)S(1)}, f32[1,128]{1,0:T(1,128)S(1)}, u32[]{:S(2)}, u32[]{:S(2)}) %collective-permute-start.20) | collective-permute-done | bytes 544 | tf_op jit(solution)/shard_map/ppermute | solution.py:274
  114.4 1.4 %collective-permute-done.19 = f32[1,128]{1,0:T(1,128)S(1)} collective-permute-done((f32[1,128]{1,0:T(1,128)S(1)}, f32[1,128]{1,0:T(1,128)S(1)}, u32[]{:S(2)}, u32[]{:S(2)}) %collective-permute-start.19) | collective-permute-done | bytes 544 | tf_op jit(solution)/shard_map/ppermute | solution.py:274
  115.9 0.6 add_add_fusion.rewards
  116.5 1.3 %shard_map.93 = f32[1,1]{1,0:T(1,128)} custom-call(f32[1,128]{1,0:T(1,128)} %add_add_fusion.rewards, f32[1,128]{1,0:T(1,128)} %pad_bitcast_fusion.shares), custom_call_target="tpu_custom_call" | custom-call | tf_op jit(solution)/shard_map/pallas_call | solution.py:282
  117.7 0.0 all-to-all-done
  117.7 1.3 %copy.13 = bf16[1,32,2,16,1024]{4,3,2,1,0:T(8,128)(2,1)} copy(bf16[1,32,2,16,1024]{4,3,2,1,0:T(8,128)(2,1)S(1)} %bitcast.30) | data formatting | bytes 4194304
  (31 shorter events, 0.3 us)
Async XLA Ops:
  0.6 26.9 %collective-permute-start.1 = (bf16[256,2048]{1,0:T(8,128)(2,1)}, bf16[256,2048]{1,0:T(8,128)(2,1)S(1)}, u32[]{:S(2)}, u32[]{:S(2)}) collective-permute-start(bf16[256,2048]{1,0:T(8,128)(2,1)} %bitcast.1.refs_0_), channel_id=1, source_target_pairs={{0,3},{1,0},{2,1},{3,2},{4,7},{5,4},{6,5},{7,6},{8,11},{9,8},{10,9... | collective-permute-start | bytes 3145736 | tf_op jit(solution)/shard_map/ppermute | solution.py:179
  4.8 26.0 %collective-permute-start = (bf16[256,2048]{1,0:T(8,128)(2,1)}, bf16[256,2048]{1,0:T(8,128)(2,1)S(1)}, u32[]{:S(2)}, u32[]{:S(2)}) collective-permute-start(bf16[256,2048]{1,0:T(8,128)(2,1)} %bitcast.1.refs_0_), channel_id=1, source_target_pairs={{0,1},{1,2},{2,3},{3,0},{4,5},{5,6},{6,7},{7,4},{8,9},{9,10},{10,1... | collective-permute-start | bytes 3145736 | tf_op jit(solution)/shard_map/ppermute | solution.py:179
  4.8 7.8 %copy-start.3 = (s32[32]{0:T(128)S(1)}, s32[32]{0:T(128)}, u32[]{:S(2)}) copy-start(s32[32]{0:T(128)} %param.11) | copy-start | bytes 388
  4.8 9.8 %copy-start.4 = (s32[32,1]{0,1:T(1,128)S(1)}, s32[32,1]{0,1:T(1,128)}, u32[]{:S(2)}) copy-start(s32[32,1]{0,1:T(1,128)} %param.13) | copy-start | bytes 388
  9.5 29.6 %collective-permute-start.3 = (bf16[256,2048]{1,0:T(8,128)(2,1)}, bf16[256,2048]{1,0:T(8,128)(2,1)S(1)}, u32[]{:S(2)}, u32[]{:S(2)}) collective-permute-start(bf16[256,2048]{1,0:T(8,128)(2,1)} %bitcast.1.refs_0_), channel_id=1, source_target_pairs={{0,64},{4,68},{8,72},{12,76},{16,80},{20,84},{24,88},{28,92},{32,9... | collective-permute-start | bytes 3145736 | tf_op jit(solution)/shard_map/ppermute | solution.py:181
  15.7 2.2 %copy-start = (bf16[1024,8,2,128]{3,1,2,0:T(8,128)(2,1)S(1)}, bf16[1024,8,2,128]{3,1,2,0:T(8,128)(2,1)}, u32[]{:S(2)}) copy-start(bf16[1024,8,2,128]{3,1,2,0:T(8,128)(2,1)} %copy.11) | copy-start | bytes 12582916
  17.9 15.3 %copy-start.1 = (bf16[1024,8,2,128]{3,1,2,0:T(8,128)(2,1)S(1)}, bf16[1024,8,2,128]{3,1,2,0:T(8,128)(2,1)}, u32[]{:S(2)}) copy-start(bf16[1024,8,2,128]{3,1,2,0:T(8,128)(2,1)} %copy.11) | copy-start | bytes 12582916
  31.0 13.5 %collective-permute-start.5 = (bf16[128,2048]{1,0:T(8,128)(2,1)S(1)}, bf16[128,2048]{1,0:T(8,128)(2,1)S(1)}, u32[]{:S(2)}, u32[]{:S(2)}) collective-permute-start(bf16[128,2048]{1,0:T(8,128)(2,1)S(1)} %slice.39), channel_id=1, source_target_pairs={{0,3},{1,0},{2,1},{3,2},{4,7},{5,4},{6,5},{7,6},{8,11},{9,8},{10,9... | collective-permute-start | bytes 1572872 | tf_op jit(solution)/shard_map/ppermute | solution.py:241
  31.4 13.7 %collective-permute-start.4 = (bf16[128,2048]{1,0:T(8,128)(2,1)S(1)}, bf16[128,2048]{1,0:T(8,128)(2,1)S(1)}, u32[]{:S(2)}, u32[]{:S(2)}) collective-permute-start(bf16[128,2048]{1,0:T(8,128)(2,1)S(1)} %slice.38), channel_id=1, source_target_pairs={{0,1},{1,2},{2,3},{3,0},{4,5},{5,6},{6,7},{7,4},{8,9},{9,10},{10,1... | collective-permute-start | bytes 1572872 | tf_op jit(solution)/shard_map/ppermute | solution.py:241
  39.2 20.6 %collective-permute-start.2 = (bf16[160,2048]{1,0:T(8,128)(2,1)S(1)}, bf16[160,2048]{1,0:T(8,128)(2,1)S(1)}, u32[]{:S(2)}, u32[]{:S(2)}) collective-permute-start(bf16[160,2048]{1,0:T(8,128)(2,1)S(1)} %pad_maximum_fusion), channel_id=1, source_target_pairs={{0,64},{4,68},{8,72},{12,76},{16,80},{20,84},{24,88},{28,92},{32,9... | collective-permute-start | bytes 1966088 | tf_op jit(solution)/shard_map/ppermute | solution.py:242
  42.4 19.5 %collective-permute-start.10 = (bf16[176,2048]{1,0:T(8,128)(2,1)S(1)}, bf16[176,2048]{1,0:T(8,128)(2,1)S(1)}, u32[]{:S(2)}, u32[]{:S(2)}) collective-permute-start(bf16[176,2048]{1,0:T(8,128)(2,1)S(1)} %get-tuple-element.38), channel_id=1, source_target_pairs={{0,3},{1,0},{2,1},{3,2},{4,7},{5,4},{6,5},{7,6},{8,11},{9,8},{10,9... | collective-permute-start | bytes 2162696 | tf_op jit(solution)/shard_map/ppermute | solution.py:245
  44.0 18.6 %collective-permute-start.9 = (bf16[176,2048]{1,0:T(8,128)(2,1)S(1)}, bf16[176,2048]{1,0:T(8,128)(2,1)S(1)}, u32[]{:S(2)}, u32[]{:S(2)}) collective-permute-start(bf16[176,2048]{1,0:T(8,128)(2,1)S(1)} %get-tuple-element.39), channel_id=1, source_target_pairs={{0,1},{1,2},{2,3},{3,0},{4,5},{5,6},{6,7},{7,4},{8,9},{9,10},{10,1... | collective-permute-start | bytes 2162696 | tf_op jit(solution)/shard_map/ppermute | solution.py:245
  45.2 8.5 %copy-start.2 = (f32[1024]{0:T(1024)S(1)}, f32[1024]{0:T(1024)}, u32[]{:S(2)}) copy-start(f32[1024]{0:T(1024)} %param.10) | copy-start | bytes 12292
  45.2 23.4 %collective-permute-start.7 = (bf16[128,2048]{1,0:T(8,128)(2,1)S(1)}, bf16[128,2048]{1,0:T(8,128)(2,1)S(1)}, u32[]{:S(2)}, u32[]{:S(2)}) collective-permute-start(bf16[128,2048]{1,0:T(8,128)(2,1)S(1)} %pad_maximum_fusion.1), channel_id=1, source_target_pairs={{0,64},{4,68},{8,72},{12,76},{16,80},{20,84},{24,88},{28,92},{32,9... | collective-permute-start | bytes 1572872 | tf_op jit(solution)/shard_map/ppermute | solution.py:247
  59.8 8.7 %collective-permute-start.8 = (bf16[64,2048]{1,0:T(8,128)(2,1)S(1)}, bf16[64,2048]{1,0:T(8,128)(2,1)S(1)}, u32[]{:S(2)}, u32[]{:S(2)}) collective-permute-start(bf16[64,2048]{1,0:T(8,128)(2,1)S(1)} %get-tuple-element.42), channel_id=1, source_target_pairs={{0,3},{1,0},{2,1},{3,2},{4,7},{5,4},{6,5},{7,6},{8,11},{9,8},{10,9... | collective-permute-start | bytes 786440 | tf_op jit(solution)/shard_map/ppermute | solution.py:251
  60.2 8.4 %collective-permute-start.6 = (bf16[64,2048]{1,0:T(8,128)(2,1)S(1)}, bf16[64,2048]{1,0:T(8,128)(2,1)S(1)}, u32[]{:S(2)}, u32[]{:S(2)}) collective-permute-start(bf16[64,2048]{1,0:T(8,128)(2,1)S(1)} %get-tuple-element.43), channel_id=1, source_target_pairs={{0,1},{1,2},{2,3},{3,0},{4,5},{5,6},{6,7},{7,4},{8,9},{9,10},{10,1... | collective-permute-start | bytes 786440 | tf_op jit(solution)/shard_map/ppermute | solution.py:251
  74.6 6.8 %collective-permute-start.13 = (f32[1,128]{1,0:T(1,128)S(1)}, f32[1,128]{1,0:T(1,128)S(1)}, u32[]{:S(2)}, u32[]{:S(2)}) collective-permute-start(f32[1,128]{1,0:T(1,128)S(1)} %get-tuple-element.35), channel_id=1, source_target_pairs={{0,24},{4,28},{8,0},{12,4},{16,8},{20,12},{24,16},{28,20},{32,56},... | collective-permute-start | bytes 1544 | tf_op jit(solution)/shard_map/ppermute | solution.py:274
  77.6 5.0 %collective-permute-start.12 = (f32[1,128]{1,0:T(1,128)S(1)}, f32[1,128]{1,0:T(1,128)S(1)}, u32[]{:S(2)}, u32[]{:S(2)}) collective-permute-start(f32[1,128]{1,0:T(1,128)S(1)} %get-tuple-element.35), channel_id=1, source_target_pairs={{0,16},{4,20},{8,24},{12,28},{16,0},{20,4},{24,8},{28,12},{32,48},... | collective-permute-start | bytes 1544 | tf_op jit(solution)/shard_map/ppermute | solution.py:274
  78.2 4.8 %collective-permute-start.11 = (f32[1,128]{1,0:T(1,128)S(1)}, f32[1,128]{1,0:T(1,128)S(1)}, u32[]{:S(2)}, u32[]{:S(2)}) collective-permute-start(f32[1,128]{1,0:T(1,128)S(1)} %get-tuple-element.35), channel_id=1, source_target_pairs={{0,8},{4,12},{8,16},{12,20},{16,24},{20,28},{24,0},{28,4},{32,40},... | collective-permute-start | bytes 1544 | tf_op jit(solution)/shard_map/ppermute | solution.py:274
  83.0 9.0 %copy-start.5 = (s32[32]{0:T(128)S(1)}, s32[32]{0:T(128)}, u32[]{:S(2)}) copy-start(s32[32]{0:T(128)} %param.12) | copy-start | bytes 388
  83.0 34.8 %all-to-all-start = ((bf16[32,2,16,1024]{3,2,1,0:T(8,128)(2,1)}), bf16[32,2,16,1024]{3,2,1,0:T(8,128)(2,1)S(1)}, u32[]{:S(2)}, u32[]{:S(2)}) async-start(bf16[32,2,16,1024]{3,2,1,0:T(8,128)(2,1)} %shard_map.92), calls=%async_computation | async-start | bytes 4194304 | tf_op jit(solution)/shard_map/all_to_all | solution.py:278
  88.8 3.8 %collective-permute-start.16 = (f32[1,128]{1,0:T(1,128)S(1)}, f32[1,128]{1,0:T(1,128)S(1)}, u32[]{:S(2)}, u32[]{:S(2)}) collective-permute-start(f32[1,128]{1,0:T(1,128)S(1)} %add_add_fusion.2), channel_id=1, source_target_pairs={{0,3},{1,0},{2,1},{3,2},{4,7},{5,4},{6,5},{7,6},{8,11},{9,8},{10,9... | collective-permute-start | bytes 1544 | tf_op jit(solution)/shard_map/ppermute | solution.py:279
  89.8 5.0 %collective-permute-start.15 = (f32[1,128]{1,0:T(1,128)S(1)}, f32[1,128]{1,0:T(1,128)S(1)}, u32[]{:S(2)}, u32[]{:S(2)}) collective-permute-start(f32[1,128]{1,0:T(1,128)S(1)} %add_add_fusion.2), channel_id=1, source_target_pairs={{0,2},{1,3},{2,0},{3,1},{4,6},{5,7},{6,4},{7,5},{8,10},{9,11},{10,... | collective-permute-start | bytes 1544 | tf_op jit(solution)/shard_map/ppermute | solution.py:279
  91.9 4.8 %collective-permute-start.14 = (f32[1,128]{1,0:T(1,128)S(1)}, f32[1,128]{1,0:T(1,128)S(1)}, u32[]{:S(2)}, u32[]{:S(2)}) collective-permute-start(f32[1,128]{1,0:T(1,128)S(1)} %add_add_fusion.2), channel_id=1, source_target_pairs={{0,1},{1,2},{2,3},{3,0},{4,5},{5,6},{6,7},{7,4},{8,9},{9,10},{10,1... | collective-permute-start | bytes 1544 | tf_op jit(solution)/shard_map/ppermute | solution.py:279
  96.7 1.1 collective-permute-start.17
  97.8 16.6 %collective-permute-start.20 = (f32[1,128]{1,0:T(1,128)S(1)}, f32[1,128]{1,0:T(1,128)S(1)}, u32[]{:S(2)}, u32[]{:S(2)}) collective-permute-start(f32[1,128]{1,0:T(1,128)S(1)} %add.127), channel_id=1, source_target_pairs={{0,96},{4,100},{8,104},{12,108},{16,112},{20,116},{24,120},{28,124... | collective-permute-start | bytes 1544 | tf_op jit(solution)/shard_map/ppermute | solution.py:274
  100.9 15.0 %collective-permute-start.19 = (f32[1,128]{1,0:T(1,128)S(1)}, f32[1,128]{1,0:T(1,128)S(1)}, u32[]{:S(2)}, u32[]{:S(2)}) collective-permute-start(f32[1,128]{1,0:T(1,128)S(1)} %add.127), channel_id=1, source_target_pairs={{0,64},{4,68},{8,72},{12,76},{16,80},{20,84},{24,88},{28,92},{32,9... | collective-permute-start | bytes 1544 | tf_op jit(solution)/shard_map/ppermute | solution.py:274
  101.7 14.2 %collective-permute-start.18 = (f32[1,128]{1,0:T(1,128)S(1)}, f32[1,128]{1,0:T(1,128)S(1)}, u32[]{:S(2)}, u32[]{:S(2)}) collective-permute-start(f32[1,128]{1,0:T(1,128)S(1)} %add.127), channel_id=1, source_target_pairs={{0,32},{4,36},{8,40},{12,44},{16,48},{20,52},{24,56},{28,60},{32,6... | collective-permute-start | bytes 1544 | tf_op jit(solution)/shard_map/ppermute | solution.py:274

commit v4 on v3

--- a/solution.py
+++ b/solution.py
@@ -122,8 +122,9 @@
     lax.fori_loop(0, shards, fill, 0, unroll=4)
 
 
-def advantage_kernel(rewards, shares, advantage):
-    advantage[...] = jnp.sum(rewards[...] * shares[...], axis=1, keepdims=True)
+def advantage_kernel(shares, *refs):
+    terms, advantage = refs[:-1], refs[-1]
+    advantage[...] = jnp.sum(sum(term[...] for term in terms) * shares[...], axis=1, keepdims=True)
 
 
 def whole(shape):
@@ -241,9 +242,7 @@
     far_low, far_high = up(below[:half]), down(above[half:])
     crossed = across(jnp.concatenate([below[:END], above[seq - END:]], axis=0))
     own_partial = middle([below, above], own_start)
-    theirs, own_partial = ahead(theirs, own_partial)
     their_below_high, their_above_low = up(theirs[END:]), down(theirs[:seq - END])
-    theirs, far_low, far_high = ahead(theirs, far_low, far_high)
     far_middle = across(jnp.concatenate([far_low[PASSED:], far_high[:half - PASSED]], axis=0))
     own_states, own_reward = finish([far_low, far_high], own_partial, own, jnp.zeros((1, LANES), jnp.float32))
     their_start = start(theirs)
@@ -269,19 +268,19 @@
     across_size = sections * 2
     along = sections * dp_size // (cores * across_size)
 
-    def summed(terms, span, size):
+    def exchanged(terms, span, size):
         pairs = [turn(sections * dp_size, span, size, step) for step in range(1, size)]
-        return terms + sum(lax.ppermute(terms, PLANE, pair) for pair in pairs)
-
-    rewards = summed(rewards, cores, along)
+        return [terms] + [lax.ppermute(terms, PLANE, pair) for pair in pairs]
+
+    rewards = sum(exchanged(rewards, cores, along))
     outgoing, rewards = ahead(outgoing, rewards)
     received = lax.all_to_all(outgoing, PLANE, split_axis=0, concat_axis=0, tiled=True)
     rewards += sum(lax.ppermute(rewards, "mp", ring(mp_size, step)) for step in range(1, mp_size))
-    rewards = summed(rewards, 1, cores)
-    rewards = summed(rewards, cores * along, across_size)
+    rewards = sum(exchanged(rewards, 1, cores))
+    terms = exchanged(rewards, cores * along, across_size)
     advantage = pl.pallas_call(
         advantage_kernel, out_shape=jax.ShapeDtypeStruct((1, 1), jnp.float32)
-    )(rewards, shares)
+    )(shares, *terms)
     return (received[None], advantage.reshape(1))
 
 

time: 120 us -> 119 us (level)
  waiting for transfers between devices: 29.1 us -> 25.1 us
  starting transfers between devices: 39.9 us -> 43 us
    ppermute x1, starting transfers between devices: 0.35 us -> 3.22 us  [body(): down(crossed[2 * END - PASSED:])]
    ppermute x1, waiting for transfers between devices: 0.01 us -> 2.68 us  [body(): theirs = across(mine_across)]
    ppermute x2, waiting for transfers between devices: 9.08 us -> 6.41 us  [body(): below, above = (up(mine), down(mine))]
    ppermute x3, waiting for transfers between devices: 4.08 us -> 1.62 us  [body(): lax.ppermute(rewards, 'mp', ring(mp_size, step))]
    ppermute x1, starting transfers between devices: 5 us -> 3.11 us  [body(): across(jnp.concatenate([far_low[PASSED:], far_high[:half - PASSED]], axis...]
    ppermute x3, starting transfers between devices: 3.12 us -> 4.94 us  [body(): lax.ppermute(rewards, 'mp', ring(mp_size, step))]
    all_to_all x1, starting transfers between devices: 5.82 us -> 4.15 us  [body(): lax.all_to_all(outgoing, PLANE, split_axis=0, concat_axis=0, tiled=True)]
    ppermute x1, starting transfers between devices: 1.75 us -> 0.08 us  [body(): up(crossed[:PASSED])]
  transfers between devices with their start and end apart: 22 -> 22, of which waited for: 11 -> 9; matrix products, arithmetic and copies ran while one was open for 9% -> 8% of each run, Pallas kernels for 24% -> 24%
where the time goes in v4:
time: 119 us; the launch traced here: 118 us
  starting transfers between devices  43 us (36%)
  Pallas kernels  34.7 us (29%)
  waiting for transfers between devices  25.1 us (21%)
  local copies, waits for them, and re-layouts  12 us (10%)
  other arithmetic  2.54 us (2%)
    pallas_call x6, Pallas kernels, call(): pl.pallas_call(functools.partial(kernel, depth_steps), grid_spec=pltpu.Pr...  31.2 us
    ppermute x7, waiting for transfers between devices, exchanged(): return [terms] + [lax.ppermute(terms, PLANE, pair) for pair in pairs]  14.4 us
    ppermute x7, starting transfers between devices, exchanged(): return [terms] + [lax.ppermute(terms, PLANE, pair) for pair in pairs]  10.5 us
    unnamed x22, local copies, waits for them, and re-layouts  9.26 us
    ppermute x2, waiting for transfers between devices, body(): below, above = (up(mine), down(mine))  6.41 us
    ppermute x3, starting transfers between devices, body(): lax.ppermute(rewards, 'mp', ring(mp_size, step))  4.94 us
    ppermute x2, starting transfers between devices, body(): below, above = (up(mine), down(mine))  4.27 us
    all_to_all x1, starting transfers between devices, body(): lax.all_to_all(outgoing, PLANE, split_axis=0, concat_axis=0, tiled=True)  4.15 us
  transfers between devices with their start and end apart: 22, of which 9 were waited for; matrix products, arithmetic and copies ran while one was open for 8% of the time, Pallas kernels for 24%

profile of v4, /device:TPU:0, one launch (start us, length us, event | category | flops | bytes accessed | tf_op | source)
XLA Modules:
  0.0 118.3 jit_solution(9043121932333319484)
XLA Ops:
  0.6 2.1 %collective-permute-start = (bf16[256,2048]{1,0:T(8,128)(2,1)}, bf16[256,2048]{1,0:T(8,128)(2,1)S(1)}, u32[]{:S(2)}, u32[]{:S(2)}) collective-permute-start(bf16[256,2048]{1,0:T(8,128)(2,1)} %bitcast.1.refs_0_), channel_id=1, source_target_pairs={{0,1},{1,2},{2,3},{3,0},{4,5},{5,6},{6,7},{7,4},{8,9},{9,10},{10,1... | collective-permute-start | bytes 3145736 | tf_op jit(solution)/shard_map/ppermute | solution.py:180
  2.7 2.2 %collective-permute-start.1 = (bf16[256,2048]{1,0:T(8,128)(2,1)}, bf16[256,2048]{1,0:T(8,128)(2,1)S(1)}, u32[]{:S(2)}, u32[]{:S(2)}) collective-permute-start(bf16[256,2048]{1,0:T(8,128)(2,1)} %bitcast.1.refs_0_), channel_id=1, source_target_pairs={{0,3},{1,0},{2,1},{3,2},{4,7},{5,4},{6,5},{7,6},{8,11},{9,8},{10,9... | collective-permute-start | bytes 3145736 | tf_op jit(solution)/shard_map/ppermute | solution.py:180
  4.9 4.7 %copy.11 = bf16[1024,8,2,128]{3,1,2,0:T(8,128)(2,1)} copy(bf16[1024,8,2,128]{3,2,1,0:T(2,128)(2,1)} %bitcast.31) | data formatting | bytes 8388608
  9.6 3.0 %collective-permute-start.8 = (bf16[256,2048]{1,0:T(8,128)(2,1)}, bf16[256,2048]{1,0:T(8,128)(2,1)S(1)}, u32[]{:S(2)}, u32[]{:S(2)}) collective-permute-start(bf16[256,2048]{1,0:T(8,128)(2,1)} %bitcast.1.refs_0_), channel_id=1, source_target_pairs={{0,64},{4,68},{8,72},{12,76},{16,80},{20,84},{24,88},{28,92},{32,9... | collective-permute-start | bytes 3145736 | tf_op jit(solution)/shard_map/ppermute | solution.py:182
  12.7 0.1 pad_add_fusion.1.refs_0_
  12.7 0.7 fusion.8
  13.4 0.6 fusion.7
  14.0 0.8 pad_add_fusion.places
  14.8 0.8 pad_add_fusion.2.places
  15.5 0.2 convert_reduce_fusion
  15.7 0.1 select_reduce_fusion
  15.8 2.2 %copy-done = bf16[1024,8,2,128]{3,1,2,0:T(8,128)(2,1)S(1)} copy-done((bf16[1024,8,2,128]{3,1,2,0:T(8,128)(2,1)S(1)}, bf16[1024,8,2,128]{3,1,2,0:T(8,128)(2,1)}, u32[]{:S(2)}) %copy-start) | copy-done | bytes 4194328
  18.0 3.8 %shard_map.86.refs_3_ = f32[256,1280]{1,0:T(8,128)S(1)} custom-call(s32[1]{0:T(128)} %bitcast.2.places, bf16[256,2048]{1,0:T(8,128)(2,1)} %bitcast.1.refs_0_, bf16[1,8192,1024]{2,1,0:T(8,128)(2,1)} %refs_4_.3, bf16[8192,256]{1,0:T(8,128)(2,1)S(1)} %bitcast.22), custom_call_target="tpu_custom_call" | custom-call | flops 1342177280 | bytes 5242880 | tf_op jit(solution)/shard_map/pallas_call | solution.py:197
  21.8 6.4 %collective-permute-done.refs_1_ = bf16[256,2048]{1,0:T(8,128)(2,1)S(1)} collective-permute-done((bf16[256,2048]{1,0:T(8,128)(2,1)}, bf16[256,2048]{1,0:T(8,128)(2,1)S(1)}, u32[]{:S(2)}, u32[]{:S(2)}) %collective-permute-start) | collective-permute-done | bytes 1048608 | tf_op jit(solution)/shard_map/ppermute | solution.py:180
  28.4 3.1 %collective-permute-start.2 = (bf16[160,2048]{1,0:T(8,128)(2,1)S(1)}, bf16[160,2048]{1,0:T(8,128)(2,1)S(1)}, u32[]{:S(2)}, u32[]{:S(2)}) collective-permute-start(bf16[160,2048]{1,0:T(8,128)(2,1)S(1)} %pad_maximum_fusion), channel_id=1, source_target_pairs={{0,64},{4,68},{8,72},{12,76},{16,80},{20,84},{24,88},{28,92},{32,9... | collective-permute-start | bytes 1966088 | tf_op jit(solution)/shard_map/ppermute | solution.py:243
  31.5 1.3 %collective-permute-start.3 = (bf16[128,2048]{1,0:T(8,128)(2,1)S(1)}, bf16[128,2048]{1,0:T(8,128)(2,1)S(1)}, u32[]{:S(2)}, u32[]{:S(2)}) collective-permute-start(bf16[128,2048]{1,0:T(8,128)(2,1)S(1)} %slice.38), channel_id=1, source_target_pairs={{0,1},{1,2},{2,3},{3,0},{4,5},{5,6},{6,7},{7,4},{8,9},{9,10},{10,1... | collective-permute-start | bytes 1572872 | tf_op jit(solution)/shard_map/ppermute | solution.py:242
  32.8 2.0 %collective-permute-start.4 = (bf16[128,2048]{1,0:T(8,128)(2,1)S(1)}, bf16[128,2048]{1,0:T(8,128)(2,1)S(1)}, u32[]{:S(2)}, u32[]{:S(2)}) collective-permute-start(bf16[128,2048]{1,0:T(8,128)(2,1)S(1)} %slice.39), channel_id=1, source_target_pairs={{0,3},{1,0},{2,1},{3,2},{4,7},{5,4},{6,5},{7,6},{8,11},{9,8},{10,9... | collective-permute-start | bytes 1572872 | tf_op jit(solution)/shard_map/ppermute | solution.py:242
  34.7 2.7 %collective-permute-done.8.refs_0_ = bf16[256,2048]{1,0:T(8,128)(2,1)S(1)} collective-permute-done((bf16[256,2048]{1,0:T(8,128)(2,1)}, bf16[256,2048]{1,0:T(8,128)(2,1)S(1)}, u32[]{:S(2)}, u32[]{:S(2)}) %collective-permute-start.8) | collective-permute-done | bytes 1048608 | tf_op jit(solution)/shard_map/ppermute | solution.py:182
  37.4 0.2 fusion.4
  37.6 0.1 collective-permute-start.9
  37.7 3.2 %collective-permute-start.10 = (bf16[176,2048]{1,0:T(8,128)(2,1)S(1)}, bf16[176,2048]{1,0:T(8,128)(2,1)S(1)}, u32[]{:S(2)}, u32[]{:S(2)}) collective-permute-start(bf16[176,2048]{1,0:T(8,128)(2,1)S(1)} %get-tuple-element.28), channel_id=1, source_target_pairs={{0,3},{1,0},{2,1},{3,2},{4,7},{5,4},{6,5},{7,6},{8,11},{9,8},{10,9... | collective-permute-start | bytes 2162696 | tf_op jit(solution)/shard_map/ppermute | solution.py:245
  40.9 3.5 %shard_map.89.refs_5_ = f32[256,1280]{1,0:T(8,128)S(1)} custom-call(s32[1]{0:T(128)} %bitcast.2.places, bf16[256,2048]{1,0:T(8,128)(2,1)S(1)} %collective-permute-done.8.refs_0_, bf16[1,8192,1024]{2,1,0:T(8,128)(2,1)} %refs_4_.3, bf16[8192,256]{1,0:T(8,128)(2,1)S(1)} %bitcast.23), custom_call_target="tpu_custom_call" | custom-call | flops 1342177280 | bytes 5242880 | tf_op jit(solution)/shard_map/pallas_call | solution.py:197
  44.4 6.0 %shard_map.87.refs_2_ = f32[256,1280]{1,0:T(8,128)S(1)} custom-call(s32[2]{0:T(128)S(1)} %pad_add_fusion.1.refs_0_, bf16[256,2048]{1,0:T(8,128)(2,1)S(1)} %collective-permute-done.refs_1_, bf16[256,2048]{1,0:T(8,128)(2,1)S(1)} %collective-permute-done.1.refs_2_, f32[256,1280]{1,0:T(8,128)S(1)} %shard_map.86.refs_3_, bf16[1,8192,1024]{2,1,0:T(8,128)(2,1)} %refs_4_.3, ...), custom_call_target="tpu_custom_call" | custom-call | flops 2684354560 | bytes 10485760 | tf_op jit(solution)/shard_map/pallas_call | solution.py:197
  50.4 0.0 copy-start.2
  50.4 0.0 collective-permute-done.4.refs_1_
  50.5 3.1 %collective-permute-start.6 = (bf16[128,2048]{1,0:T(8,128)(2,1)S(1)}, bf16[128,2048]{1,0:T(8,128)(2,1)S(1)}, u32[]{:S(2)}, u32[]{:S(2)}) collective-permute-start(bf16[128,2048]{1,0:T(8,128)(2,1)S(1)} %pad_maximum_fusion.1), channel_id=1, source_target_pairs={{0,64},{4,68},{8,72},{12,76},{16,80},{20,84},{24,88},{28,92},{32,9... | collective-permute-start | bytes 1572872 | tf_op jit(solution)/shard_map/ppermute | solution.py:246
  53.6 6.0 %shard_map.88 = (bf16[256,1024]{1,0:T(8,128)(2,1)S(1)}, f32[1,128]{1,0:T(1,128)S(1)}) custom-call(s32[3]{0:T(128)S(1)} %pad_add_fusion.places, bf16[128,2048]{1,0:T(8,128)(2,1)S(1)} %collective-permute-done.3.refs_0_, bf16[128,2048]{1,0:T(8,128)(2,1)S(1)} %collective-permute-done.4.refs_1_, f32[256,1280]{1,0:T(8,128)S(1)} %shard_map.87.refs_2_, ...), custom_call_target="tpu_custom_call" | custom-call | flops 1342177280 | bytes 5242880 | tf_op jit(solution)/shard_map/pallas_call | solution.py:197
  59.7 0.1 collective-permute-start.5
  59.8 3.2 %collective-permute-start.7 = (bf16[64,2048]{1,0:T(8,128)(2,1)S(1)}, bf16[64,2048]{1,0:T(8,128)(2,1)S(1)}, u32[]{:S(2)}, u32[]{:S(2)}) collective-permute-start(bf16[64,2048]{1,0:T(8,128)(2,1)S(1)} %get-tuple-element.32), channel_id=1, source_target_pairs={{0,3},{1,0},{2,1},{3,2},{4,7},{5,4},{6,5},{7,6},{8,11},{9,8},{10,9... | collective-permute-start | bytes 786440 | tf_op jit(solution)/shard_map/ppermute | solution.py:250
  63.0 0.1 fusion.5
  63.0 0.0 collective-permute-done.9.refs_2_
  63.1 6.0 %shard_map.90.refs_3_ = f32[256,1280]{1,0:T(8,128)S(1)} custom-call(s32[2]{0:T(128)S(1)} %pad_add_fusion.1.refs_0_, bf16[80,2048]{1,0:T(8,128)(2,1)S(1)} %get-tuple-element.31.refs_1_, bf16[176,2048]{1,0:T(8,128)(2,1)S(1)} %collective-permute-done.9.refs_2_, bf16[176,2048]{1,0:T(8,128)(2,1)S(1)} %collective-permute-done.10.refs_3_, ...), custom_call_target="tpu_custom_call" | custom-call | flops 2684354560 | bytes 10485760 | tf_op jit(solution)/shard_map/pallas_call | solution.py:197
  69.1 0.0 collective-permute-done.5.refs_0_
  69.1 0.0 collective-permute-done.7.refs_2_
  69.1 6.0 %shard_map.91 = (bf16[256,1024]{1,0:T(8,128)(2,1)S(1)}, f32[1,128]{1,0:T(1,128)S(1)}) custom-call(s32[3]{0:T(128)S(1)} %pad_add_fusion.2.places, bf16[64,2048]{1,0:T(8,128)(2,1)S(1)} %collective-permute-done.5.refs_0_, bf16[128,2048]{1,0:T(8,128)(2,1)S(1)} %collective-permute-done.6.refs_1_, bf16[64,2048]{1,0:T(8,128)(2,1)S(1)} %collective-permute-done.7.refs_2_, ...), custom_call_target="tpu_custom_call" | custom-call | flops 1342177280 | bytes 5242880 | tf_op jit(solution)/shard_map/pallas_call | solution.py:197
  75.1 3.0 %collective-permute-start.13 = (f32[1,128]{1,0:T(1,128)S(1)}, f32[1,128]{1,0:T(1,128)S(1)}, u32[]{:S(2)}, u32[]{:S(2)}) collective-permute-start(f32[1,128]{1,0:T(1,128)S(1)} %get-tuple-element.25), channel_id=1, source_target_pairs={{0,24},{4,28},{8,0},{12,4},{16,8},{20,12},{24,16},{28,20},{32,56},... | collective-permute-start | bytes 1544 | tf_op jit(solution)/shard_map/ppermute | solution.py:273
  78.1 0.6 collective-permute-start.12
  78.7 1.0 collective-permute-start.11
  79.7 2.2 %shard_map.92 = bf16[32,2,16,1024]{3,2,1,0:T(8,128)(2,1)} custom-call(s32[64]{0:T(128)S(1)} %broadcast_add_fusion.slots, bf16[256,1024]{1,0:T(8,128)(2,1)S(1)} %get-tuple-element.20.first, bf16[256,1024]{1,0:T(8,128)(2,1)S(1)} %get-tuple-element.24.second), custom_call_target="tpu_custom_call" | custom-call | bytes 1572864 | tf_op jit(solution)/shard_map/pallas_call | solution.py:255
  81.9 0.0 collective-permute-done.13
  81.9 1.2 %collective-permute-done.12 = f32[1,128]{1,0:T(1,128)S(1)} collective-permute-done((f32[1,128]{1,0:T(1,128)S(1)}, f32[1,128]{1,0:T(1,128)S(1)}, u32[]{:S(2)}, u32[]{:S(2)}) %collective-permute-start.12) | collective-permute-done | bytes 544 | tf_op jit(solution)/shard_map/ppermute | solution.py:273
  83.2 0.3 collective-permute-done.11
  83.5 4.1 %all-to-all-start = ((bf16[32,2,16,1024]{3,2,1,0:T(8,128)(2,1)}), bf16[32,2,16,1024]{3,2,1,0:T(8,128)(2,1)S(1)}, u32[]{:S(2)}, u32[]{:S(2)}) async-start(bf16[32,2,16,1024]{3,2,1,0:T(8,128)(2,1)} %shard_map.92), calls=%async_computation | async-start | bytes 4194304 | tf_op jit(solution)/shard_map/all_to_all | solution.py:277
  87.7 2.0 %collective-permute-start.16 = (f32[1,128]{1,0:T(1,128)S(1)}, f32[1,128]{1,0:T(1,128)S(1)}, u32[]{:S(2)}, u32[]{:S(2)}) collective-permute-start(f32[1,128]{1,0:T(1,128)S(1)} %add_add_fusion.1), channel_id=1, source_target_pairs={{0,3},{1,0},{2,1},{3,2},{4,7},{5,4},{6,5},{7,6},{8,11},{9,8},{10,9... | collective-permute-start | bytes 1544 | tf_op jit(solution)/shard_map/ppermute | solution.py:278
  89.6 0.1 collective-permute-start.14
  89.7 2.8 %collective-permute-start.15 = (f32[1,128]{1,0:T(1,128)S(1)}, f32[1,128]{1,0:T(1,128)S(1)}, u32[]{:S(2)}, u32[]{:S(2)}) collective-permute-start(f32[1,128]{1,0:T(1,128)S(1)} %add_add_fusion.1), channel_id=1, source_target_pairs={{0,2},{1,3},{2,0},{3,1},{4,6},{5,7},{6,4},{7,5},{8,10},{9,11},{10,... | collective-permute-start | bytes 1544 | tf_op jit(solution)/shard_map/ppermute | solution.py:278
  92.6 0.6 dynamic_slice.19
  93.2 0.0 collective-permute-done.16
  93.2 1.2 %collective-permute-done.14 = f32[1,128]{1,0:T(1,128)S(1)} collective-permute-done((f32[1,128]{1,0:T(1,128)S(1)}, f32[1,128]{1,0:T(1,128)S(1)}, u32[]{:S(2)}, u32[]{:S(2)}) %collective-permute-start.14) | collective-permute-done | bytes 544 | tf_op jit(solution)/shard_map/ppermute | solution.py:278
  94.4 0.4 collective-permute-done.15
  94.8 0.0 collective-permute-start.17
  94.8 0.6 fusion.1
  95.4 0.5 collective-permute-done.17
  95.9 1.7 %collective-permute-start.18 = (f32[1,128]{1,0:T(1,128)S(1)}, f32[1,128]{1,0:T(1,128)S(1)}, u32[]{:S(2)}, u32[]{:S(2)}) collective-permute-start(f32[1,128]{1,0:T(1,128)S(1)} %add.118.refs_0_), channel_id=1, source_target_pairs={{0,32},{4,36},{8,40},{12,44},{16,48},{20,52},{24,56},{28,60},{32,6... | collective-permute-start | bytes 1544 | tf_op jit(solution)/shard_map/ppermute | solution.py:273
  97.7 2.8 %collective-permute-start.19 = (f32[1,128]{1,0:T(1,128)S(1)}, f32[1,128]{1,0:T(1,128)S(1)}, u32[]{:S(2)}, u32[]{:S(2)}) collective-permute-start(f32[1,128]{1,0:T(1,128)S(1)} %add.118.refs_0_), channel_id=1, source_target_pairs={{0,64},{4,68},{8,72},{12,76},{16,80},{20,84},{24,88},{28,92},{32,9... | collective-permute-start | bytes 1544 | tf_op jit(solution)/shard_map/ppermute | solution.py:273
  100.4 1.4 %collective-permute-start.20 = (f32[1,128]{1,0:T(1,128)S(1)}, f32[1,128]{1,0:T(1,128)S(1)}, u32[]{:S(2)}, u32[]{:S(2)}) collective-permute-start(f32[1,128]{1,0:T(1,128)S(1)} %add.118.refs_0_), channel_id=1, source_target_pairs={{0,96},{4,100},{8,104},{12,108},{16,112},{20,116},{24,120},{28,124... | collective-permute-start | bytes 1544 | tf_op jit(solution)/shard_map/ppermute | solution.py:273
  101.8 0.5 pad_bitcast_fusion.shares
  102.3 9.3 %collective-permute-done.18.refs_1_ = f32[1,128]{1,0:T(1,128)S(1)} collective-permute-done((f32[1,128]{1,0:T(1,128)S(1)}, f32[1,128]{1,0:T(1,128)S(1)}, u32[]{:S(2)}, u32[]{:S(2)}) %collective-permute-start.18) | collective-permute-done | bytes 544 | tf_op jit(solution)/shard_map/ppermute | solution.py:273
  111.7 3.0 %collective-permute-done.19.refs_2_ = f32[1,128]{1,0:T(1,128)S(1)} collective-permute-done((f32[1,128]{1,0:T(1,128)S(1)}, f32[1,128]{1,0:T(1,128)S(1)}, u32[]{:S(2)}, u32[]{:S(2)}) %collective-permute-start.19) | collective-permute-done | bytes 544 | tf_op jit(solution)/shard_map/ppermute | solution.py:273
  114.7 0.5 copy-done.8
  115.2 0.5 copy-done.9
  115.7 1.3 %shard_map.93 = f32[1,1]{1,0:T(1,128)} custom-call(f32[1,128]{1,0:T(1,128)} %pad_bitcast_fusion.shares, f32[1,128]{1,0:T(1,128)} %copy-done.6, f32[1,128]{1,0:T(1,128)} %copy-done.7, f32[1,128]{1,0:T(1,128)} %copy-done.8, f32[1,128]{1,0:T(1,128)} %copy-done.9), custom_call_target="tpu_custom_call" | custom-call | tf_op jit(solution)/shard_map/pallas_call | solution.py:281
  116.9 0.0 all-to-all-done
  116.9 1.3 %copy.13 = bf16[1,32,2,16,1024]{4,3,2,1,0:T(8,128)(2,1)} copy(bf16[1,32,2,16,1024]{4,3,2,1,0:T(8,128)(2,1)S(1)} %bitcast.30) | data formatting | bytes 4194304
  (38 shorter events, 0.4 us)
Async XLA Ops:
  0.6 27.6 %collective-permute-start = (bf16[256,2048]{1,0:T(8,128)(2,1)}, bf16[256,2048]{1,0:T(8,128)(2,1)S(1)}, u32[]{:S(2)}, u32[]{:S(2)}) collective-permute-start(bf16[256,2048]{1,0:T(8,128)(2,1)} %bitcast.1.refs_0_), channel_id=1, source_target_pairs={{0,1},{1,2},{2,3},{3,0},{4,5},{5,6},{6,7},{7,4},{8,9},{9,10},{10,1... | collective-permute-start | bytes 3145736 | tf_op jit(solution)/shard_map/ppermute | solution.py:180
  2.7 25.5 %collective-permute-start.1 = (bf16[256,2048]{1,0:T(8,128)(2,1)}, bf16[256,2048]{1,0:T(8,128)(2,1)S(1)}, u32[]{:S(2)}, u32[]{:S(2)}) collective-permute-start(bf16[256,2048]{1,0:T(8,128)(2,1)} %bitcast.1.refs_0_), channel_id=1, source_target_pairs={{0,3},{1,0},{2,1},{3,2},{4,7},{5,4},{6,5},{7,6},{8,11},{9,8},{10,9... | collective-permute-start | bytes 3145736 | tf_op jit(solution)/shard_map/ppermute | solution.py:180
  4.9 7.8 %copy-start.3 = (s32[32]{0:T(128)S(1)}, s32[32]{0:T(128)}, u32[]{:S(2)}) copy-start(s32[32]{0:T(128)} %param.11) | copy-start | bytes 388
  4.9 10.6 %copy-start.4 = (s32[32,1]{0,1:T(1,128)S(1)}, s32[32,1]{0,1:T(1,128)}, u32[]{:S(2)}) copy-start(s32[32,1]{0,1:T(1,128)} %param.13) | copy-start | bytes 388
  9.6 27.8 %collective-permute-start.8 = (bf16[256,2048]{1,0:T(8,128)(2,1)}, bf16[256,2048]{1,0:T(8,128)(2,1)S(1)}, u32[]{:S(2)}, u32[]{:S(2)}) collective-permute-start(bf16[256,2048]{1,0:T(8,128)(2,1)} %bitcast.1.refs_0_), channel_id=1, source_target_pairs={{0,64},{4,68},{8,72},{12,76},{16,80},{20,84},{24,88},{28,92},{32,9... | collective-permute-start | bytes 3145736 | tf_op jit(solution)/shard_map/ppermute | solution.py:182
  15.8 2.2 %copy-start = (bf16[1024,8,2,128]{3,1,2,0:T(8,128)(2,1)S(1)}, bf16[1024,8,2,128]{3,1,2,0:T(8,128)(2,1)}, u32[]{:S(2)}) copy-start(bf16[1024,8,2,128]{3,1,2,0:T(8,128)(2,1)} %copy.11) | copy-start | bytes 12582916
  28.3 12.6 %copy-start.1 = (bf16[1024,8,2,128]{3,1,2,0:T(8,128)(2,1)S(1)}, bf16[1024,8,2,128]{3,1,2,0:T(8,128)(2,1)}, u32[]{:S(2)}) copy-start(bf16[1024,8,2,128]{3,1,2,0:T(8,128)(2,1)} %copy.11) | copy-start | bytes 12582916
  28.4 31.2 %collective-permute-start.2 = (bf16[160,2048]{1,0:T(8,128)(2,1)S(1)}, bf16[160,2048]{1,0:T(8,128)(2,1)S(1)}, u32[]{:S(2)}, u32[]{:S(2)}) collective-permute-start(bf16[160,2048]{1,0:T(8,128)(2,1)S(1)} %pad_maximum_fusion), channel_id=1, source_target_pairs={{0,64},{4,68},{8,72},{12,76},{16,80},{20,84},{24,88},{28,92},{32,9... | collective-permute-start | bytes 1966088 | tf_op jit(solution)/shard_map/ppermute | solution.py:243
  31.5 18.9 %collective-permute-start.3 = (bf16[128,2048]{1,0:T(8,128)(2,1)S(1)}, bf16[128,2048]{1,0:T(8,128)(2,1)S(1)}, u32[]{:S(2)}, u32[]{:S(2)}) collective-permute-start(bf16[128,2048]{1,0:T(8,128)(2,1)S(1)} %slice.38), channel_id=1, source_target_pairs={{0,1},{1,2},{2,3},{3,0},{4,5},{5,6},{6,7},{7,4},{8,9},{9,10},{10,1... | collective-permute-start | bytes 1572872 | tf_op jit(solution)/shard_map/ppermute | solution.py:242
  32.8 17.6 %collective-permute-start.4 = (bf16[128,2048]{1,0:T(8,128)(2,1)S(1)}, bf16[128,2048]{1,0:T(8,128)(2,1)S(1)}, u32[]{:S(2)}, u32[]{:S(2)}) collective-permute-start(bf16[128,2048]{1,0:T(8,128)(2,1)S(1)} %slice.39), channel_id=1, source_target_pairs={{0,3},{1,0},{2,1},{3,2},{4,7},{5,4},{6,5},{7,6},{8,11},{9,8},{10,9... | collective-permute-start | bytes 1572872 | tf_op jit(solution)/shard_map/ppermute | solution.py:242
  37.6 25.5 %collective-permute-start.9 = (bf16[176,2048]{1,0:T(8,128)(2,1)S(1)}, bf16[176,2048]{1,0:T(8,128)(2,1)S(1)}, u32[]{:S(2)}, u32[]{:S(2)}) collective-permute-start(bf16[176,2048]{1,0:T(8,128)(2,1)S(1)} %get-tuple-element.29), channel_id=1, source_target_pairs={{0,1},{1,2},{2,3},{3,0},{4,5},{5,6},{6,7},{7,4},{8,9},{9,10},{10,1... | collective-permute-start | bytes 2162696 | tf_op jit(solution)/shard_map/ppermute | solution.py:245
  37.7 25.4 %collective-permute-start.10 = (bf16[176,2048]{1,0:T(8,128)(2,1)S(1)}, bf16[176,2048]{1,0:T(8,128)(2,1)S(1)}, u32[]{:S(2)}, u32[]{:S(2)}) collective-permute-start(bf16[176,2048]{1,0:T(8,128)(2,1)S(1)} %get-tuple-element.28), channel_id=1, source_target_pairs={{0,3},{1,0},{2,1},{3,2},{4,7},{5,4},{6,5},{7,6},{8,11},{9,8},{10,9... | collective-permute-start | bytes 2162696 | tf_op jit(solution)/shard_map/ppermute | solution.py:245
  50.4 3.2 %copy-start.2 = (f32[1024]{0:T(1024)S(1)}, f32[1024]{0:T(1024)}, u32[]{:S(2)}) copy-start(f32[1024]{0:T(1024)} %param.10) | copy-start | bytes 12292
  50.5 18.6 %collective-permute-start.6 = (bf16[128,2048]{1,0:T(8,128)(2,1)S(1)}, bf16[128,2048]{1,0:T(8,128)(2,1)S(1)}, u32[]{:S(2)}, u32[]{:S(2)}) collective-permute-start(bf16[128,2048]{1,0:T(8,128)(2,1)S(1)} %pad_maximum_fusion.1), channel_id=1, source_target_pairs={{0,64},{4,68},{8,72},{12,76},{16,80},{20,84},{24,88},{28,92},{32,9... | collective-permute-start | bytes 1572872 | tf_op jit(solution)/shard_map/ppermute | solution.py:246
  59.7 9.4 %collective-permute-start.5 = (bf16[64,2048]{1,0:T(8,128)(2,1)S(1)}, bf16[64,2048]{1,0:T(8,128)(2,1)S(1)}, u32[]{:S(2)}, u32[]{:S(2)}) collective-permute-start(bf16[64,2048]{1,0:T(8,128)(2,1)S(1)} %get-tuple-element.33), channel_id=1, source_target_pairs={{0,1},{1,2},{2,3},{3,0},{4,5},{5,6},{6,7},{7,4},{8,9},{9,10},{10,1... | collective-permute-start | bytes 786440 | tf_op jit(solution)/shard_map/ppermute | solution.py:250
  59.8 9.3 %collective-permute-start.7 = (bf16[64,2048]{1,0:T(8,128)(2,1)S(1)}, bf16[64,2048]{1,0:T(8,128)(2,1)S(1)}, u32[]{:S(2)}, u32[]{:S(2)}) collective-permute-start(bf16[64,2048]{1,0:T(8,128)(2,1)S(1)} %get-tuple-element.32), channel_id=1, source_target_pairs={{0,3},{1,0},{2,1},{3,2},{4,7},{5,4},{6,5},{7,6},{8,11},{9,8},{10,9... | collective-permute-start | bytes 786440 | tf_op jit(solution)/shard_map/ppermute | solution.py:250
  75.1 6.9 %collective-permute-start.13 = (f32[1,128]{1,0:T(1,128)S(1)}, f32[1,128]{1,0:T(1,128)S(1)}, u32[]{:S(2)}, u32[]{:S(2)}) collective-permute-start(f32[1,128]{1,0:T(1,128)S(1)} %get-tuple-element.25), channel_id=1, source_target_pairs={{0,24},{4,28},{8,0},{12,4},{16,8},{20,12},{24,16},{28,20},{32,56},... | collective-permute-start | bytes 1544 | tf_op jit(solution)/shard_map/ppermute | solution.py:273
  78.1 5.0 %collective-permute-start.12 = (f32[1,128]{1,0:T(1,128)S(1)}, f32[1,128]{1,0:T(1,128)S(1)}, u32[]{:S(2)}, u32[]{:S(2)}) collective-permute-start(f32[1,128]{1,0:T(1,128)S(1)} %get-tuple-element.25), channel_id=1, source_target_pairs={{0,16},{4,20},{8,24},{12,28},{16,0},{20,4},{24,8},{28,12},{32,48},... | collective-permute-start | bytes 1544 | tf_op jit(solution)/shard_map/ppermute | solution.py:273
  78.7 4.8 %collective-permute-start.11 = (f32[1,128]{1,0:T(1,128)S(1)}, f32[1,128]{1,0:T(1,128)S(1)}, u32[]{:S(2)}, u32[]{:S(2)}) collective-permute-start(f32[1,128]{1,0:T(1,128)S(1)} %get-tuple-element.25), channel_id=1, source_target_pairs={{0,8},{4,12},{8,16},{12,20},{16,24},{20,28},{24,0},{28,4},{32,40},... | collective-permute-start | bytes 1544 | tf_op jit(solution)/shard_map/ppermute | solution.py:273
  83.5 9.1 %copy-start.5 = (s32[32]{0:T(128)S(1)}, s32[32]{0:T(128)}, u32[]{:S(2)}) copy-start(s32[32]{0:T(128)} %param.12) | copy-start | bytes 388
  83.5 33.4 %all-to-all-start = ((bf16[32,2,16,1024]{3,2,1,0:T(8,128)(2,1)}), bf16[32,2,16,1024]{3,2,1,0:T(8,128)(2,1)S(1)}, u32[]{:S(2)}, u32[]{:S(2)}) async-start(bf16[32,2,16,1024]{3,2,1,0:T(8,128)(2,1)} %shard_map.92), calls=%async_computation | async-start | bytes 4194304 | tf_op jit(solution)/shard_map/all_to_all | solution.py:277
  87.7 5.5 %collective-permute-start.16 = (f32[1,128]{1,0:T(1,128)S(1)}, f32[1,128]{1,0:T(1,128)S(1)}, u32[]{:S(2)}, u32[]{:S(2)}) collective-permute-start(f32[1,128]{1,0:T(1,128)S(1)} %add_add_fusion.1), channel_id=1, source_target_pairs={{0,3},{1,0},{2,1},{3,2},{4,7},{5,4},{6,5},{7,6},{8,11},{9,8},{10,9... | collective-permute-start | bytes 1544 | tf_op jit(solution)/shard_map/ppermute | solution.py:278
  89.6 4.8 %collective-permute-start.14 = (f32[1,128]{1,0:T(1,128)S(1)}, f32[1,128]{1,0:T(1,128)S(1)}, u32[]{:S(2)}, u32[]{:S(2)}) collective-permute-start(f32[1,128]{1,0:T(1,128)S(1)} %add_add_fusion.1), channel_id=1, source_target_pairs={{0,1},{1,2},{2,3},{3,0},{4,5},{5,6},{6,7},{7,4},{8,9},{9,10},{10,1... | collective-permute-start | bytes 1544 | tf_op jit(solution)/shard_map/ppermute | solution.py:278
  89.7 5.0 %collective-permute-start.15 = (f32[1,128]{1,0:T(1,128)S(1)}, f32[1,128]{1,0:T(1,128)S(1)}, u32[]{:S(2)}, u32[]{:S(2)}) collective-permute-start(f32[1,128]{1,0:T(1,128)S(1)} %add_add_fusion.1), channel_id=1, source_target_pairs={{0,2},{1,3},{2,0},{3,1},{4,6},{5,7},{6,4},{7,5},{8,10},{9,11},{10,... | collective-permute-start | bytes 1544 | tf_op jit(solution)/shard_map/ppermute | solution.py:278
  94.8 1.1 collective-permute-start.17
  95.9 18.7 %copy-start.6 = (f32[1,128]{1,0:T(1,128)}, f32[1,128]{1,0:T(1,128)S(1)}, u32[]{:S(2)}) copy-start(f32[1,128]{1,0:T(1,128)S(1)} %add.118.refs_0_) | copy-start | bytes 1540
  95.9 15.8 %collective-permute-start.18 = (f32[1,128]{1,0:T(1,128)S(1)}, f32[1,128]{1,0:T(1,128)S(1)}, u32[]{:S(2)}, u32[]{:S(2)}) collective-permute-start(f32[1,128]{1,0:T(1,128)S(1)} %add.118.refs_0_), channel_id=1, source_target_pairs={{0,32},{4,36},{8,40},{12,44},{16,48},{20,52},{24,56},{28,60},{32,6... | collective-permute-start | bytes 1544 | tf_op jit(solution)/shard_map/ppermute | solution.py:273
  97.7 17.0 %collective-permute-start.19 = (f32[1,128]{1,0:T(1,128)S(1)}, f32[1,128]{1,0:T(1,128)S(1)}, u32[]{:S(2)}, u32[]{:S(2)}) collective-permute-start(f32[1,128]{1,0:T(1,128)S(1)} %add.118.refs_0_), channel_id=1, source_target_pairs={{0,64},{4,68},{8,72},{12,76},{16,80},{20,84},{24,88},{28,92},{32,9... | collective-permute-start | bytes 1544 | tf_op jit(solution)/shard_map/ppermute | solution.py:273
  100.4 14.2 %collective-permute-start.20 = (f32[1,128]{1,0:T(1,128)S(1)}, f32[1,128]{1,0:T(1,128)S(1)}, u32[]{:S(2)}, u32[]{:S(2)}) collective-permute-start(f32[1,128]{1,0:T(1,128)S(1)} %add.118.refs_0_), channel_id=1, source_target_pairs={{0,96},{4,100},{8,104},{12,108},{16,112},{20,116},{24,120},{28,124... | collective-permute-start | bytes 1544 | tf_op jit(solution)/shard_map/ppermute | solution.py:273
  111.7 3.0 %copy-start.7 = (f32[1,128]{1,0:T(1,128)}, f32[1,128]{1,0:T(1,128)S(1)}, u32[]{:S(2)}) copy-start(f32[1,128]{1,0:T(1,128)S(1)} %collective-permute-done.18.refs_1_) | copy-start | bytes 1540
  114.7 0.5 copy-start.8
  115.2 0.5 copy-start.9

commit v5 on v4

--- a/solution.py
+++ b/solution.py
@@ -244,10 +244,10 @@
     own_partial = middle([below, above], own_start)
     their_below_high, their_above_low = up(theirs[END:]), down(theirs[:seq - END])
     far_middle = across(jnp.concatenate([far_low[PASSED:], far_high[:half - PASSED]], axis=0))
+    their_start = start(theirs)
+    crossed, own_partial = ahead(crossed, own_partial)
+    their_far_low, their_far_high = up(crossed[:PASSED]), down(crossed[2 * END - PASSED:])
     own_states, own_reward = finish([far_low, far_high], own_partial, own, jnp.zeros((1, LANES), jnp.float32))
-    their_start = start(theirs)
-    crossed, own_states = ahead(crossed, own_states)
-    their_far_low, their_far_high = up(crossed[:PASSED]), down(crossed[2 * END - PASSED:])
     their_partial = middle([crossed[:END], their_below_high, their_above_low, crossed[END:]], their_start)
     their_states, rewards = finish([their_far_low, far_middle, their_far_high], their_partial, other, own_reward)
 

time: 119 us -> 119 us (level)
  no operation moved by 1% of the time
where the time goes in v5:
time: 119 us; the launch traced here: 118 us
  starting transfers between devices  42.3 us (36%)
  Pallas kernels  34.7 us (29%)
  waiting for transfers between devices  25.6 us (22%)
  local copies, waits for them, and re-layouts  12 us (10%)
  other arithmetic  2.55 us (2%)
    pallas_call x6, Pallas kernels, call(): pl.pallas_call(functools.partial(kernel, depth_steps), grid_spec=pltpu.Pr...  31.2 us
    ppermute x7, waiting for transfers between devices, exchanged(): return [terms] + [lax.ppermute(terms, PLANE, pair) for pair in pairs]  14.3 us
    ppermute x7, starting transfers between devices, exchanged(): return [terms] + [lax.ppermute(terms, PLANE, pair) for pair in pairs]  10.6 us
    unnamed x22, local copies, waits for them, and re-layouts  9.26 us
    ppermute x2, waiting for transfers between devices, body(): below, above = (up(mine), down(mine))  6.41 us
    ppermute x2, starting transfers between devices, body(): below, above = (up(mine), down(mine))  4.27 us
    ppermute x3, starting transfers between devices, body(): lax.ppermute(rewards, 'mp', ring(mp_size, step))  4.23 us
    all_to_all x1, starting transfers between devices, body(): lax.all_to_all(outgoing, PLANE, split_axis=0, concat_axis=0, tiled=True)  4.15 us
  transfers between devices with their start and end apart: 22, of which 9 were waited for; matrix products, arithmetic and copies ran while one was open for 8% of the time, Pallas kernels for 24%

profile of v5, /device:TPU:0, one launch (start us, length us, event | category | flops | bytes accessed | tf_op | source)
XLA Modules:
  0.0 118.1 jit_solution(8012051582480573840)
XLA Ops:
  0.6 2.1 %collective-permute-start = (bf16[256,2048]{1,0:T(8,128)(2,1)}, bf16[256,2048]{1,0:T(8,128)(2,1)S(1)}, u32[]{:S(2)}, u32[]{:S(2)}) collective-permute-start(bf16[256,2048]{1,0:T(8,128)(2,1)} %bitcast.3.refs_0_), channel_id=1, source_target_pairs={{0,1},{1,2},{2,3},{3,0},{4,5},{5,6},{6,7},{7,4},{8,9},{9,10},{10,1... | collective-permute-start | bytes 3145736 | tf_op jit(solution)/shard_map/ppermute | solution.py:180
  2.7 2.2 %collective-permute-start.1 = (bf16[256,2048]{1,0:T(8,128)(2,1)}, bf16[256,2048]{1,0:T(8,128)(2,1)S(1)}, u32[]{:S(2)}, u32[]{:S(2)}) collective-permute-start(bf16[256,2048]{1,0:T(8,128)(2,1)} %bitcast.3.refs_0_), channel_id=1, source_target_pairs={{0,3},{1,0},{2,1},{3,2},{4,7},{5,4},{6,5},{7,6},{8,11},{9,8},{10,9... | collective-permute-start | bytes 3145736 | tf_op jit(solution)/shard_map/ppermute | solution.py:180
  4.9 4.7 %copy.11 = bf16[1024,8,2,128]{3,1,2,0:T(8,128)(2,1)} copy(bf16[1024,8,2,128]{3,2,1,0:T(2,128)(2,1)} %bitcast.31) | data formatting | bytes 8388608
  9.6 3.0 %collective-permute-start.8 = (bf16[256,2048]{1,0:T(8,128)(2,1)}, bf16[256,2048]{1,0:T(8,128)(2,1)S(1)}, u32[]{:S(2)}, u32[]{:S(2)}) collective-permute-start(bf16[256,2048]{1,0:T(8,128)(2,1)} %bitcast.3.refs_0_), channel_id=1, source_target_pairs={{0,64},{4,68},{8,72},{12,76},{16,80},{20,84},{24,88},{28,92},{32,9... | collective-permute-start | bytes 3145736 | tf_op jit(solution)/shard_map/ppermute | solution.py:182
  12.7 0.1 pad_add_fusion.1.refs_0_
  12.7 0.7 fusion.8
  13.4 0.6 fusion.7
  14.0 0.8 pad_add_fusion.places
  14.8 0.8 pad_add_fusion.2.places
  15.5 0.2 convert_reduce_fusion
  15.7 0.1 select_reduce_fusion
  15.8 2.2 %copy-done = bf16[1024,8,2,128]{3,1,2,0:T(8,128)(2,1)S(1)} copy-done((bf16[1024,8,2,128]{3,1,2,0:T(8,128)(2,1)S(1)}, bf16[1024,8,2,128]{3,1,2,0:T(8,128)(2,1)}, u32[]{:S(2)}) %copy-start) | copy-done | bytes 4194328
  18.0 3.8 %shard_map.86.refs_3_ = f32[256,1280]{1,0:T(8,128)S(1)} custom-call(s32[1]{0:T(128)} %bitcast.4.places, bf16[256,2048]{1,0:T(8,128)(2,1)} %bitcast.3.refs_0_, bf16[1,8192,1024]{2,1,0:T(8,128)(2,1)} %refs_4_.3, bf16[8192,256]{1,0:T(8,128)(2,1)S(1)} %bitcast.22), custom_call_target="tpu_custom_call" | custom-call | flops 1342177280 | bytes 5242880 | tf_op jit(solution)/shard_map/pallas_call | solution.py:197
  21.8 6.4 %collective-permute-done.refs_1_ = bf16[256,2048]{1,0:T(8,128)(2,1)S(1)} collective-permute-done((bf16[256,2048]{1,0:T(8,128)(2,1)}, bf16[256,2048]{1,0:T(8,128)(2,1)S(1)}, u32[]{:S(2)}, u32[]{:S(2)}) %collective-permute-start) | collective-permute-done | bytes 1048608 | tf_op jit(solution)/shard_map/ppermute | solution.py:180
  28.3 1.3 %collective-permute-start.2 = (bf16[128,2048]{1,0:T(8,128)(2,1)S(1)}, bf16[128,2048]{1,0:T(8,128)(2,1)S(1)}, u32[]{:S(2)}, u32[]{:S(2)}) collective-permute-start(bf16[128,2048]{1,0:T(8,128)(2,1)S(1)} %slice.36), channel_id=1, source_target_pairs={{0,1},{1,2},{2,3},{3,0},{4,5},{5,6},{6,7},{7,4},{8,9},{9,10},{10,1... | collective-permute-start | bytes 1572872 | tf_op jit(solution)/shard_map/ppermute | solution.py:242
  29.7 2.0 %collective-permute-start.3 = (bf16[128,2048]{1,0:T(8,128)(2,1)S(1)}, bf16[128,2048]{1,0:T(8,128)(2,1)S(1)}, u32[]{:S(2)}, u32[]{:S(2)}) collective-permute-start(bf16[128,2048]{1,0:T(8,128)(2,1)S(1)} %slice.37), channel_id=1, source_target_pairs={{0,3},{1,0},{2,1},{3,2},{4,7},{5,4},{6,5},{7,6},{8,11},{9,8},{10,9... | collective-permute-start | bytes 1572872 | tf_op jit(solution)/shard_map/ppermute | solution.py:242
  31.6 0.1 pad_maximum_fusion
  31.7 3.1 %collective-permute-start.4 = (bf16[160,2048]{1,0:T(8,128)(2,1)S(1)}, bf16[160,2048]{1,0:T(8,128)(2,1)S(1)}, u32[]{:S(2)}, u32[]{:S(2)}) collective-permute-start(bf16[160,2048]{1,0:T(8,128)(2,1)S(1)} %pad_maximum_fusion), channel_id=1, source_target_pairs={{0,64},{4,68},{8,72},{12,76},{16,80},{20,84},{24,88},{28,92},{32,9... | collective-permute-start | bytes 1966088 | tf_op jit(solution)/shard_map/ppermute | solution.py:243
  34.8 2.4 %collective-permute-done.8.refs_0_ = bf16[256,2048]{1,0:T(8,128)(2,1)S(1)} collective-permute-done((bf16[256,2048]{1,0:T(8,128)(2,1)}, bf16[256,2048]{1,0:T(8,128)(2,1)S(1)}, u32[]{:S(2)}, u32[]{:S(2)}) %collective-permute-start.8) | collective-permute-done | bytes 1048608 | tf_op jit(solution)/shard_map/ppermute | solution.py:182
  37.2 0.2 fusion.4
  37.4 0.1 collective-permute-start.9
  37.5 3.2 %collective-permute-start.10 = (bf16[176,2048]{1,0:T(8,128)(2,1)S(1)}, bf16[176,2048]{1,0:T(8,128)(2,1)S(1)}, u32[]{:S(2)}, u32[]{:S(2)}) collective-permute-start(bf16[176,2048]{1,0:T(8,128)(2,1)S(1)} %get-tuple-element.28), channel_id=1, source_target_pairs={{0,3},{1,0},{2,1},{3,2},{4,7},{5,4},{6,5},{7,6},{8,11},{9,8},{10,9... | collective-permute-start | bytes 2162696 | tf_op jit(solution)/shard_map/ppermute | solution.py:245
  40.7 3.5 %shard_map.89.refs_5_ = f32[256,1280]{1,0:T(8,128)S(1)} custom-call(s32[1]{0:T(128)} %bitcast.4.places, bf16[256,2048]{1,0:T(8,128)(2,1)S(1)} %collective-permute-done.8.refs_0_, bf16[1,8192,1024]{2,1,0:T(8,128)(2,1)} %refs_4_.3, bf16[8192,256]{1,0:T(8,128)(2,1)S(1)} %bitcast.23), custom_call_target="tpu_custom_call" | custom-call | flops 1342177280 | bytes 5242880 | tf_op jit(solution)/shard_map/pallas_call | solution.py:197
  44.2 6.0 %shard_map.87.refs_2_ = f32[256,1280]{1,0:T(8,128)S(1)} custom-call(s32[2]{0:T(128)S(1)} %pad_add_fusion.1.refs_0_, bf16[256,2048]{1,0:T(8,128)(2,1)S(1)} %collective-permute-done.refs_1_, bf16[256,2048]{1,0:T(8,128)(2,1)S(1)} %collective-permute-done.1.refs_2_, f32[256,1280]{1,0:T(8,128)S(1)} %shard_map.86.refs_3_, bf16[1,8192,1024]{2,1,0:T(8,128)(2,1)} %refs_4_.3, ...), custom_call_target="tpu_custom_call" | custom-call | flops 2684354560 | bytes 10485760 | tf_op jit(solution)/shard_map/pallas_call | solution.py:197
  50.2 0.0 collective-permute-done.3.refs_1_
  50.2 0.0 collective-permute-done.2.refs_0_
  50.3 0.0 copy-start.2
  50.3 3.1 %collective-permute-start.6 = (bf16[128,2048]{1,0:T(8,128)(2,1)S(1)}, bf16[128,2048]{1,0:T(8,128)(2,1)S(1)}, u32[]{:S(2)}, u32[]{:S(2)}) collective-permute-start(bf16[128,2048]{1,0:T(8,128)(2,1)S(1)} %pad_maximum_fusion.1), channel_id=1, source_target_pairs={{0,64},{4,68},{8,72},{12,76},{16,80},{20,84},{24,88},{28,92},{32,9... | collective-permute-start | bytes 1572872 | tf_op jit(solution)/shard_map/ppermute | solution.py:246
  53.4 0.1 fusion.5
  53.5 0.1 collective-permute-start.5
  53.6 3.2 %collective-permute-start.7 = (bf16[64,2048]{1,0:T(8,128)(2,1)S(1)}, bf16[64,2048]{1,0:T(8,128)(2,1)S(1)}, u32[]{:S(2)}, u32[]{:S(2)}) collective-permute-start(bf16[64,2048]{1,0:T(8,128)(2,1)S(1)} %get-tuple-element.32), channel_id=1, source_target_pairs={{0,3},{1,0},{2,1},{3,2},{4,7},{5,4},{6,5},{7,6},{8,11},{9,8},{10,9... | collective-permute-start | bytes 786440 | tf_op jit(solution)/shard_map/ppermute | solution.py:249
  56.9 6.0 %shard_map.88 = (bf16[256,1024]{1,0:T(8,128)(2,1)S(1)}, f32[1,128]{1,0:T(1,128)S(1)}) custom-call(s32[3]{0:T(128)S(1)} %pad_add_fusion.places, bf16[128,2048]{1,0:T(8,128)(2,1)S(1)} %collective-permute-done.2.refs_0_, bf16[128,2048]{1,0:T(8,128)(2,1)S(1)} %collective-permute-done.3.refs_1_, f32[256,1280]{1,0:T(8,128)S(1)} %shard_map.87.refs_2_, ...), custom_call_target="tpu_custom_call" | custom-call | flops 1342177280 | bytes 5242880 | tf_op jit(solution)/shard_map/pallas_call | solution.py:197
  62.9 0.0 collective-permute-done.10.refs_3_
  62.9 6.0 %shard_map.90.refs_3_ = f32[256,1280]{1,0:T(8,128)S(1)} custom-call(s32[2]{0:T(128)S(1)} %pad_add_fusion.1.refs_0_, bf16[80,2048]{1,0:T(8,128)(2,1)S(1)} %get-tuple-element.31.refs_1_, bf16[176,2048]{1,0:T(8,128)(2,1)S(1)} %collective-permute-done.9.refs_2_, bf16[176,2048]{1,0:T(8,128)(2,1)S(1)} %collective-permute-done.10.refs_3_, ...), custom_call_target="tpu_custom_call" | custom-call | flops 2684354560 | bytes 10485760 | tf_op jit(solution)/shard_map/pallas_call | solution.py:197
  68.9 0.0 collective-permute-done.5.refs_0_
  68.9 0.0 collective-permute-done.6.refs_1_
  68.9 6.0 %shard_map.91 = (bf16[256,1024]{1,0:T(8,128)(2,1)S(1)}, f32[1,128]{1,0:T(1,128)S(1)}) custom-call(s32[3]{0:T(128)S(1)} %pad_add_fusion.2.places, bf16[64,2048]{1,0:T(8,128)(2,1)S(1)} %collective-permute-done.5.refs_0_, bf16[128,2048]{1,0:T(8,128)(2,1)S(1)} %collective-permute-done.6.refs_1_, bf16[64,2048]{1,0:T(8,128)(2,1)S(1)} %collective-permute-done.7.refs_2_, ...), custom_call_target="tpu_custom_call" | custom-call | flops 1342177280 | bytes 5242880 | tf_op jit(solution)/shard_map/pallas_call | solution.py:197
  74.9 3.0 %collective-permute-start.13 = (f32[1,128]{1,0:T(1,128)S(1)}, f32[1,128]{1,0:T(1,128)S(1)}, u32[]{:S(2)}, u32[]{:S(2)}) collective-permute-start(f32[1,128]{1,0:T(1,128)S(1)} %get-tuple-element.25), channel_id=1, source_target_pairs={{0,24},{4,28},{8,0},{12,4},{16,8},{20,12},{24,16},{28,20},{32,56},... | collective-permute-start | bytes 1544 | tf_op jit(solution)/shard_map/ppermute | solution.py:273
  77.9 0.6 collective-permute-start.12
  78.5 1.0 collective-permute-start.11
  79.5 2.2 %shard_map.92 = bf16[32,2,16,1024]{3,2,1,0:T(8,128)(2,1)} custom-call(s32[64]{0:T(128)S(1)} %broadcast_add_fusion.slots, bf16[256,1024]{1,0:T(8,128)(2,1)S(1)} %get-tuple-element.20.first, bf16[256,1024]{1,0:T(8,128)(2,1)S(1)} %get-tuple-element.24.second), custom_call_target="tpu_custom_call" | custom-call | bytes 1572864 | tf_op jit(solution)/shard_map/pallas_call | solution.py:255
  81.8 0.0 collective-permute-done.13
  81.8 1.2 %collective-permute-done.12 = f32[1,128]{1,0:T(1,128)S(1)} collective-permute-done((f32[1,128]{1,0:T(1,128)S(1)}, f32[1,128]{1,0:T(1,128)S(1)}, u32[]{:S(2)}, u32[]{:S(2)}) %collective-permute-start.12) | collective-permute-done | bytes 544 | tf_op jit(solution)/shard_map/ppermute | solution.py:273
  83.0 0.3 collective-permute-done.11
  83.3 4.1 %all-to-all-start = ((bf16[32,2,16,1024]{3,2,1,0:T(8,128)(2,1)}), bf16[32,2,16,1024]{3,2,1,0:T(8,128)(2,1)S(1)}, u32[]{:S(2)}, u32[]{:S(2)}) async-start(bf16[32,2,16,1024]{3,2,1,0:T(8,128)(2,1)} %shard_map.92), calls=%async_computation | async-start | bytes 4194304 | tf_op jit(solution)/shard_map/all_to_all | solution.py:277
  87.5 2.2 %collective-permute-start.16 = (f32[1,128]{1,0:T(1,128)S(1)}, f32[1,128]{1,0:T(1,128)S(1)}, u32[]{:S(2)}, u32[]{:S(2)}) collective-permute-start(f32[1,128]{1,0:T(1,128)S(1)} %add_add_fusion.1), channel_id=1, source_target_pairs={{0,3},{1,0},{2,1},{3,2},{4,7},{5,4},{6,5},{7,6},{8,11},{9,8},{10,9... | collective-permute-start | bytes 1544 | tf_op jit(solution)/shard_map/ppermute | solution.py:278
  89.6 2.1 %collective-permute-start.15 = (f32[1,128]{1,0:T(1,128)S(1)}, f32[1,128]{1,0:T(1,128)S(1)}, u32[]{:S(2)}, u32[]{:S(2)}) collective-permute-start(f32[1,128]{1,0:T(1,128)S(1)} %add_add_fusion.1), channel_id=1, source_target_pairs={{0,2},{1,3},{2,0},{3,1},{4,6},{5,7},{6,4},{7,5},{8,10},{9,11},{10,... | collective-permute-start | bytes 1544 | tf_op jit(solution)/shard_map/ppermute | solution.py:278
  91.7 0.6 dynamic_slice.19
  92.3 2.1 %collective-permute-done.14 = f32[1,128]{1,0:T(1,128)S(1)} collective-permute-done((f32[1,128]{1,0:T(1,128)S(1)}, f32[1,128]{1,0:T(1,128)S(1)}, u32[]{:S(2)}, u32[]{:S(2)}) %collective-permute-start.14) | collective-permute-done | bytes 544 | tf_op jit(solution)/shard_map/ppermute | solution.py:278
  94.4 0.3 collective-permute-done.15
  94.7 0.0 collective-permute-start.17
  94.7 0.6 fusion.1
  95.2 0.5 collective-permute-done.17
  95.8 1.8 %collective-permute-start.18 = (f32[1,128]{1,0:T(1,128)S(1)}, f32[1,128]{1,0:T(1,128)S(1)}, u32[]{:S(2)}, u32[]{:S(2)}) collective-permute-start(f32[1,128]{1,0:T(1,128)S(1)} %add.118.refs_0_), channel_id=1, source_target_pairs={{0,32},{4,36},{8,40},{12,44},{16,48},{20,52},{24,56},{28,60},{32,6... | collective-permute-start | bytes 1544 | tf_op jit(solution)/shard_map/ppermute | solution.py:273
  97.6 2.7 %collective-permute-start.19 = (f32[1,128]{1,0:T(1,128)S(1)}, f32[1,128]{1,0:T(1,128)S(1)}, u32[]{:S(2)}, u32[]{:S(2)}) collective-permute-start(f32[1,128]{1,0:T(1,128)S(1)} %add.118.refs_0_), channel_id=1, source_target_pairs={{0,64},{4,68},{8,72},{12,76},{16,80},{20,84},{24,88},{28,92},{32,9... | collective-permute-start | bytes 1544 | tf_op jit(solution)/shard_map/ppermute | solution.py:273
  100.3 1.4 %collective-permute-start.20 = (f32[1,128]{1,0:T(1,128)S(1)}, f32[1,128]{1,0:T(1,128)S(1)}, u32[]{:S(2)}, u32[]{:S(2)}) collective-permute-start(f32[1,128]{1,0:T(1,128)S(1)} %add.118.refs_0_), channel_id=1, source_target_pairs={{0,96},{4,100},{8,104},{12,108},{16,112},{20,116},{24,120},{28,124... | collective-permute-start | bytes 1544 | tf_op jit(solution)/shard_map/ppermute | solution.py:273
  101.7 0.5 pad_bitcast_fusion.shares
  102.2 9.3 %collective-permute-done.18.refs_1_ = f32[1,128]{1,0:T(1,128)S(1)} collective-permute-done((f32[1,128]{1,0:T(1,128)S(1)}, f32[1,128]{1,0:T(1,128)S(1)}, u32[]{:S(2)}, u32[]{:S(2)}) %collective-permute-start.18) | collective-permute-done | bytes 544 | tf_op jit(solution)/shard_map/ppermute | solution.py:273
  111.5 3.0 %collective-permute-done.19.refs_2_ = f32[1,128]{1,0:T(1,128)S(1)} collective-permute-done((f32[1,128]{1,0:T(1,128)S(1)}, f32[1,128]{1,0:T(1,128)S(1)}, u32[]{:S(2)}, u32[]{:S(2)}) %collective-permute-start.19) | collective-permute-done | bytes 544 | tf_op jit(solution)/shard_map/ppermute | solution.py:273
  114.5 0.5 copy-done.8
  115.0 0.5 copy-done.9
  115.5 1.3 %shard_map.93 = f32[1,1]{1,0:T(1,128)} custom-call(f32[1,128]{1,0:T(1,128)} %pad_bitcast_fusion.shares, f32[1,128]{1,0:T(1,128)} %copy-done.6, f32[1,128]{1,0:T(1,128)} %copy-done.7, f32[1,128]{1,0:T(1,128)} %copy-done.8, f32[1,128]{1,0:T(1,128)} %copy-done.9), custom_call_target="tpu_custom_call" | custom-call | tf_op jit(solution)/shard_map/pallas_call | solution.py:281
  116.8 0.0 all-to-all-done
  116.8 1.3 %copy.13 = bf16[1,32,2,16,1024]{4,3,2,1,0:T(8,128)(2,1)} copy(bf16[1,32,2,16,1024]{4,3,2,1,0:T(8,128)(2,1)S(1)} %bitcast.30) | data formatting | bytes 4194304
  (38 shorter events, 0.3 us)
Async XLA Ops:
  0.6 27.6 %collective-permute-start = (bf16[256,2048]{1,0:T(8,128)(2,1)}, bf16[256,2048]{1,0:T(8,128)(2,1)S(1)}, u32[]{:S(2)}, u32[]{:S(2)}) collective-permute-start(bf16[256,2048]{1,0:T(8,128)(2,1)} %bitcast.3.refs_0_), channel_id=1, source_target_pairs={{0,1},{1,2},{2,3},{3,0},{4,5},{5,6},{6,7},{7,4},{8,9},{9,10},{10,1... | collective-permute-start | bytes 3145736 | tf_op jit(solution)/shard_map/ppermute | solution.py:180
  2.7 25.5 %collective-permute-start.1 = (bf16[256,2048]{1,0:T(8,128)(2,1)}, bf16[256,2048]{1,0:T(8,128)(2,1)S(1)}, u32[]{:S(2)}, u32[]{:S(2)}) collective-permute-start(bf16[256,2048]{1,0:T(8,128)(2,1)} %bitcast.3.refs_0_), channel_id=1, source_target_pairs={{0,3},{1,0},{2,1},{3,2},{4,7},{5,4},{6,5},{7,6},{8,11},{9,8},{10,9... | collective-permute-start | bytes 3145736 | tf_op jit(solution)/shard_map/ppermute | solution.py:180
  4.9 7.8 %copy-start.3 = (s32[32]{0:T(128)S(1)}, s32[32]{0:T(128)}, u32[]{:S(2)}) copy-start(s32[32]{0:T(128)} %param.11) | copy-start | bytes 388
  4.9 10.6 %copy-start.4 = (s32[32,1]{0,1:T(1,128)S(1)}, s32[32,1]{0,1:T(1,128)}, u32[]{:S(2)}) copy-start(s32[32,1]{0,1:T(1,128)} %param.13) | copy-start | bytes 388
  9.6 27.6 %collective-permute-start.8 = (bf16[256,2048]{1,0:T(8,128)(2,1)}, bf16[256,2048]{1,0:T(8,128)(2,1)S(1)}, u32[]{:S(2)}, u32[]{:S(2)}) collective-permute-start(bf16[256,2048]{1,0:T(8,128)(2,1)} %bitcast.3.refs_0_), channel_id=1, source_target_pairs={{0,64},{4,68},{8,72},{12,76},{16,80},{20,84},{24,88},{28,92},{32,9... | collective-permute-start | bytes 3145736 | tf_op jit(solution)/shard_map/ppermute | solution.py:182
  15.8 2.2 %copy-start = (bf16[1024,8,2,128]{3,1,2,0:T(8,128)(2,1)S(1)}, bf16[1024,8,2,128]{3,1,2,0:T(8,128)(2,1)}, u32[]{:S(2)}) copy-start(bf16[1024,8,2,128]{3,1,2,0:T(8,128)(2,1)} %copy.11) | copy-start | bytes 12582916
  28.3 21.9 %collective-permute-start.2 = (bf16[128,2048]{1,0:T(8,128)(2,1)S(1)}, bf16[128,2048]{1,0:T(8,128)(2,1)S(1)}, u32[]{:S(2)}, u32[]{:S(2)}) collective-permute-start(bf16[128,2048]{1,0:T(8,128)(2,1)S(1)} %slice.36), channel_id=1, source_target_pairs={{0,1},{1,2},{2,3},{3,0},{4,5},{5,6},{6,7},{7,4},{8,9},{9,10},{10,1... | collective-permute-start | bytes 1572872 | tf_op jit(solution)/shard_map/ppermute | solution.py:242
  29.7 20.5 %collective-permute-start.3 = (bf16[128,2048]{1,0:T(8,128)(2,1)S(1)}, bf16[128,2048]{1,0:T(8,128)(2,1)S(1)}, u32[]{:S(2)}, u32[]{:S(2)}) collective-permute-start(bf16[128,2048]{1,0:T(8,128)(2,1)S(1)} %slice.37), channel_id=1, source_target_pairs={{0,3},{1,0},{2,1},{3,2},{4,7},{5,4},{6,5},{7,6},{8,11},{9,8},{10,9... | collective-permute-start | bytes 1572872 | tf_op jit(solution)/shard_map/ppermute | solution.py:242
  31.6 9.1 %copy-start.1 = (bf16[1024,8,2,128]{3,1,2,0:T(8,128)(2,1)S(1)}, bf16[1024,8,2,128]{3,1,2,0:T(8,128)(2,1)}, u32[]{:S(2)}) copy-start(bf16[1024,8,2,128]{3,1,2,0:T(8,128)(2,1)} %copy.11) | copy-start | bytes 12582916
  31.7 21.7 %collective-permute-start.4 = (bf16[160,2048]{1,0:T(8,128)(2,1)S(1)}, bf16[160,2048]{1,0:T(8,128)(2,1)S(1)}, u32[]{:S(2)}, u32[]{:S(2)}) collective-permute-start(bf16[160,2048]{1,0:T(8,128)(2,1)S(1)} %pad_maximum_fusion), channel_id=1, source_target_pairs={{0,64},{4,68},{8,72},{12,76},{16,80},{20,84},{24,88},{28,92},{32,9... | collective-permute-start | bytes 1966088 | tf_op jit(solution)/shard_map/ppermute | solution.py:243
  37.4 25.5 %collective-permute-start.9 = (bf16[176,2048]{1,0:T(8,128)(2,1)S(1)}, bf16[176,2048]{1,0:T(8,128)(2,1)S(1)}, u32[]{:S(2)}, u32[]{:S(2)}) collective-permute-start(bf16[176,2048]{1,0:T(8,128)(2,1)S(1)} %get-tuple-element.29), channel_id=1, source_target_pairs={{0,1},{1,2},{2,3},{3,0},{4,5},{5,6},{6,7},{7,4},{8,9},{9,10},{10,1... | collective-permute-start | bytes 2162696 | tf_op jit(solution)/shard_map/ppermute | solution.py:245
  37.5 25.4 %collective-permute-start.10 = (bf16[176,2048]{1,0:T(8,128)(2,1)S(1)}, bf16[176,2048]{1,0:T(8,128)(2,1)S(1)}, u32[]{:S(2)}, u32[]{:S(2)}) collective-permute-start(bf16[176,2048]{1,0:T(8,128)(2,1)S(1)} %get-tuple-element.28), channel_id=1, source_target_pairs={{0,3},{1,0},{2,1},{3,2},{4,7},{5,4},{6,5},{7,6},{8,11},{9,8},{10,9... | collective-permute-start | bytes 2162696 | tf_op jit(solution)/shard_map/ppermute | solution.py:245
  50.3 6.5 %copy-start.2 = (f32[1024]{0:T(1024)S(1)}, f32[1024]{0:T(1024)}, u32[]{:S(2)}) copy-start(f32[1024]{0:T(1024)} %param.10) | copy-start | bytes 12292
  50.3 18.6 %collective-permute-start.6 = (bf16[128,2048]{1,0:T(8,128)(2,1)S(1)}, bf16[128,2048]{1,0:T(8,128)(2,1)S(1)}, u32[]{:S(2)}, u32[]{:S(2)}) collective-permute-start(bf16[128,2048]{1,0:T(8,128)(2,1)S(1)} %pad_maximum_fusion.1), channel_id=1, source_target_pairs={{0,64},{4,68},{8,72},{12,76},{16,80},{20,84},{24,88},{28,92},{32,9... | collective-permute-start | bytes 1572872 | tf_op jit(solution)/shard_map/ppermute | solution.py:246
  53.5 15.3 %collective-permute-start.5 = (bf16[64,2048]{1,0:T(8,128)(2,1)S(1)}, bf16[64,2048]{1,0:T(8,128)(2,1)S(1)}, u32[]{:S(2)}, u32[]{:S(2)}) collective-permute-start(bf16[64,2048]{1,0:T(8,128)(2,1)S(1)} %get-tuple-element.33), channel_id=1, source_target_pairs={{0,1},{1,2},{2,3},{3,0},{4,5},{5,6},{6,7},{7,4},{8,9},{9,10},{10,1... | collective-permute-start | bytes 786440 | tf_op jit(solution)/shard_map/ppermute | solution.py:249
  53.6 15.2 %collective-permute-start.7 = (bf16[64,2048]{1,0:T(8,128)(2,1)S(1)}, bf16[64,2048]{1,0:T(8,128)(2,1)S(1)}, u32[]{:S(2)}, u32[]{:S(2)}) collective-permute-start(bf16[64,2048]{1,0:T(8,128)(2,1)S(1)} %get-tuple-element.32), channel_id=1, source_target_pairs={{0,3},{1,0},{2,1},{3,2},{4,7},{5,4},{6,5},{7,6},{8,11},{9,8},{10,9... | collective-permute-start | bytes 786440 | tf_op jit(solution)/shard_map/ppermute | solution.py:249
  74.9 6.9 %collective-permute-start.13 = (f32[1,128]{1,0:T(1,128)S(1)}, f32[1,128]{1,0:T(1,128)S(1)}, u32[]{:S(2)}, u32[]{:S(2)}) collective-permute-start(f32[1,128]{1,0:T(1,128)S(1)} %get-tuple-element.25), channel_id=1, source_target_pairs={{0,24},{4,28},{8,0},{12,4},{16,8},{20,12},{24,16},{28,20},{32,56},... | collective-permute-start | bytes 1544 | tf_op jit(solution)/shard_map/ppermute | solution.py:273
  77.9 5.0 %collective-permute-start.12 = (f32[1,128]{1,0:T(1,128)S(1)}, f32[1,128]{1,0:T(1,128)S(1)}, u32[]{:S(2)}, u32[]{:S(2)}) collective-permute-start(f32[1,128]{1,0:T(1,128)S(1)} %get-tuple-element.25), channel_id=1, source_target_pairs={{0,16},{4,20},{8,24},{12,28},{16,0},{20,4},{24,8},{28,12},{32,48},... | collective-permute-start | bytes 1544 | tf_op jit(solution)/shard_map/ppermute | solution.py:273
  78.5 4.8 %collective-permute-start.11 = (f32[1,128]{1,0:T(1,128)S(1)}, f32[1,128]{1,0:T(1,128)S(1)}, u32[]{:S(2)}, u32[]{:S(2)}) collective-permute-start(f32[1,128]{1,0:T(1,128)S(1)} %get-tuple-element.25), channel_id=1, source_target_pairs={{0,8},{4,12},{8,16},{12,20},{16,24},{20,28},{24,0},{28,4},{32,40},... | collective-permute-start | bytes 1544 | tf_op jit(solution)/shard_map/ppermute | solution.py:273
  83.3 8.4 %copy-start.5 = (s32[32]{0:T(128)S(1)}, s32[32]{0:T(128)}, u32[]{:S(2)}) copy-start(s32[32]{0:T(128)} %param.12) | copy-start | bytes 388
  83.3 33.4 %all-to-all-start = ((bf16[32,2,16,1024]{3,2,1,0:T(8,128)(2,1)}), bf16[32,2,16,1024]{3,2,1,0:T(8,128)(2,1)S(1)}, u32[]{:S(2)}, u32[]{:S(2)}) async-start(bf16[32,2,16,1024]{3,2,1,0:T(8,128)(2,1)} %shard_map.92), calls=%async_computation | async-start | bytes 4194304 | tf_op jit(solution)/shard_map/all_to_all | solution.py:277
  87.5 4.8 %collective-permute-start.16 = (f32[1,128]{1,0:T(1,128)S(1)}, f32[1,128]{1,0:T(1,128)S(1)}, u32[]{:S(2)}, u32[]{:S(2)}) collective-permute-start(f32[1,128]{1,0:T(1,128)S(1)} %add_add_fusion.1), channel_id=1, source_target_pairs={{0,3},{1,0},{2,1},{3,2},{4,7},{5,4},{6,5},{7,6},{8,11},{9,8},{10,9... | collective-permute-start | bytes 1544 | tf_op jit(solution)/shard_map/ppermute | solution.py:278
  89.6 4.8 %collective-permute-start.14 = (f32[1,128]{1,0:T(1,128)S(1)}, f32[1,128]{1,0:T(1,128)S(1)}, u32[]{:S(2)}, u32[]{:S(2)}) collective-permute-start(f32[1,128]{1,0:T(1,128)S(1)} %add_add_fusion.1), channel_id=1, source_target_pairs={{0,1},{1,2},{2,3},{3,0},{4,5},{5,6},{6,7},{7,4},{8,9},{9,10},{10,1... | collective-permute-start | bytes 1544 | tf_op jit(solution)/shard_map/ppermute | solution.py:278
  89.6 5.0 %collective-permute-start.15 = (f32[1,128]{1,0:T(1,128)S(1)}, f32[1,128]{1,0:T(1,128)S(1)}, u32[]{:S(2)}, u32[]{:S(2)}) collective-permute-start(f32[1,128]{1,0:T(1,128)S(1)} %add_add_fusion.1), channel_id=1, source_target_pairs={{0,2},{1,3},{2,0},{3,1},{4,6},{5,7},{6,4},{7,5},{8,10},{9,11},{10,... | collective-permute-start | bytes 1544 | tf_op jit(solution)/shard_map/ppermute | solution.py:278
  94.7 1.1 collective-permute-start.17
  95.8 18.7 %copy-start.6 = (f32[1,128]{1,0:T(1,128)}, f32[1,128]{1,0:T(1,128)S(1)}, u32[]{:S(2)}) copy-start(f32[1,128]{1,0:T(1,128)S(1)} %add.118.refs_0_) | copy-start | bytes 1540
  95.8 15.7 %collective-permute-start.18 = (f32[1,128]{1,0:T(1,128)S(1)}, f32[1,128]{1,0:T(1,128)S(1)}, u32[]{:S(2)}, u32[]{:S(2)}) collective-permute-start(f32[1,128]{1,0:T(1,128)S(1)} %add.118.refs_0_), channel_id=1, source_target_pairs={{0,32},{4,36},{8,40},{12,44},{16,48},{20,52},{24,56},{28,60},{32,6... | collective-permute-start | bytes 1544 | tf_op jit(solution)/shard_map/ppermute | solution.py:273
  97.6 16.9 %collective-permute-start.19 = (f32[1,128]{1,0:T(1,128)S(1)}, f32[1,128]{1,0:T(1,128)S(1)}, u32[]{:S(2)}, u32[]{:S(2)}) collective-permute-start(f32[1,128]{1,0:T(1,128)S(1)} %add.118.refs_0_), channel_id=1, source_target_pairs={{0,64},{4,68},{8,72},{12,76},{16,80},{20,84},{24,88},{28,92},{32,9... | collective-permute-start | bytes 1544 | tf_op jit(solution)/shard_map/ppermute | solution.py:273
  100.3 14.2 %collective-permute-start.20 = (f32[1,128]{1,0:T(1,128)S(1)}, f32[1,128]{1,0:T(1,128)S(1)}, u32[]{:S(2)}, u32[]{:S(2)}) collective-permute-start(f32[1,128]{1,0:T(1,128)S(1)} %add.118.refs_0_), channel_id=1, source_target_pairs={{0,96},{4,100},{8,104},{12,108},{16,112},{20,116},{24,120},{28,124... | collective-permute-start | bytes 1544 | tf_op jit(solution)/shard_map/ppermute | solution.py:273
  111.5 3.0 %copy-start.7 = (f32[1,128]{1,0:T(1,128)}, f32[1,128]{1,0:T(1,128)S(1)}, u32[]{:S(2)}) copy-start(f32[1,128]{1,0:T(1,128)S(1)} %collective-permute-done.18.refs_1_) | copy-start | bytes 1540
  114.5 0.5 copy-start.8
  115.0 0.5 copy-start.9

commit v6 on v5

--- a/solution.py
+++ b/solution.py
@@ -18,7 +18,7 @@
 END = 80
 PASSED = 64
 PLANE = ("section", "dp")
-VMEM_LIMIT = 32 * 1024 * 1024
+VMEM_LIMIT = 40 * 1024 * 1024
 
 
 def x_opposite(sections, dp_size):

time: 119 us -> 119 us (level)
  no operation moved by 1% of the time
where the time goes in v6:
time: 119 us; the launch traced here: 118 us
  starting transfers between devices  42.3 us (36%)
  Pallas kernels  34.7 us (29%)
  waiting for transfers between devices  25.6 us (22%)
  local copies, waits for them, and re-layouts  12 us (10%)
  other arithmetic  2.55 us (2%)
    pallas_call x6, Pallas kernels, call(): pl.pallas_call(functools.partial(kernel, depth_steps), grid_spec=pltpu.Pr...  31.2 us
    ppermute x7, waiting for transfers between devices, exchanged(): return [terms] + [lax.ppermute(terms, PLANE, pair) for pair in pairs]  14.3 us
    ppermute x7, starting transfers between devices, exchanged(): return [terms] + [lax.ppermute(terms, PLANE, pair) for pair in pairs]  10.6 us
    unnamed x22, local copies, waits for them, and re-layouts  9.26 us
    ppermute x2, waiting for transfers between devices, body(): below, above = (up(mine), down(mine))  6.41 us
    ppermute x2, starting transfers between devices, body(): below, above = (up(mine), down(mine))  4.27 us
    ppermute x3, starting transfers between devices, body(): lax.ppermute(rewards, 'mp', ring(mp_size, step))  4.23 us
    all_to_all x1, starting transfers between devices, body(): lax.all_to_all(outgoing, PLANE, split_axis=0, concat_axis=0, tiled=True)  4.15 us
  transfers between devices with their start and end apart: 22, of which 9 were waited for; matrix products, arithmetic and copies ran while one was open for 8% of the time, Pallas kernels for 24%

profile of v6, /device:TPU:0, one launch (start us, length us, event | category | flops | bytes accessed | tf_op | source)
XLA Modules:
  0.0 118.1 jit_solution(7385934488817899413)
XLA Ops:
  0.6 2.1 %collective-permute-start = (bf16[256,2048]{1,0:T(8,128)(2,1)}, bf16[256,2048]{1,0:T(8,128)(2,1)S(1)}, u32[]{:S(2)}, u32[]{:S(2)}) collective-permute-start(bf16[256,2048]{1,0:T(8,128)(2,1)} %bitcast.3.refs_0_), channel_id=1, source_target_pairs={{0,1},{1,2},{2,3},{3,0},{4,5},{5,6},{6,7},{7,4},{8,9},{9,10},{10,1... | collective-permute-start | bytes 3145736 | tf_op jit(solution)/shard_map/ppermute | solution.py:180
  2.7 2.2 %collective-permute-start.1 = (bf16[256,2048]{1,0:T(8,128)(2,1)}, bf16[256,2048]{1,0:T(8,128)(2,1)S(1)}, u32[]{:S(2)}, u32[]{:S(2)}) collective-permute-start(bf16[256,2048]{1,0:T(8,128)(2,1)} %bitcast.3.refs_0_), channel_id=1, source_target_pairs={{0,3},{1,0},{2,1},{3,2},{4,7},{5,4},{6,5},{7,6},{8,11},{9,8},{10,9... | collective-permute-start | bytes 3145736 | tf_op jit(solution)/shard_map/ppermute | solution.py:180
  4.9 4.7 %copy.11 = bf16[1024,8,2,128]{3,1,2,0:T(8,128)(2,1)} copy(bf16[1024,8,2,128]{3,2,1,0:T(2,128)(2,1)} %bitcast.31) | data formatting | bytes 8388608
  9.6 3.0 %collective-permute-start.8 = (bf16[256,2048]{1,0:T(8,128)(2,1)}, bf16[256,2048]{1,0:T(8,128)(2,1)S(1)}, u32[]{:S(2)}, u32[]{:S(2)}) collective-permute-start(bf16[256,2048]{1,0:T(8,128)(2,1)} %bitcast.3.refs_0_), channel_id=1, source_target_pairs={{0,64},{4,68},{8,72},{12,76},{16,80},{20,84},{24,88},{28,92},{32,9... | collective-permute-start | bytes 3145736 | tf_op jit(solution)/shard_map/ppermute | solution.py:182
  12.7 0.1 pad_add_fusion.1.refs_0_
  12.7 0.7 fusion.8
  13.4 0.6 fusion.7
  14.0 0.8 pad_add_fusion.places
  14.8 0.8 pad_add_fusion.2.places
  15.5 0.2 convert_reduce_fusion
  15.7 0.1 select_reduce_fusion
  15.8 2.2 %copy-done = bf16[1024,8,2,128]{3,1,2,0:T(8,128)(2,1)S(1)} copy-done((bf16[1024,8,2,128]{3,1,2,0:T(8,128)(2,1)S(1)}, bf16[1024,8,2,128]{3,1,2,0:T(8,128)(2,1)}, u32[]{:S(2)}) %copy-start) | copy-done | bytes 4194328
  18.0 3.8 %shard_map.86.refs_3_ = f32[256,1280]{1,0:T(8,128)S(1)} custom-call(s32[1]{0:T(128)} %bitcast.4.places, bf16[256,2048]{1,0:T(8,128)(2,1)} %bitcast.3.refs_0_, bf16[1,8192,1024]{2,1,0:T(8,128)(2,1)} %refs_4_.3, bf16[8192,256]{1,0:T(8,128)(2,1)S(1)} %bitcast.22), custom_call_target="tpu_custom_call" | custom-call | flops 1342177280 | bytes 5242880 | tf_op jit(solution)/shard_map/pallas_call | solution.py:197
  21.8 6.4 %collective-permute-done.refs_1_ = bf16[256,2048]{1,0:T(8,128)(2,1)S(1)} collective-permute-done((bf16[256,2048]{1,0:T(8,128)(2,1)}, bf16[256,2048]{1,0:T(8,128)(2,1)S(1)}, u32[]{:S(2)}, u32[]{:S(2)}) %collective-permute-start) | collective-permute-done | bytes 1048608 | tf_op jit(solution)/shard_map/ppermute | solution.py:180
  28.3 1.3 %collective-permute-start.2 = (bf16[128,2048]{1,0:T(8,128)(2,1)S(1)}, bf16[128,2048]{1,0:T(8,128)(2,1)S(1)}, u32[]{:S(2)}, u32[]{:S(2)}) collective-permute-start(bf16[128,2048]{1,0:T(8,128)(2,1)S(1)} %slice.36), channel_id=1, source_target_pairs={{0,1},{1,2},{2,3},{3,0},{4,5},{5,6},{6,7},{7,4},{8,9},{9,10},{10,1... | collective-permute-start | bytes 1572872 | tf_op jit(solution)/shard_map/ppermute | solution.py:242
  29.7 2.0 %collective-permute-start.3 = (bf16[128,2048]{1,0:T(8,128)(2,1)S(1)}, bf16[128,2048]{1,0:T(8,128)(2,1)S(1)}, u32[]{:S(2)}, u32[]{:S(2)}) collective-permute-start(bf16[128,2048]{1,0:T(8,128)(2,1)S(1)} %slice.37), channel_id=1, source_target_pairs={{0,3},{1,0},{2,1},{3,2},{4,7},{5,4},{6,5},{7,6},{8,11},{9,8},{10,9... | collective-permute-start | bytes 1572872 | tf_op jit(solution)/shard_map/ppermute | solution.py:242
  31.6 0.1 pad_maximum_fusion
  31.7 3.1 %collective-permute-start.4 = (bf16[160,2048]{1,0:T(8,128)(2,1)S(1)}, bf16[160,2048]{1,0:T(8,128)(2,1)S(1)}, u32[]{:S(2)}, u32[]{:S(2)}) collective-permute-start(bf16[160,2048]{1,0:T(8,128)(2,1)S(1)} %pad_maximum_fusion), channel_id=1, source_target_pairs={{0,64},{4,68},{8,72},{12,76},{16,80},{20,84},{24,88},{28,92},{32,9... | collective-permute-start | bytes 1966088 | tf_op jit(solution)/shard_map/ppermute | solution.py:243
  34.8 2.4 %collective-permute-done.8.refs_0_ = bf16[256,2048]{1,0:T(8,128)(2,1)S(1)} collective-permute-done((bf16[256,2048]{1,0:T(8,128)(2,1)}, bf16[256,2048]{1,0:T(8,128)(2,1)S(1)}, u32[]{:S(2)}, u32[]{:S(2)}) %collective-permute-start.8) | collective-permute-done | bytes 1048608 | tf_op jit(solution)/shard_map/ppermute | solution.py:182
  37.2 0.2 fusion.4
  37.4 0.1 collective-permute-start.9
  37.5 3.2 %collective-permute-start.10 = (bf16[176,2048]{1,0:T(8,128)(2,1)S(1)}, bf16[176,2048]{1,0:T(8,128)(2,1)S(1)}, u32[]{:S(2)}, u32[]{:S(2)}) collective-permute-start(bf16[176,2048]{1,0:T(8,128)(2,1)S(1)} %get-tuple-element.28), channel_id=1, source_target_pairs={{0,3},{1,0},{2,1},{3,2},{4,7},{5,4},{6,5},{7,6},{8,11},{9,8},{10,9... | collective-permute-start | bytes 2162696 | tf_op jit(solution)/shard_map/ppermute | solution.py:245
  40.7 3.5 %shard_map.89.refs_5_ = f32[256,1280]{1,0:T(8,128)S(1)} custom-call(s32[1]{0:T(128)} %bitcast.4.places, bf16[256,2048]{1,0:T(8,128)(2,1)S(1)} %collective-permute-done.8.refs_0_, bf16[1,8192,1024]{2,1,0:T(8,128)(2,1)} %refs_4_.3, bf16[8192,256]{1,0:T(8,128)(2,1)S(1)} %bitcast.23), custom_call_target="tpu_custom_call" | custom-call | flops 1342177280 | bytes 5242880 | tf_op jit(solution)/shard_map/pallas_call | solution.py:197
  44.2 6.0 %shard_map.87.refs_2_ = f32[256,1280]{1,0:T(8,128)S(1)} custom-call(s32[2]{0:T(128)S(1)} %pad_add_fusion.1.refs_0_, bf16[256,2048]{1,0:T(8,128)(2,1)S(1)} %collective-permute-done.refs_1_, bf16[256,2048]{1,0:T(8,128)(2,1)S(1)} %collective-permute-done.1.refs_2_, f32[256,1280]{1,0:T(8,128)S(1)} %shard_map.86.refs_3_, bf16[1,8192,1024]{2,1,0:T(8,128)(2,1)} %refs_4_.3, ...), custom_call_target="tpu_custom_call" | custom-call | flops 2684354560 | bytes 10485760 | tf_op jit(solution)/shard_map/pallas_call | solution.py:197
  50.2 0.0 collective-permute-done.3.refs_1_
  50.2 0.0 collective-permute-done.2.refs_0_
  50.3 0.0 copy-start.2
  50.3 3.1 %collective-permute-start.6 = (bf16[128,2048]{1,0:T(8,128)(2,1)S(1)}, bf16[128,2048]{1,0:T(8,128)(2,1)S(1)}, u32[]{:S(2)}, u32[]{:S(2)}) collective-permute-start(bf16[128,2048]{1,0:T(8,128)(2,1)S(1)} %pad_maximum_fusion.1), channel_id=1, source_target_pairs={{0,64},{4,68},{8,72},{12,76},{16,80},{20,84},{24,88},{28,92},{32,9... | collective-permute-start | bytes 1572872 | tf_op jit(solution)/shard_map/ppermute | solution.py:246
  53.4 0.1 fusion.5
  53.5 0.1 collective-permute-start.5
  53.6 3.2 %collective-permute-start.7 = (bf16[64,2048]{1,0:T(8,128)(2,1)S(1)}, bf16[64,2048]{1,0:T(8,128)(2,1)S(1)}, u32[]{:S(2)}, u32[]{:S(2)}) collective-permute-start(bf16[64,2048]{1,0:T(8,128)(2,1)S(1)} %get-tuple-element.32), channel_id=1, source_target_pairs={{0,3},{1,0},{2,1},{3,2},{4,7},{5,4},{6,5},{7,6},{8,11},{9,8},{10,9... | collective-permute-start | bytes 786440 | tf_op jit(solution)/shard_map/ppermute | solution.py:249
  56.9 6.0 %shard_map.88 = (bf16[256,1024]{1,0:T(8,128)(2,1)S(1)}, f32[1,128]{1,0:T(1,128)S(1)}) custom-call(s32[3]{0:T(128)S(1)} %pad_add_fusion.places, bf16[128,2048]{1,0:T(8,128)(2,1)S(1)} %collective-permute-done.2.refs_0_, bf16[128,2048]{1,0:T(8,128)(2,1)S(1)} %collective-permute-done.3.refs_1_, f32[256,1280]{1,0:T(8,128)S(1)} %shard_map.87.refs_2_, ...), custom_call_target="tpu_custom_call" | custom-call | flops 1342177280 | bytes 5242880 | tf_op jit(solution)/shard_map/pallas_call | solution.py:197
  62.9 0.0 collective-permute-done.10.refs_3_
  62.9 6.0 %shard_map.90.refs_3_ = f32[256,1280]{1,0:T(8,128)S(1)} custom-call(s32[2]{0:T(128)S(1)} %pad_add_fusion.1.refs_0_, bf16[80,2048]{1,0:T(8,128)(2,1)S(1)} %get-tuple-element.31.refs_1_, bf16[176,2048]{1,0:T(8,128)(2,1)S(1)} %collective-permute-done.9.refs_2_, bf16[176,2048]{1,0:T(8,128)(2,1)S(1)} %collective-permute-done.10.refs_3_, ...), custom_call_target="tpu_custom_call" | custom-call | flops 2684354560 | bytes 10485760 | tf_op jit(solution)/shard_map/pallas_call | solution.py:197
  68.9 0.0 collective-permute-done.5.refs_0_
  68.9 0.0 collective-permute-done.6.refs_1_
  68.9 6.0 %shard_map.91 = (bf16[256,1024]{1,0:T(8,128)(2,1)S(1)}, f32[1,128]{1,0:T(1,128)S(1)}) custom-call(s32[3]{0:T(128)S(1)} %pad_add_fusion.2.places, bf16[64,2048]{1,0:T(8,128)(2,1)S(1)} %collective-permute-done.5.refs_0_, bf16[128,2048]{1,0:T(8,128)(2,1)S(1)} %collective-permute-done.6.refs_1_, bf16[64,2048]{1,0:T(8,128)(2,1)S(1)} %collective-permute-done.7.refs_2_, ...), custom_call_target="tpu_custom_call" | custom-call | flops 1342177280 | bytes 5242880 | tf_op jit(solution)/shard_map/pallas_call | solution.py:197
  74.9 3.0 %collective-permute-start.13 = (f32[1,128]{1,0:T(1,128)S(1)}, f32[1,128]{1,0:T(1,128)S(1)}, u32[]{:S(2)}, u32[]{:S(2)}) collective-permute-start(f32[1,128]{1,0:T(1,128)S(1)} %get-tuple-element.25), channel_id=1, source_target_pairs={{0,24},{4,28},{8,0},{12,4},{16,8},{20,12},{24,16},{28,20},{32,56},... | collective-permute-start | bytes 1544 | tf_op jit(solution)/shard_map/ppermute | solution.py:273
  77.9 0.6 collective-permute-start.12
  78.5 1.0 collective-permute-start.11
  79.5 2.2 %shard_map.92 = bf16[32,2,16,1024]{3,2,1,0:T(8,128)(2,1)} custom-call(s32[64]{0:T(128)S(1)} %broadcast_add_fusion.slots, bf16[256,1024]{1,0:T(8,128)(2,1)S(1)} %get-tuple-element.20.first, bf16[256,1024]{1,0:T(8,128)(2,1)S(1)} %get-tuple-element.24.second), custom_call_target="tpu_custom_call" | custom-call | bytes 1572864 | tf_op jit(solution)/shard_map/pallas_call | solution.py:255
  81.8 0.0 collective-permute-done.13
  81.8 1.2 %collective-permute-done.12 = f32[1,128]{1,0:T(1,128)S(1)} collective-permute-done((f32[1,128]{1,0:T(1,128)S(1)}, f32[1,128]{1,0:T(1,128)S(1)}, u32[]{:S(2)}, u32[]{:S(2)}) %collective-permute-start.12) | collective-permute-done | bytes 544 | tf_op jit(solution)/shard_map/ppermute | solution.py:273
  83.0 0.3 collective-permute-done.11
  83.3 4.1 %all-to-all-start = ((bf16[32,2,16,1024]{3,2,1,0:T(8,128)(2,1)}), bf16[32,2,16,1024]{3,2,1,0:T(8,128)(2,1)S(1)}, u32[]{:S(2)}, u32[]{:S(2)}) async-start(bf16[32,2,16,1024]{3,2,1,0:T(8,128)(2,1)} %shard_map.92), calls=%async_computation | async-start | bytes 4194304 | tf_op jit(solution)/shard_map/all_to_all | solution.py:277
  87.5 2.2 %collective-permute-start.16 = (f32[1,128]{1,0:T(1,128)S(1)}, f32[1,128]{1,0:T(1,128)S(1)}, u32[]{:S(2)}, u32[]{:S(2)}) collective-permute-start(f32[1,128]{1,0:T(1,128)S(1)} %add_add_fusion.1), channel_id=1, source_target_pairs={{0,3},{1,0},{2,1},{3,2},{4,7},{5,4},{6,5},{7,6},{8,11},{9,8},{10,9... | collective-permute-start | bytes 1544 | tf_op jit(solution)/shard_map/ppermute | solution.py:278
  89.6 2.1 %collective-permute-start.15 = (f32[1,128]{1,0:T(1,128)S(1)}, f32[1,128]{1,0:T(1,128)S(1)}, u32[]{:S(2)}, u32[]{:S(2)}) collective-permute-start(f32[1,128]{1,0:T(1,128)S(1)} %add_add_fusion.1), channel_id=1, source_target_pairs={{0,2},{1,3},{2,0},{3,1},{4,6},{5,7},{6,4},{7,5},{8,10},{9,11},{10,... | collective-permute-start | bytes 1544 | tf_op jit(solution)/shard_map/ppermute | solution.py:278
  91.7 0.6 dynamic_slice.19
  92.3 2.1 %collective-permute-done.14 = f32[1,128]{1,0:T(1,128)S(1)} collective-permute-done((f32[1,128]{1,0:T(1,128)S(1)}, f32[1,128]{1,0:T(1,128)S(1)}, u32[]{:S(2)}, u32[]{:S(2)}) %collective-permute-start.14) | collective-permute-done | bytes 544 | tf_op jit(solution)/shard_map/ppermute | solution.py:278
  94.4 0.3 collective-permute-done.15
  94.7 0.0 collective-permute-start.17
  94.7 0.6 fusion.1
  95.2 0.5 collective-permute-done.17
  95.8 1.8 %collective-permute-start.18 = (f32[1,128]{1,0:T(1,128)S(1)}, f32[1,128]{1,0:T(1,128)S(1)}, u32[]{:S(2)}, u32[]{:S(2)}) collective-permute-start(f32[1,128]{1,0:T(1,128)S(1)} %add.118.refs_0_), channel_id=1, source_target_pairs={{0,32},{4,36},{8,40},{12,44},{16,48},{20,52},{24,56},{28,60},{32,6... | collective-permute-start | bytes 1544 | tf_op jit(solution)/shard_map/ppermute | solution.py:273
  97.6 2.7 %collective-permute-start.19 = (f32[1,128]{1,0:T(1,128)S(1)}, f32[1,128]{1,0:T(1,128)S(1)}, u32[]{:S(2)}, u32[]{:S(2)}) collective-permute-start(f32[1,128]{1,0:T(1,128)S(1)} %add.118.refs_0_), channel_id=1, source_target_pairs={{0,64},{4,68},{8,72},{12,76},{16,80},{20,84},{24,88},{28,92},{32,9... | collective-permute-start | bytes 1544 | tf_op jit(solution)/shard_map/ppermute | solution.py:273
  100.3 1.4 %collective-permute-start.20 = (f32[1,128]{1,0:T(1,128)S(1)}, f32[1,128]{1,0:T(1,128)S(1)}, u32[]{:S(2)}, u32[]{:S(2)}) collective-permute-start(f32[1,128]{1,0:T(1,128)S(1)} %add.118.refs_0_), channel_id=1, source_target_pairs={{0,96},{4,100},{8,104},{12,108},{16,112},{20,116},{24,120},{28,124... | collective-permute-start | bytes 1544 | tf_op jit(solution)/shard_map/ppermute | solution.py:273
  101.7 0.5 pad_bitcast_fusion.shares
  102.2 9.3 %collective-permute-done.18.refs_1_ = f32[1,128]{1,0:T(1,128)S(1)} collective-permute-done((f32[1,128]{1,0:T(1,128)S(1)}, f32[1,128]{1,0:T(1,128)S(1)}, u32[]{:S(2)}, u32[]{:S(2)}) %collective-permute-start.18) | collective-permute-done | bytes 544 | tf_op jit(solution)/shard_map/ppermute | solution.py:273
  111.5 3.0 %collective-permute-done.19.refs_2_ = f32[1,128]{1,0:T(1,128)S(1)} collective-permute-done((f32[1,128]{1,0:T(1,128)S(1)}, f32[1,128]{1,0:T(1,128)S(1)}, u32[]{:S(2)}, u32[]{:S(2)}) %collective-permute-start.19) | collective-permute-done | bytes 544 | tf_op jit(solution)/shard_map/ppermute | solution.py:273
  114.5 0.5 copy-done.8
  115.0 0.5 copy-done.9
  115.5 1.3 %shard_map.93 = f32[1,1]{1,0:T(1,128)} custom-call(f32[1,128]{1,0:T(1,128)} %pad_bitcast_fusion.shares, f32[1,128]{1,0:T(1,128)} %copy-done.6, f32[1,128]{1,0:T(1,128)} %copy-done.7, f32[1,128]{1,0:T(1,128)} %copy-done.8, f32[1,128]{1,0:T(1,128)} %copy-done.9), custom_call_target="tpu_custom_call" | custom-call | tf_op jit(solution)/shard_map/pallas_call | solution.py:281
  116.8 0.0 all-to-all-done
  116.8 1.3 %copy.13 = bf16[1,32,2,16,1024]{4,3,2,1,0:T(8,128)(2,1)} copy(bf16[1,32,2,16,1024]{4,3,2,1,0:T(8,128)(2,1)S(1)} %bitcast.30) | data formatting | bytes 4194304
  (38 shorter events, 0.3 us)
Async XLA Ops:
  0.6 27.6 %collective-permute-start = (bf16[256,2048]{1,0:T(8,128)(2,1)}, bf16[256,2048]{1,0:T(8,128)(2,1)S(1)}, u32[]{:S(2)}, u32[]{:S(2)}) collective-permute-start(bf16[256,2048]{1,0:T(8,128)(2,1)} %bitcast.3.refs_0_), channel_id=1, source_target_pairs={{0,1},{1,2},{2,3},{3,0},{4,5},{5,6},{6,7},{7,4},{8,9},{9,10},{10,1... | collective-permute-start | bytes 3145736 | tf_op jit(solution)/shard_map/ppermute | solution.py:180
  2.7 25.5 %collective-permute-start.1 = (bf16[256,2048]{1,0:T(8,128)(2,1)}, bf16[256,2048]{1,0:T(8,128)(2,1)S(1)}, u32[]{:S(2)}, u32[]{:S(2)}) collective-permute-start(bf16[256,2048]{1,0:T(8,128)(2,1)} %bitcast.3.refs_0_), channel_id=1, source_target_pairs={{0,3},{1,0},{2,1},{3,2},{4,7},{5,4},{6,5},{7,6},{8,11},{9,8},{10,9... | collective-permute-start | bytes 3145736 | tf_op jit(solution)/shard_map/ppermute | solution.py:180
  4.9 7.8 %copy-start.3 = (s32[32]{0:T(128)S(1)}, s32[32]{0:T(128)}, u32[]{:S(2)}) copy-start(s32[32]{0:T(128)} %param.11) | copy-start | bytes 388
  4.9 10.6 %copy-start.4 = (s32[32,1]{0,1:T(1,128)S(1)}, s32[32,1]{0,1:T(1,128)}, u32[]{:S(2)}) copy-start(s32[32,1]{0,1:T(1,128)} %param.13) | copy-start | bytes 388
  9.6 27.6 %collective-permute-start.8 = (bf16[256,2048]{1,0:T(8,128)(2,1)}, bf16[256,2048]{1,0:T(8,128)(2,1)S(1)}, u32[]{:S(2)}, u32[]{:S(2)}) collective-permute-start(bf16[256,2048]{1,0:T(8,128)(2,1)} %bitcast.3.refs_0_), channel_id=1, source_target_pairs={{0,64},{4,68},{8,72},{12,76},{16,80},{20,84},{24,88},{28,92},{32,9... | collective-permute-start | bytes 3145736 | tf_op jit(solution)/shard_map/ppermute | solution.py:182
  15.8 2.2 %copy-start = (bf16[1024,8,2,128]{3,1,2,0:T(8,128)(2,1)S(1)}, bf16[1024,8,2,128]{3,1,2,0:T(8,128)(2,1)}, u32[]{:S(2)}) copy-start(bf16[1024,8,2,128]{3,1,2,0:T(8,128)(2,1)} %copy.11) | copy-start | bytes 12582916
  28.3 21.9 %collective-permute-start.2 = (bf16[128,2048]{1,0:T(8,128)(2,1)S(1)}, bf16[128,2048]{1,0:T(8,128)(2,1)S(1)}, u32[]{:S(2)}, u32[]{:S(2)}) collective-permute-start(bf16[128,2048]{1,0:T(8,128)(2,1)S(1)} %slice.36), channel_id=1, source_target_pairs={{0,1},{1,2},{2,3},{3,0},{4,5},{5,6},{6,7},{7,4},{8,9},{9,10},{10,1... | collective-permute-start | bytes 1572872 | tf_op jit(solution)/shard_map/ppermute | solution.py:242
  29.7 20.5 %collective-permute-start.3 = (bf16[128,2048]{1,0:T(8,128)(2,1)S(1)}, bf16[128,2048]{1,0:T(8,128)(2,1)S(1)}, u32[]{:S(2)}, u32[]{:S(2)}) collective-permute-start(bf16[128,2048]{1,0:T(8,128)(2,1)S(1)} %slice.37), channel_id=1, source_target_pairs={{0,3},{1,0},{2,1},{3,2},{4,7},{5,4},{6,5},{7,6},{8,11},{9,8},{10,9... | collective-permute-start | bytes 1572872 | tf_op jit(solution)/shard_map/ppermute | solution.py:242
  31.6 9.1 %copy-start.1 = (bf16[1024,8,2,128]{3,1,2,0:T(8,128)(2,1)S(1)}, bf16[1024,8,2,128]{3,1,2,0:T(8,128)(2,1)}, u32[]{:S(2)}) copy-start(bf16[1024,8,2,128]{3,1,2,0:T(8,128)(2,1)} %copy.11) | copy-start | bytes 12582916
  31.7 21.7 %collective-permute-start.4 = (bf16[160,2048]{1,0:T(8,128)(2,1)S(1)}, bf16[160,2048]{1,0:T(8,128)(2,1)S(1)}, u32[]{:S(2)}, u32[]{:S(2)}) collective-permute-start(bf16[160,2048]{1,0:T(8,128)(2,1)S(1)} %pad_maximum_fusion), channel_id=1, source_target_pairs={{0,64},{4,68},{8,72},{12,76},{16,80},{20,84},{24,88},{28,92},{32,9... | collective-permute-start | bytes 1966088 | tf_op jit(solution)/shard_map/ppermute | solution.py:243
  37.4 25.5 %collective-permute-start.9 = (bf16[176,2048]{1,0:T(8,128)(2,1)S(1)}, bf16[176,2048]{1,0:T(8,128)(2,1)S(1)}, u32[]{:S(2)}, u32[]{:S(2)}) collective-permute-start(bf16[176,2048]{1,0:T(8,128)(2,1)S(1)} %get-tuple-element.29), channel_id=1, source_target_pairs={{0,1},{1,2},{2,3},{3,0},{4,5},{5,6},{6,7},{7,4},{8,9},{9,10},{10,1... | collective-permute-start | bytes 2162696 | tf_op jit(solution)/shard_map/ppermute | solution.py:245
  37.5 25.4 %collective-permute-start.10 = (bf16[176,2048]{1,0:T(8,128)(2,1)S(1)}, bf16[176,2048]{1,0:T(8,128)(2,1)S(1)}, u32[]{:S(2)}, u32[]{:S(2)}) collective-permute-start(bf16[176,2048]{1,0:T(8,128)(2,1)S(1)} %get-tuple-element.28), channel_id=1, source_target_pairs={{0,3},{1,0},{2,1},{3,2},{4,7},{5,4},{6,5},{7,6},{8,11},{9,8},{10,9... | collective-permute-start | bytes 2162696 | tf_op jit(solution)/shard_map/ppermute | solution.py:245
  50.3 6.5 %copy-start.2 = (f32[1024]{0:T(1024)S(1)}, f32[1024]{0:T(1024)}, u32[]{:S(2)}) copy-start(f32[1024]{0:T(1024)} %param.10) | copy-start | bytes 12292
  50.3 18.6 %collective-permute-start.6 = (bf16[128,2048]{1,0:T(8,128)(2,1)S(1)}, bf16[128,2048]{1,0:T(8,128)(2,1)S(1)}, u32[]{:S(2)}, u32[]{:S(2)}) collective-permute-start(bf16[128,2048]{1,0:T(8,128)(2,1)S(1)} %pad_maximum_fusion.1), channel_id=1, source_target_pairs={{0,64},{4,68},{8,72},{12,76},{16,80},{20,84},{24,88},{28,92},{32,9... | collective-permute-start | bytes 1572872 | tf_op jit(solution)/shard_map/ppermute | solution.py:246
  53.5 15.3 %collective-permute-start.5 = (bf16[64,2048]{1,0:T(8,128)(2,1)S(1)}, bf16[64,2048]{1,0:T(8,128)(2,1)S(1)}, u32[]{:S(2)}, u32[]{:S(2)}) collective-permute-start(bf16[64,2048]{1,0:T(8,128)(2,1)S(1)} %get-tuple-element.33), channel_id=1, source_target_pairs={{0,1},{1,2},{2,3},{3,0},{4,5},{5,6},{6,7},{7,4},{8,9},{9,10},{10,1... | collective-permute-start | bytes 786440 | tf_op jit(solution)/shard_map/ppermute | solution.py:249
  53.6 15.2 %collective-permute-start.7 = (bf16[64,2048]{1,0:T(8,128)(2,1)S(1)}, bf16[64,2048]{1,0:T(8,128)(2,1)S(1)}, u32[]{:S(2)}, u32[]{:S(2)}) collective-permute-start(bf16[64,2048]{1,0:T(8,128)(2,1)S(1)} %get-tuple-element.32), channel_id=1, source_target_pairs={{0,3},{1,0},{2,1},{3,2},{4,7},{5,4},{6,5},{7,6},{8,11},{9,8},{10,9... | collective-permute-start | bytes 786440 | tf_op jit(solution)/shard_map/ppermute | solution.py:249
  74.9 6.9 %collective-permute-start.13 = (f32[1,128]{1,0:T(1,128)S(1)}, f32[1,128]{1,0:T(1,128)S(1)}, u32[]{:S(2)}, u32[]{:S(2)}) collective-permute-start(f32[1,128]{1,0:T(1,128)S(1)} %get-tuple-element.25), channel_id=1, source_target_pairs={{0,24},{4,28},{8,0},{12,4},{16,8},{20,12},{24,16},{28,20},{32,56},... | collective-permute-start | bytes 1544 | tf_op jit(solution)/shard_map/ppermute | solution.py:273
  77.9 5.0 %collective-permute-start.12 = (f32[1,128]{1,0:T(1,128)S(1)}, f32[1,128]{1,0:T(1,128)S(1)}, u32[]{:S(2)}, u32[]{:S(2)}) collective-permute-start(f32[1,128]{1,0:T(1,128)S(1)} %get-tuple-element.25), channel_id=1, source_target_pairs={{0,16},{4,20},{8,24},{12,28},{16,0},{20,4},{24,8},{28,12},{32,48},... | collective-permute-start | bytes 1544 | tf_op jit(solution)/shard_map/ppermute | solution.py:273
  78.5 4.8 %collective-permute-start.11 = (f32[1,128]{1,0:T(1,128)S(1)}, f32[1,128]{1,0:T(1,128)S(1)}, u32[]{:S(2)}, u32[]{:S(2)}) collective-permute-start(f32[1,128]{1,0:T(1,128)S(1)} %get-tuple-element.25), channel_id=1, source_target_pairs={{0,8},{4,12},{8,16},{12,20},{16,24},{20,28},{24,0},{28,4},{32,40},... | collective-permute-start | bytes 1544 | tf_op jit(solution)/shard_map/ppermute | solution.py:273
  83.3 8.4 %copy-start.5 = (s32[32]{0:T(128)S(1)}, s32[32]{0:T(128)}, u32[]{:S(2)}) copy-start(s32[32]{0:T(128)} %param.12) | copy-start | bytes 388
  83.3 33.4 %all-to-all-start = ((bf16[32,2,16,1024]{3,2,1,0:T(8,128)(2,1)}), bf16[32,2,16,1024]{3,2,1,0:T(8,128)(2,1)S(1)}, u32[]{:S(2)}, u32[]{:S(2)}) async-start(bf16[32,2,16,1024]{3,2,1,0:T(8,128)(2,1)} %shard_map.92), calls=%async_computation | async-start | bytes 4194304 | tf_op jit(solution)/shard_map/all_to_all | solution.py:277
  87.5 4.8 %collective-permute-start.16 = (f32[1,128]{1,0:T(1,128)S(1)}, f32[1,128]{1,0:T(1,128)S(1)}, u32[]{:S(2)}, u32[]{:S(2)}) collective-permute-start(f32[1,128]{1,0:T(1,128)S(1)} %add_add_fusion.1), channel_id=1, source_target_pairs={{0,3},{1,0},{2,1},{3,2},{4,7},{5,4},{6,5},{7,6},{8,11},{9,8},{10,9... | collective-permute-start | bytes 1544 | tf_op jit(solution)/shard_map/ppermute | solution.py:278
  89.6 4.8 %collective-permute-start.14 = (f32[1,128]{1,0:T(1,128)S(1)}, f32[1,128]{1,0:T(1,128)S(1)}, u32[]{:S(2)}, u32[]{:S(2)}) collective-permute-start(f32[1,128]{1,0:T(1,128)S(1)} %add_add_fusion.1), channel_id=1, source_target_pairs={{0,1},{1,2},{2,3},{3,0},{4,5},{5,6},{6,7},{7,4},{8,9},{9,10},{10,1... | collective-permute-start | bytes 1544 | tf_op jit(solution)/shard_map/ppermute | solution.py:278
  89.6 5.0 %collective-permute-start.15 = (f32[1,128]{1,0:T(1,128)S(1)}, f32[1,128]{1,0:T(1,128)S(1)}, u32[]{:S(2)}, u32[]{:S(2)}) collective-permute-start(f32[1,128]{1,0:T(1,128)S(1)} %add_add_fusion.1), channel_id=1, source_target_pairs={{0,2},{1,3},{2,0},{3,1},{4,6},{5,7},{6,4},{7,5},{8,10},{9,11},{10,... | collective-permute-start | bytes 1544 | tf_op jit(solution)/shard_map/ppermute | solution.py:278
  94.7 1.1 collective-permute-start.17
  95.8 18.7 %copy-start.6 = (f32[1,128]{1,0:T(1,128)}, f32[1,128]{1,0:T(1,128)S(1)}, u32[]{:S(2)}) copy-start(f32[1,128]{1,0:T(1,128)S(1)} %add.118.refs_0_) | copy-start | bytes 1540
  95.8 15.7 %collective-permute-start.18 = (f32[1,128]{1,0:T(1,128)S(1)}, f32[1,128]{1,0:T(1,128)S(1)}, u32[]{:S(2)}, u32[]{:S(2)}) collective-permute-start(f32[1,128]{1,0:T(1,128)S(1)} %add.118.refs_0_), channel_id=1, source_target_pairs={{0,32},{4,36},{8,40},{12,44},{16,48},{20,52},{24,56},{28,60},{32,6... | collective-permute-start | bytes 1544 | tf_op jit(solution)/shard_map/ppermute | solution.py:273
  97.6 16.9 %collective-permute-start.19 = (f32[1,128]{1,0:T(1,128)S(1)}, f32[1,128]{1,0:T(1,128)S(1)}, u32[]{:S(2)}, u32[]{:S(2)}) collective-permute-start(f32[1,128]{1,0:T(1,128)S(1)} %add.118.refs_0_), channel_id=1, source_target_pairs={{0,64},{4,68},{8,72},{12,76},{16,80},{20,84},{24,88},{28,92},{32,9... | collective-permute-start | bytes 1544 | tf_op jit(solution)/shard_map/ppermute | solution.py:273
  100.3 14.2 %collective-permute-start.20 = (f32[1,128]{1,0:T(1,128)S(1)}, f32[1,128]{1,0:T(1,128)S(1)}, u32[]{:S(2)}, u32[]{:S(2)}) collective-permute-start(f32[1,128]{1,0:T(1,128)S(1)} %add.118.refs_0_), channel_id=1, source_target_pairs={{0,96},{4,100},{8,104},{12,108},{16,112},{20,116},{24,120},{28,124... | collective-permute-start | bytes 1544 | tf_op jit(solution)/shard_map/ppermute | solution.py:273
  111.5 3.0 %copy-start.7 = (f32[1,128]{1,0:T(1,128)}, f32[1,128]{1,0:T(1,128)S(1)}, u32[]{:S(2)}) copy-start(f32[1,128]{1,0:T(1,128)S(1)} %collective-permute-done.18.refs_1_) | copy-start | bytes 1540
  114.5 0.5 copy-start.8
  115.0 0.5 copy-start.9
